TPU v7x, 32 devices: a whole 2x2x4 slice. The times are simulated.
32 devices in a mesh: groups: 2 (over x), expert: 16 (over z, y, core).
Axes of the slice: x: 2, y: 2, z: 4, core: 2. Of those that a mesh axis runs over, the one named last changes fastest.
Arguments:
- tokens: bfloat16 [4096, 2048], P(('groups', 'expert')), parts along dimension 0, may hold values from -6 to 6
- expert_picks: int32 [4096, 6], P(('groups', 'expert')), parts along dimension 0, may hold values from 0 to 15, all different within a row; in each aligned block of 128 rows (0 to 127, 128 to 255, ...) at most 60 rows name the same one
- router: bfloat16 [2048, 16], replicated, may hold values from -0.125 to 0.125
- gate_weight: bfloat16 [16, 2048, 704], P('expert'), may hold values from -0.125 to 0.125
- up_weight: bfloat16 [16, 2048, 704], P('expert'), may hold values from -0.125 to 0.125
- down_weight: bfloat16 [16, 704, 2048], P('expert'), may hold values from -0.21875 to 0.21875
- image_rows: bfloat16 [32, 16, 8, 2048], P(('groups', 'expert')), parts along dimension 0, may hold values from -6 to 6
- image_counts: int32 [32, 16], P('groups'), parts along dimension 0, may hold values from 0 to 8
- span_owner: int32 [32], P('groups'), parts along dimension 0, may hold values from 0 to 15, each once
- text_rows: bfloat16 [4096, 2048], P(('groups', 'expert')), parts along dimension 0, may hold values from -6 to 6
Outputs:
- moe_out: bfloat16 [4096, 2048], P(('groups', 'expert')), parts along dimension 0
- next_span: bfloat16 [4096, 2048], P(('groups', 'expert')), parts along dimension 0
There are 2 independent parts, one for each index of `groups`. A program takes and returns all parts, laid end to end along the dimension named above; an argument that names none is the same for every part. Nothing has to cross between parts.
Inputs may be any that keep to these rules, and one draw needn't show every extreme that they name: `expert_picks`: among one device's 128 rows no expert is picked more than 60 times; a token's 6 picks differ. `span_owner`: each device owns exactly one span.
All inputs are finite; a program needn't handle non-finite values.
Results may differ from a plain program's by a relative error of at most 0.0057.
Values may be sent and summed in bfloat16 or wider, within the bound.
No kernel may reach another device: no remote copies, remote signals or barrier semaphores. Data moves between devices by JAX's collectives and lax.ppermute only.
A program may use at most 128 MiB of HBM per device.

v0:
```python
import jax
import jax.numpy as jnp
from jax import lax
from jax.sharding import PartitionSpec as P

route_scale = 2.446


def place_images(arrived, column, text_block, slots):
    ends = jnp.cumsum(column)
    starts = ends - column
    total = ends[-1]
    position = jnp.arange(text_block.shape[0], dtype=jnp.int32)
    source = jnp.sum((position[:, None] >= ends[None, :]).astype(jnp.int32), axis=1)
    source = jnp.minimum(source, column.shape[0] - 1)
    offset = jnp.clip(position - starts[source], 0, slots - 1)
    picked = arrived[source * slots + offset]
    return jnp.where((position < total)[:, None], picked, text_block)


def expert_block(received, gate_weight, up_weight, down_weight):
    gate = jnp.einsum("nekd,edf->nekf", received, gate_weight, preferred_element_type=jnp.float32)
    upward = jnp.einsum("nekd,edf->nekf", received, up_weight, preferred_element_type=jnp.float32)
    hidden = (jax.nn.silu(gate) * upward).astype(jnp.bfloat16)
    return jnp.einsum(
        "nekf,efd->nekd", hidden, down_weight, preferred_element_type=jnp.float32
    ).astype(jnp.bfloat16)


def local(
    tokens,
    expert_picks,
    router,
    gate_weight,
    up_weight,
    down_weight,
    image_rows,
    image_counts,
    span_owner,
    text_rows,
):
    devices = lax.axis_size("expert")
    my_index = lax.axis_index("expert")
    rows_dev = tokens.shape[0]
    width = tokens.shape[1]
    topk = expert_picks.shape[1]
    exp_dev = gate_weight.shape[0]
    experts = exp_dev * devices
    capacity = 5 * rows_dev * topk // (4 * experts)
    slots = image_rows.shape[2]
    span_of = (
        jnp.zeros((devices,), jnp.int32).at[span_owner].set(jnp.arange(devices, dtype=jnp.int32))
    )
    image_send = image_rows[0][span_of]
    logits = jnp.dot(tokens, router, preferred_element_type=jnp.float32)
    score = jax.nn.sigmoid(logits)
    chosen = jnp.take_along_axis(score, expert_picks, axis=1)
    route = route_scale * chosen / jnp.sum(chosen, axis=1, keepdims=True)
    flat = expert_picks.reshape(-1)
    onehot = (flat[:, None] == jnp.arange(experts, dtype=jnp.int32)[None, :]).astype(jnp.int32)
    ranks = jnp.sum((jnp.cumsum(onehot, axis=0) - 1) * onehot, axis=1)
    target = flat * capacity + ranks
    token_index = jnp.arange(rows_dev * topk, dtype=jnp.int32) // topk
    holder = jnp.full((experts * capacity,), rows_dev, jnp.int32).at[target].set(token_index)
    padded = jnp.concatenate([tokens, jnp.zeros((1, width), tokens.dtype)], axis=0)
    dispatch = padded[holder].reshape(devices, exp_dev, capacity, width)
    arrived = lax.all_to_all(image_send, "expert", split_axis=0, concat_axis=0, tiled=True)
    produced = expert_block(
        lax.all_to_all(dispatch, "expert", split_axis=0, concat_axis=0, tiled=True),
        gate_weight,
        up_weight,
        down_weight,
    )
    returned = lax.all_to_all(produced, "expert", split_axis=0, concat_axis=0, tiled=True)
    my_span = span_of[my_index]
    column = image_counts[:, my_span]
    next_span = place_images(arrived.reshape(devices * slots, width), column, text_rows, slots)
    gathered = returned.reshape(experts * capacity, width)[target].reshape(rows_dev, topk, width)
    moe_out = jnp.sum(route[:, :, None] * gathered.astype(jnp.float32), axis=1).astype(jnp.bfloat16)
    return (moe_out, next_span)


def solution(mesh):
    return jax.shard_map(
        local,
        mesh=mesh,
        in_specs=(
            P(("groups", "expert"), None),
            P(("groups", "expert"), None),
            P(),
            P("expert", None, None),
            P("expert", None, None),
            P("expert", None, None),
            P(("groups", "expert"), None, None, None),
            P("groups", None),
            P("groups"),
            P(("groups", "expert"), None),
        ),
        out_specs=(P(("groups", "expert"), None), P(("groups", "expert"), None)),
        check_vma=False,
    )
```

profile of v0, /device:TPU:13, one launch (start us, length us, event | category | flops | bytes accessed | tf_op | source)
XLA Modules:
  0.0 272.1 jit_solution(16825930592238603300)
XLA Ops:
  0.6 0.0 copy-start
  0.6 0.8 broadcast_multiply_fusion
  1.5 0.8 copy.48
  2.3 0.1 eq.25
  2.4 0.1 eq.29
  2.6 0.1 copy.47
  2.7 0.1 mul.60
  2.9 1.7 reduce-window.10
  4.6 0.3 slice_reduce_fusion
  4.9 0.1 fusion.28
  5.0 3.4 %scatter_custom_fusion = s32[960]{0:T(1024)S(1)} fusion(s32[768]{0:T(1024)S(1)} %fusion.33, s32[768]{0:T(1024)S(1)} %add_select_fusion, s32[]{:T(128)} %constant.26.clone.1), kind=kCustom, calls=%fused_computation.62 | custom fusion | bytes 3844 | tf_op jit(solution)/shard_map/scatter | solution.py:64
  8.4 1.1 concatenate.3
  9.5 5.9 %gather_fusion = bf16[960,2048]{1,0:T(8,128)(2,1)} fusion(bf16[129,2048]{1,0:T(8,128)(2,1)S(1)} %concatenate.3, s32[1024]{0:T(1024)S(1)} %pad_clamp_fusion.3), kind=kCustom, calls=%fused_computation | custom fusion | bytes 7868160 | tf_op jit(solution)/shard_map/gather | solution.py:66
  15.4 4.9 %reshape.169 = bf16[16,1,60,2048]{3,2,0,1:T(8,128)(2,1)} reshape(bf16[960,2048]{1,0:T(8,128)(2,1)} %gather_fusion) | data formatting | bytes 7864320 | tf_op jit(solution)/shard_map/reshape | solution.py:66
  20.3 0.0 copy-start.4
  20.3 0.0 copy-start.1
  20.3 6.7 %all-to-all-start = ((bf16[16,1,60,2048]{3,2,1,0:T(8,128)(2,1)}), bf16[16,1,60,2048]{3,2,1,0:T(8,128)(2,1)}, u32[]{:S(2)}, u32[]{:S(2)}) async-start(bf16[16,1,60,2048]{3,2,1,0:T(8,128)(2,1)} %bitcast.232), calls=%async_computation | async-start | bytes 8388608 | tf_op jit(solution)/shard_map/all_to_all | solution.py:69
  27.0 0.0 copy-done.4
  27.0 0.6 scatter_custom_fusion.1
  27.7 0.0 copy-done.1
  27.7 1.4 gather_fusion.2
  29.0 90.4 %all-to-all-done = bf16[16,1,60,2048]{3,2,1,0:T(8,128)(2,1)} async-done(((bf16[16,1,60,2048]{3,2,1,0:T(8,128)(2,1)}), bf16[16,1,60,2048]{3,2,1,0:T(8,128)(2,1)}, u32[]{:S(2)}, u32[]{:S(2)}) %all-to-all-start) | async-done | bytes 3932192 | tf_op jit(solution)/shard_map/all_to_all | solution.py:69
  119.5 4.9 %all-to-all-start.2 = ((bf16[16,8,2048]{2,1,0:T(8,128)(2,1)}), bf16[16,8,2048]{2,1,0:T(8,128)(2,1)S(1)}, u32[]{:S(2)}, u32[]{:S(2)}) async-start(bf16[16,8,2048]{2,1,0:T(8,128)(2,1)} %gather_fusion.2), calls=%async_computation.2 | async-start | bytes 1048576 | tf_op jit(solution)/shard_map/all_to_all | solution.py:67
  124.4 8.3 %fusion = f32[16,60,704]{2,1,0:T(8,128)} fusion(bf16[16,1,60,2048]{3,2,1,0:T(8,128)(2,1)} %all-to-all-done, bf16[1,2048,704]{1,2,0:T(8,128)(2,1)} %param.14), kind=kOutput, calls=%fused_computation.8 | convolution fusion | flops 2768240640 | bytes 9519104 | tf_op jit(solution)/shard_map/nekd,edf->nekf/dot_general | solution.py:23
  132.7 0.0 copy-done
  132.7 12.3 %convert_bitcast_fusion = bf16[16,1,60,2048]{3,2,1,0:T(8,128)(2,1)} fusion(bf16[1,704,2048]{2,1,0:T(8,128)(2,1)S(1)} %copy-done, f32[16,60,704]{2,1,0:T(8,128)} %fusion, bf16[1,2048,704]{1,2,0:T(8,128)(2,1)} %param.13, bf16[16,1,60,2048]{3,2,1,0:T(8,128)(2,1)} %all-to-all-done), kind=kOutput, calls=%fused_computation.12 | convolution fusion | flops 5542502400 | bytes 16334848 | tf_op jit(solution)/shard_map/nekf,efd->nekd/dot_general | solution.py:25
  145.0 0.0 copy-start.3
  145.0 0.0 copy-start.2
  145.0 0.0 all-to-all-done.2
  145.0 6.2 %all-to-all-start.1 = ((bf16[16,1,60,2048]{3,2,1,0:T(8,128)(2,1)}), bf16[16,1,60,2048]{3,2,1,0:T(8,128)(2,1)}, u32[]{:S(2)}, u32[]{:S(2)}) async-start(bf16[16,1,60,2048]{3,2,1,0:T(8,128)(2,1)} %convert_bitcast_fusion), calls=%async_computation.1 | async-start | bytes 8388608 | tf_op jit(solution)/shard_map/all_to_all | solution.py:74
  151.2 0.6 dynamic_slice.6
  153.7 0.0 copy-done.3
  153.7 0.2 fusion.45
  153.9 0.1 reduce.2
  154.0 0.5 slice.41
  154.5 0.0 copy-done.2
  154.6 0.1 copy.44
  154.7 0.1 reshape.233
  154.8 1.3 fusion.26
  156.1 5.1 %gather_fusion.4 = f32[768]{0:T(1024)S(1)} fusion(f32[128,16]{0,1:T(8,128)S(1)} %fusion.26, s32[768]{0:T(1024)S(1)} %reshape.233), kind=kCustom, calls=%fused_computation.4 | custom fusion | bytes 12288 | tf_op jit(solution)/shard_map/jit(take_along_axis)/gather | solution.py:57
  161.2 0.1 reshape.236
  161.4 0.1 copy.45
  161.5 0.1 copy.46
  161.6 0.7 iota_compare_fusion.3
  162.3 0.7 fusion.46
  163.0 0.1 convert_reduce_fusion
  163.1 10.0 %fusion.39 = s32[128]{0:T(128)S(1)} fusion(s32[128]{0:T(128)S(1)} %convert_reduce_fusion, s32[]{:T(128)} %bitcast.46, s32[]{:T(128)} %bitcast.47, s32[]{:T(128)} %bitcast.48, s32[]{:T(128)} %bitcast.49, s32[]{:T(128)} %bitcast.50, s32[]{:T(128)} %bitcast.52, s32[]{:T(128)} %bitcast.51, s32[]{:T(128)} %bitcast.29, s32[]{:T(128)} %bitcast.31, s32[]{:T(128)} %bitcast.33, ...), kind=kLoop, calls=%fused_computation.82 | loop fusion | flops 5248 | bytes 1088 | tf_op jit(solution)/shard_map/select_n | solution.py:17
  173.1 1.7 gather_fusion.3
  174.9 2.1 broadcast_select_fusion
  177.0 66.6 %all-to-all-done.1 = bf16[16,1,60,2048]{3,2,1,0:T(8,128)(2,1)} async-done(((bf16[16,1,60,2048]{3,2,1,0:T(8,128)(2,1)}), bf16[16,1,60,2048]{3,2,1,0:T(8,128)(2,1)}, u32[]{:S(2)}, u32[]{:S(2)}) %all-to-all-start.1) | async-done | bytes 3932192 | tf_op jit(solution)/shard_map/all_to_all | solution.py:74
  243.6 4.8 %reshape.175 = bf16[960,2048]{1,0:T(8,128)(2,1)} reshape(bf16[16,1,60,2048]{3,2,1,0:T(8,128)(2,1)} %all-to-all-done.1) | data formatting | bytes 7864320 | tf_op jit(solution)/shard_map/reshape | solution.py:78
  248.5 9.7 %gather_fusion.1 = bf16[768,2048]{1,0:T(8,128)(2,1)} fusion(bf16[960,2048]{1,0:T(8,128)(2,1)} %reshape.175, s32[1024]{0:T(1024)S(1)} %pad_clamp_fusion.2), kind=kCustom, calls=%fused_computation.1 | custom fusion | bytes 6294528 | tf_op jit(solution)/shard_map/gather | solution.py:78
  258.2 6.6 %reshape.177 = f32[128,6,2048]{2,1,0:T(8,128)} reshape(bf16[768,2048]{1,0:T(8,128)(2,1)} %gather_fusion.1) | data formatting | bytes 9437184 | tf_op jit(solution)/shard_map/convert_element_type | solution.py:79
  264.7 7.4 %multiply_reduce_fusion = bf16[128,2048]{1,0:T(8,128)(2,1)} fusion(f32[128,6,2048]{2,1,0:T(8,128)} %reshape.177, f32[128,6]{1,0:T(8,128)S(1)} %copy.46), kind=kLoop, calls=%fused_computation.7 | loop fusion | flops 2883584 | bytes 6818816 | tf_op jit(solution)/shard_map/reduce_sum | solution.py:79
  (17 shorter events, 0.2 us)
Async XLA Ops:
  0.6 132.0 %copy-start = (bf16[1,704,2048]{2,1,0:T(8,128)(2,1)S(1)}, bf16[1,704,2048]{2,1,0:T(8,128)(2,1)}, u32[]{:S(2)}) copy-start(bf16[1,704,2048]{2,1,0:T(8,128)(2,1)} %param.15) | copy-start | bytes 8650756
  20.3 6.7 %copy-start.4 = (s32[16]{0:T(128)S(1)}, s32[16]{0:T(128)}, u32[]{:S(2)}) copy-start(s32[16]{0:T(128)} %param.18) | copy-start | bytes 196
  20.3 7.4 %copy-start.1 = (bf16[1,16,8,2048]{3,2,1,0:T(8,128)(2,1)S(1)}, bf16[1,16,8,2048]{3,2,1,0:T(8,128)(2,1)}, u32[]{:S(2)}) copy-start(bf16[1,16,8,2048]{3,2,1,0:T(8,128)(2,1)} %param.16) | copy-start | bytes 1572868
  20.3 99.2 %all-to-all-start = ((bf16[16,1,60,2048]{3,2,1,0:T(8,128)(2,1)}), bf16[16,1,60,2048]{3,2,1,0:T(8,128)(2,1)}, u32[]{:S(2)}, u32[]{:S(2)}) async-start(bf16[16,1,60,2048]{3,2,1,0:T(8,128)(2,1)} %bitcast.232), calls=%async_computation | async-start | bytes 8388608 | tf_op jit(solution)/shard_map/all_to_all | solution.py:69
  119.5 25.5 %all-to-all-start.2 = ((bf16[16,8,2048]{2,1,0:T(8,128)(2,1)}), bf16[16,8,2048]{2,1,0:T(8,128)(2,1)S(1)}, u32[]{:S(2)}, u32[]{:S(2)}) async-start(bf16[16,8,2048]{2,1,0:T(8,128)(2,1)} %gather_fusion.2), calls=%async_computation.2 | async-start | bytes 1048576 | tf_op jit(solution)/shard_map/all_to_all | solution.py:67
  145.0 8.7 %copy-start.3 = (s32[16,16]{1,0:T(8,128)S(1)}, s32[16,16]{1,0:T(8,128)}, u32[]{:S(2)}) copy-start(s32[16,16]{1,0:T(8,128)} %param.17) | copy-start | bytes 3076
  145.0 9.6 %copy-start.2 = (s32[128,6]{0,1:T(8,128)S(1)}, s32[128,6]{0,1:T(8,128)}, u32[]{:S(2)}) copy-start(s32[128,6]{0,1:T(8,128)} %param.11) | copy-start | bytes 9220
  145.0 98.6 %all-to-all-start.1 = ((bf16[16,1,60,2048]{3,2,1,0:T(8,128)(2,1)}), bf16[16,1,60,2048]{3,2,1,0:T(8,128)(2,1)}, u32[]{:S(2)}, u32[]{:S(2)}) async-start(bf16[16,1,60,2048]{3,2,1,0:T(8,128)(2,1)} %convert_bitcast_fusion), calls=%async_computation.1 | async-start | bytes 8388608 | tf_op jit(solution)/shard_map/all_to_all | solution.py:74
where the time goes:
time: 273 us; the launch traced here: 272 us
  waiting for transfers between devices  157 us (58%)
  local copies, waits for them, and re-layouts  49.4 us (18%)
  other arithmetic  23.2 us (8%)
  matrix products  21.9 us (8%)
  starting transfers between devices  17.8 us (7%)
  between operations  2.82 us (1%)
    all_to_all x1, waiting for transfers between devices, local(): lax.all_to_all(dispatch, 'expert', split_axis=0, concat_axis=0, tiled=True)  90.4 us
    all_to_all x1, waiting for transfers between devices, local(): lax.all_to_all(produced, 'expert', split_axis=0, concat_axis=0, tiled=True)  66.6 us
    dot_general x1, matrix products, expert_block(): jnp.einsum('nekf,efd->nekd', hidden, down_weight, preferred_element_type=...  12.3 us
    select_n x1, other arithmetic, place_images(): picked = arrived[source * slots + offset]  10 us
    gather x1, local copies, waits for them, and re-layouts, local(): returned.reshape(experts * capacity, width)[target]  9.71 us
    dot_general x1, matrix products, expert_block(): jnp.einsum('nekd,edf->nekf', received, up_weight, preferred_element_type=...  8.29 us
    reduce_sum x1, other arithmetic, local(): jnp.sum(route[:, :, None] * gathered.astype(jnp.float32), axis=1)  7.4 us
    all_to_all x1, starting transfers between devices, local(): lax.all_to_all(dispatch, 'expert', split_axis=0, concat_axis=0, tiled=True)  6.69 us
  transfers between devices with their start and end apart: 3, of which 2 were waited for; matrix products, arithmetic and copies ran while one was open for 17% of the time, Pallas kernels for 0%

commit v1 on v0

v1 whole, which is shorter than its diff:
```python
import functools

import jax
import jax.numpy as jnp
from jax import lax
from jax.experimental import pallas as pl
from jax.experimental.pallas import tpu as pltpu
from jax.sharding import PartitionSpec as P

route_scale = 2.446
NT = (((1,), (1,)), ((), ()))


def ring_of(chips):
    if chips <= 8:
        return list(range(0, chips, 2)) + list(range(chips - 1, 0, -2))
    return list(range(chips))


def pieces(total, step):
    return [(a, min(step, total - a)) for a in range(0, total, step)]


def ffn_kernel(count, sizes, columns, *refs):
    shards = refs[:count]
    route_ref, g0, u0, d0, g1, u1, d1 = refs[count : count + 7]
    outs = refs[count + 7 : count + 7 + len(columns)]
    x, hidden, total, wg, wu, wd, sems = refs[count + 7 + len(columns) :]
    rows = sum(sizes)
    ff = g0.shape[0]
    width = g0.shape[1]
    fs = pieces(ff, 256)
    copies = []
    for e, (g, u, d) in enumerate(((g0, u0, d0), (g1, u1, d1))):
        for i, (a, m) in enumerate(fs):
            copies.append(pltpu.make_async_copy(g.at[pl.ds(a, m)], wg.at[e, pl.ds(a, m)], sems.at[e, i, 0]))
            copies.append(pltpu.make_async_copy(u.at[pl.ds(a, m)], wu.at[e, pl.ds(a, m)], sems.at[e, i, 1]))
        copies.append(pltpu.make_async_copy(d, wd.at[e], sems.at[e, 0, 2]))
    for copy in copies:
        copy.start()
    at = 0
    for ref, m in zip(shards, sizes):
        x[pl.ds(at, m), :] = ref[...]
        at += m
    per = 2 * len(fs) + 1
    block = rows // len(columns)
    for e in range(2):
        for i, (a, m) in enumerate(fs):
            copies[e * per + 2 * i].wait()
            copies[e * per + 2 * i + 1].wait()
            gate = lax.dot_general(x[...], wg[e, pl.ds(a, m), :], NT, preferred_element_type=jnp.float32)
            upward = lax.dot_general(x[...], wu[e, pl.ds(a, m), :], NT, preferred_element_type=jnp.float32)
            hidden[:, pl.ds(a, m)] = (gate / (1.0 + jnp.exp(-gate)) * upward).astype(jnp.bfloat16)
        copies[e * per + per - 1].wait()

        @pl.loop(0, width // 256)
        def _(j):
            lanes = pl.ds(pl.multiple_of(j * 256, 256), 256)
            row = jnp.dot(hidden[...], wd[e, :, lanes], preferred_element_type=jnp.float32)
            row = row.astype(jnp.bfloat16).astype(jnp.float32)
            for k, c in enumerate(columns):
                part = row[k * block : (k + 1) * block] * route_ref[:, 2 * c + e : 2 * c + e + 1]
                if e == 0:
                    total[pl.ds(k * block, block), lanes] = part
                else:
                    outs[k][:, lanes] = (total[pl.ds(k * block, block), lanes] + part).astype(outs[k].dtype)


def ffn(shards, columns, route, weights, dtype):
    sizes = [s.shape[0] for s in shards]
    rows = sum(sizes)
    ff, width = weights[0].shape
    block = rows // len(columns)
    vmem = pl.BlockSpec(memory_space=pltpu.VMEM)
    hbm = pl.BlockSpec(memory_space=pl.ANY)
    return pl.pallas_call(
        functools.partial(ffn_kernel, len(shards), sizes, columns),
        out_shape=[jax.ShapeDtypeStruct((block, width), dtype) for _ in columns],
        in_specs=[vmem] * (len(shards) + 1) + [hbm] * 6,
        out_specs=[vmem] * len(columns),
        scratch_shapes=[
            pltpu.VMEM((rows, width), jnp.bfloat16),
            pltpu.VMEM((rows, ff), jnp.bfloat16),
            pltpu.VMEM((rows, width), jnp.float32),
            pltpu.VMEM((2, ff, width), jnp.bfloat16),
            pltpu.VMEM((2, ff, width), jnp.bfloat16),
            pltpu.VMEM((2, ff, width), jnp.bfloat16),
            pltpu.SemaphoreType.DMA((2, 3, 3)),
        ],
        compiler_params=pltpu.CompilerParams(vmem_limit_bytes=40 * 2**20),
        cost_estimate=pl.CostEstimate(
            flops=12 * rows * ff * width, bytes_accessed=12 * ff * width, transcendentals=2 * rows * ff
        ),
    )(*shards, route, *weights)


def place_kernel(slots, arrived_ref, counts_ref, owner_ref, me_ref, text_ref, out_ref):
    rows = text_ref.shape[0]
    devices = counts_ref.shape[0]
    held = arrived_ref.shape[0]
    mine = (owner_ref[...] == me_ref[0]).astype(jnp.int32)
    live = jnp.sum(counts_ref[...] * mine, axis=1, keepdims=True)
    total = jnp.sum(live)
    lane = lax.broadcasted_iota(jnp.int32, (devices, held), 1)
    holder = lane // slots
    which = lax.broadcasted_iota(jnp.int32, (devices, held), 0)
    own = jnp.sum(jnp.where(which == holder, live, 0), axis=0, keepdims=True)
    start = jnp.sum(jnp.where(which < holder, live, 0), axis=0, keepdims=True)
    offset = lane[:1] - holder[:1] * slots
    place = jnp.where(offset < own, start + offset, -1)
    row = lax.broadcasted_iota(jnp.int32, (rows, held), 0)
    pick = (row == place).astype(jnp.bfloat16)
    image = jnp.dot(pick, arrived_ref[...], preferred_element_type=jnp.float32).astype(jnp.bfloat16)
    position = lax.broadcasted_iota(jnp.int32, (rows, 1), 0)
    out_ref[...] = jnp.where(position < total, image, text_ref[...])


def place_images(arrived, counts, owner, me, text_block, slots):
    vmem = pl.BlockSpec(memory_space=pltpu.VMEM)
    return pl.pallas_call(
        functools.partial(place_kernel, slots),
        out_shape=jax.ShapeDtypeStruct(text_block.shape, text_block.dtype),
        in_specs=[vmem, vmem, vmem, pl.BlockSpec(memory_space=pltpu.SMEM), vmem],
        out_specs=vmem,
    )(arrived, counts, owner[None, :], me[None], text_block)


def local(
    tokens,
    expert_picks,
    router,
    gate_weight,
    up_weight,
    down_weight,
    image_rows,
    image_counts,
    span_owner,
    text_rows,
):
    devices = lax.axis_size("expert")
    me = lax.axis_index("expert")
    rows, width = tokens.shape
    half = rows // 2
    experts = gate_weight.shape[0] * devices
    slots = image_rows.shape[2]
    chips = devices // 2
    far = chips // 2
    ring = ring_of(chips)
    pos = {c: i for i, c in enumerate(ring)}

    def send(x, pairs):
        return lax.ppermute(x, "expert", pairs)

    def by_chip(target):
        return [(2 * c + k, 2 * target(c) + k) for c in range(chips) for k in range(2)]

    up = by_chip(lambda c: ring[(pos[c] + 1) % chips])
    down = by_chip(lambda c: ring[(pos[c] - 1) % chips])
    sibling = [(d, d ^ 1) for d in range(devices)]

    from_below, from_above = [tokens], [tokens]
    for s in range(1, far):
        from_below.append(send(from_below[-1], up))
        from_above.append(send(from_above[-1], down))
    last = [send(from_below[-1][:half], up), send(from_above[-1][half:], down)]

    own = [gate_weight[0].T, up_weight[0].T, down_weight[0]]
    weights = own + [send(w, sibling) for w in own]

    logits = lax.dot_general(router, tokens, (((0,), (1,)), ((), ())), preferred_element_type=jnp.float32)
    score = jax.nn.sigmoid(logits)
    expert = lax.broadcasted_iota(jnp.int32, (experts, rows), 0)
    picked = functools.reduce(
        jnp.logical_or, [expert == expert_picks[:, k][None, :] for k in range(expert_picks.shape[1])]
    )
    chosen = jnp.where(picked, score, 0.0)
    table = jnp.where(picked, route_scale * score / jnp.sum(chosen, axis=0, keepdims=True), 0.0)[None]
    bit = 1
    while bit < chips:
        table = jnp.concatenate([table, send(table, by_chip(lambda c: c ^ bit))], axis=0)
        bit *= 2
    chip = me // 2
    order = jnp.array(ring, jnp.int32)
    place = jnp.array([pos[c] for c in range(chips)], jnp.int32)[chip]
    source = order[(place + jnp.arange(chips, dtype=jnp.int32)) % chips] ^ chip
    wanted = (source[:, None] * experts + jnp.stack([me, me ^ 1])[None, :]).reshape(-1)
    route = table.reshape(chips * experts, rows)[wanted].T

    sums = {}
    for s in range(1, far):
        shards, columns = [from_above[s], from_below[s]], [s, chips - s]
        if s == 1:
            shards, columns = [tokens] + shards, [0] + columns
        for c, value in zip(columns, ffn(shards, columns, route, weights, jnp.float32)):
            sums[c] = value
    (farthest,) = ffn(last, [far], route, weights, jnp.bfloat16)

    def low(x):
        return x.astype(jnp.bfloat16)

    def wide(x):
        return x.astype(jnp.float32)

    going_down = send(farthest[:half], down)
    going_up = send(farthest[half:], up)
    going_down = low(sums[chips - far + 1] + jnp.pad(wide(going_down), ((0, rows - half), (0, 0))))
    going_up = low(sums[far - 1] + jnp.pad(wide(going_up), ((half, 0), (0, 0))))
    for s in range(far - 1, 0, -1):
        going_down = send(going_down, down)
        going_up = send(going_up, up)
        if s > 1:
            going_down = low(sums[chips - s + 1] + wide(going_down))
            going_up = low(sums[s - 1] + wide(going_up))
    moe_out = low(sums[0] + wide(going_down) + wide(going_up))

    number = jnp.arange(devices, dtype=jnp.int32)
    span_of = jnp.sum(jnp.where(span_owner[:, None] == number[None, :], number[:, None], 0), axis=0)
    image_send = image_rows[0][span_of]
    arrived = lax.all_to_all(image_send, "expert", split_axis=0, concat_axis=0, tiled=True)
    next_span = place_images(
        arrived.reshape(devices * slots, width), image_counts, span_owner, me, text_rows, slots
    )
    return (moe_out, next_span)


def solution(mesh):
    return jax.shard_map(
        local,
        mesh=mesh,
        in_specs=(
            P(("groups", "expert"), None),
            P(("groups", "expert"), None),
            P(),
            P("expert", None, None),
            P("expert", None, None),
            P("expert", None, None),
            P(("groups", "expert"), None, None, None),
            P("groups", None),
            P("groups"),
            P(("groups", "expert"), None),
        ),
        out_specs=(P(("groups", "expert"), None), P(("groups", "expert"), None)),
        check_vma=False,
    )
```

time: 273 us -> 154 us (0.56)
  the two profiles are of different devices: /device:TPU:13 before, /device:TPU:0 now
where the time goes in v1:
time: 154 us; the launch traced here: 153 us
  waiting for transfers between devices  49.8 us (32%)
  Pallas kernels  48.6 us (32%)
  starting transfers between devices  35.6 us (23%)
  local copies, waits for them, and re-layouts  12.9 us (8%)
  other arithmetic  3.88 us (3%)
    ppermute x22, waiting for transfers between devices, send(): return lax.ppermute(x, 'expert', pairs)  49.7 us
    pallas_call x4, Pallas kernels, ffn(): pl.pallas_call(functools.partial(ffn_kernel, len(shards), sizes, columns)...  46.2 us
    ppermute x22, starting transfers between devices, send(): return lax.ppermute(x, 'expert', pairs)  29.8 us
    all_to_all x1, starting transfers between devices, local(): lax.all_to_all(image_send, 'expert', split_axis=0, concat_axis=0, tiled=T...  5.83 us
    unnamed x20, local copies, waits for them, and re-layouts  4.64 us
    slice x2, local copies, waits for them, and re-layouts, local(): last = [send(from_below[-1][:half], up), send(from_above[-1][half:], down)]  3.34 us
  transfers between devices with their start and end apart: 23, of which 9 were waited for; matrix products, arithmetic and copies ran while one was open for 8% of the time, Pallas kernels for 32%

profile of v1, /device:TPU:0, one launch (start us, length us, event | category | flops | bytes accessed | tf_op | source)
XLA Modules:
  0.0 153.1 jit_solution(6500941404006981293)
XLA Ops:
  0.6 0.0 copy-start
  0.6 0.0 copy-start.9
  0.7 0.5 collective-permute-start.5
  1.2 0.1 collective-permute-start.6
  1.3 0.4 collective-permute-start.7
  1.7 0.9 slice_bitcast_fusion.5
  2.6 1.3 select_reduce_fusion.1
  4.0 2.9 %collective-permute-start.2 = (f32[1,16,128]{2,1,0:T(8,128)S(1)}, f32[1,16,128]{2,1,0:T(8,128)S(1)}, u32[]{:S(2)}, u32[]{:S(2)}) collective-permute-start(f32[1,16,128]{2,1,0:T(8,128)S(1)} %select_bitcast_fusion), channel_id=1, source_target_pairs={{0,2},{1,3},{2,0},{3,1},{4,6},{5,7},{6,4},{7,5},{8,10},{9,11},{10,... | collective-permute-start | bytes 24584 | tf_op jit(solution)/shard_map/ppermute | solution.py:152
  6.9 1.6 %collective-permute-start.1 = (bf16[128,2048]{1,0:T(8,128)(2,1)}, bf16[128,2048]{1,0:T(8,128)(2,1)}, u32[]{:S(2)}, u32[]{:S(2)}) collective-permute-start(bf16[128,2048]{1,0:T(8,128)(2,1)} %refs_0_.1), channel_id=1, source_target_pairs={{0,4},{1,5},{2,0},{3,1},{4,8},{5,9},{6,2},{7,3},{8,12},{9,13},{10,... | collective-permute-start | bytes 1572872 | tf_op jit(solution)/shard_map/ppermute | solution.py:152
  8.4 0.1 collective-permute-done.2
  8.5 2.1 %collective-permute-start.3 = (f32[2,16,128]{2,1,0:T(8,128)S(1)}, f32[2,16,128]{2,1,0:T(8,128)S(1)}, u32[]{:S(2)}, u32[]{:S(2)}) collective-permute-start(f32[2,16,128]{2,1,0:T(8,128)S(1)} %pad_maximum_fusion.2), channel_id=1, source_target_pairs={{0,4},{1,5},{2,6},{3,7},{4,0},{5,1},{6,2},{7,3},{8,12},{9,13},{10,... | collective-permute-start | bytes 49160 | tf_op jit(solution)/shard_map/ppermute | solution.py:152
  10.6 9.7 %collective-permute-done.3 = f32[2,16,128]{2,1,0:T(8,128)S(1)} collective-permute-done((f32[2,16,128]{2,1,0:T(8,128)S(1)}, f32[2,16,128]{2,1,0:T(8,128)S(1)}, u32[]{:S(2)}, u32[]{:S(2)}) %collective-permute-start.3) | collective-permute-done | bytes 16416 | tf_op jit(solution)/shard_map/ppermute | solution.py:152
  20.3 1.2 collective-permute-start
  21.5 1.2 collective-permute-start.9
  22.8 0.7 select_reduce_fusion
  23.5 10.8 %collective-permute-done.refs_1_ = bf16[128,2048]{1,0:T(8,128)(2,1)} collective-permute-done((bf16[128,2048]{1,0:T(8,128)(2,1)}, bf16[128,2048]{1,0:T(8,128)(2,1)}, u32[]{:S(2)}, u32[]{:S(2)}) %collective-permute-start) | collective-permute-done | bytes 524320 | tf_op jit(solution)/shard_map/ppermute | solution.py:152
  34.4 0.8 collective-permute-start.8
  35.2 1.4 gather_fusion.2
  36.6 5.8 %all-to-all-start = ((bf16[16,8,2048]{2,1,0:T(8,128)(2,1)}), bf16[16,8,2048]{2,1,0:T(8,128)(2,1)}, u32[]{:S(2)}, u32[]{:S(2)}) async-start(bf16[16,8,2048]{2,1,0:T(8,128)(2,1)} %gather_fusion.2), calls=%async_computation | async-start | bytes 1048576 | tf_op jit(solution)/shard_map/all_to_all | solution.py:219
  42.4 1.2 dynamic_slice.3
  43.7 0.6 fusion.9
  44.3 1.9 %collective-permute-start.11 = (bf16[128,2048]{1,0:T(8,128)(2,1)}, bf16[128,2048]{1,0:T(8,128)(2,1)}, u32[]{:S(2)}, u32[]{:S(2)}) collective-permute-start(bf16[128,2048]{1,0:T(8,128)(2,1)} %collective-permute-done.9.refs_1_), channel_id=1, source_target_pairs={{0,4},{1,5},{2,0},{3,1},{4,8},{5,9},{6,2},{7,3},{8,12},{9,13},{10,... | collective-permute-start | bytes 1572872 | tf_op jit(solution)/shard_map/ppermute | solution.py:152
  46.2 0.6 gather_fusion
  46.8 0.1 pad_add_fusion
  46.9 2.9 %collective-permute-done.8.refs_0_ = bf16[128,2048]{1,0:T(8,128)(2,1)} collective-permute-done((bf16[128,2048]{1,0:T(8,128)(2,1)}, bf16[128,2048]{1,0:T(8,128)(2,1)}, u32[]{:S(2)}, u32[]{:S(2)}) %collective-permute-start.8) | collective-permute-done | bytes 524320 | tf_op jit(solution)/shard_map/ppermute | solution.py:152
  49.8 13.4 %collective-permute-done.11.refs_1_ = bf16[128,2048]{1,0:T(8,128)(2,1)} collective-permute-done((bf16[128,2048]{1,0:T(8,128)(2,1)}, bf16[128,2048]{1,0:T(8,128)(2,1)}, u32[]{:S(2)}, u32[]{:S(2)}) %collective-permute-start.11) | collective-permute-done | bytes 524320 | tf_op jit(solution)/shard_map/ppermute | solution.py:152
  63.2 6.4 %collective-permute-start.4 = (f32[4,16,128]{2,1,0:T(8,128)S(1)}, f32[4,16,128]{2,1,0:T(8,128)S(1)}, u32[]{:S(2)}, u32[]{:S(2)}) collective-permute-start(f32[4,16,128]{2,1,0:T(8,128)S(1)} %pad_maximum_fusion.1), channel_id=1, source_target_pairs={{0,8},{1,9},{2,10},{3,11},{4,12},{5,13},{6,14},{7,15},{8,0},{9,1},... | collective-permute-start | bytes 98312 | tf_op jit(solution)/shard_map/ppermute | solution.py:152
  69.6 0.1 broadcast_add_fusion
  69.7 0.1 add.124
  69.8 1.7 %slice.46 = bf16[64,2048]{1,0:T(8,128)(2,1)} slice(bf16[128,2048]{1,0:T(8,128)(2,1)} %collective-permute-done.11.refs_1_), slice={[0:64], [0:2048]} | slice | bytes 524288 | tf_op jit(solution)/shard_map/slice | solution.py:165
  71.4 0.0 collective-permute-start.12
  71.5 1.7 %slice.47 = bf16[64,2048]{1,0:T(8,128)(2,1)} slice(bf16[128,2048]{1,0:T(8,128)(2,1)} %collective-permute-done.10.refs_0_), slice={[64:128], [0:2048]} | slice | bytes 524288 | tf_op jit(solution)/shard_map/slice | solution.py:165
  73.2 2.0 %collective-permute-start.13 = (bf16[64,2048]{1,0:T(8,128)(2,1)}, bf16[64,2048]{1,0:T(8,128)(2,1)}, u32[]{:S(2)}, u32[]{:S(2)}) collective-permute-start(bf16[64,2048]{1,0:T(8,128)(2,1)} %slice.47), channel_id=1, source_target_pairs={{0,2},{1,3},{2,6},{3,7},{4,0},{5,1},{6,10},{7,11},{8,4},{9,5},{10,... | collective-permute-start | bytes 786440 | tf_op jit(solution)/shard_map/ppermute | solution.py:152
  75.2 0.6 gather_fusion.1
  75.7 0.1 copy.16
  75.8 3.5 %collective-permute-done.12.refs_0_ = bf16[64,2048]{1,0:T(8,128)(2,1)} collective-permute-done((bf16[64,2048]{1,0:T(8,128)(2,1)}, bf16[64,2048]{1,0:T(8,128)(2,1)}, u32[]{:S(2)}, u32[]{:S(2)}) %collective-permute-start.12) | collective-permute-done | bytes 262176 | tf_op jit(solution)/shard_map/ppermute | solution.py:152
  79.3 1.7 %collective-permute-done.13.refs_1_ = bf16[64,2048]{1,0:T(8,128)(2,1)} collective-permute-done((bf16[64,2048]{1,0:T(8,128)(2,1)}, bf16[64,2048]{1,0:T(8,128)(2,1)}, u32[]{:S(2)}, u32[]{:S(2)}) %collective-permute-start.13) | collective-permute-done | bytes 262176 | tf_op jit(solution)/shard_map/ppermute | solution.py:152
  81.0 0.0 copy-start.2
  81.0 1.8 %copy-done.2 = bf16[1,2048,704]{1,2,0:T(8,128)(2,1)S(1)} copy-done((bf16[1,2048,704]{1,2,0:T(8,128)(2,1)S(1)}, bf16[1,2048,704]{1,2,0:T(8,128)(2,1)}, u32[]{:S(2)}) %copy-start.2) | copy-done | bytes 2883608
  82.8 1.8 %copy-done.4 = bf16[1,704,2048]{2,1,0:T(8,128)(2,1)S(1)} copy-done((bf16[1,704,2048]{2,1,0:T(8,128)(2,1)S(1)}, bf16[1,704,2048]{2,1,0:T(8,128)(2,1)}, u32[]{:S(2)}) %copy-start.4) | copy-done | bytes 2883608
  84.7 10.3 %shard_map.134 = bf16[128,2048]{1,0:T(8,128)(2,1)S(1)} custom-call(bf16[64,2048]{1,0:T(8,128)(2,1)} %collective-permute-done.12.refs_0_, bf16[64,2048]{1,0:T(8,128)(2,1)} %collective-permute-done.13.refs_1_, f32[128,16]{1,0:T(8,128)S(1)} %bitcast.55, bf16[704,2048]{1,0:T(8,128)(2,1)S(1)} %bitcast.41, bf16[704,2048]{1,0:T(8,128)(2,1)S(1)} %bitcast.46, ...), custom_call_target="tpu_custom_call" | custom-call | flops 2214592512 | bytes 17301504 | tf_op jit(solution)/shard_map/pallas_call | solution.py:76
  95.0 1.8 %collective-permute-start.14 = (bf16[64,2048]{1,0:T(8,128)(2,1)S(1)}, bf16[64,2048]{1,0:T(8,128)(2,1)S(1)}, u32[]{:S(2)}, u32[]{:S(2)}) collective-permute-start(bf16[64,2048]{1,0:T(8,128)(2,1)S(1)} %get-tuple-element.16), channel_id=1, source_target_pairs={{0,2},{1,3},{2,6},{3,7},{4,0},{5,1},{6,10},{7,11},{8,4},{9,5},{10,... | collective-permute-start | bytes 786440 | tf_op jit(solution)/shard_map/ppermute | solution.py:152
  96.8 0.3 collective-permute-start.18
  97.1 11.1 %shard_map.133 = (f32[128,2048]{1,0:T(8,128)S(1)}, f32[128,2048]{1,0:T(8,128)S(1)}) custom-call(bf16[128,2048]{1,0:T(8,128)(2,1)} %collective-permute-done.10.refs_0_, bf16[128,2048]{1,0:T(8,128)(2,1)} %collective-permute-done.11.refs_1_, f32[128,16]{1,0:T(8,128)S(1)} %bitcast.56, bf16[704,2048]{1,0:T(8,128)(2,1)S(1)} %bitcast.42, ...), custom_call_target="tpu_custom_call" | custom-call | flops 4429185024 | bytes 17301504 | tf_op jit(solution)/shard_map/pallas_call | solution.py:76
  108.2 0.1 add_convert_fusion.6
  108.2 1.8 %collective-permute-start.15 = (bf16[128,2048]{1,0:T(8,128)(2,1)S(1)}, bf16[128,2048]{1,0:T(8,128)(2,1)S(1)}, u32[]{:S(2)}, u32[]{:S(2)}) collective-permute-start(bf16[128,2048]{1,0:T(8,128)(2,1)S(1)} %add_convert_fusion.6), channel_id=1, source_target_pairs={{0,2},{1,3},{2,6},{3,7},{4,0},{5,1},{6,10},{7,11},{8,4},{9,5},{10,... | collective-permute-start | bytes 1572872 | tf_op jit(solution)/shard_map/ppermute | solution.py:152
  110.0 0.1 add_convert_fusion.3
  110.1 0.5 collective-permute-start.19
  110.6 11.2 %shard_map.132 = (f32[128,2048]{1,0:T(8,128)S(1)}, f32[128,2048]{1,0:T(8,128)S(1)}) custom-call(bf16[128,2048]{1,0:T(8,128)(2,1)} %collective-permute-done.8.refs_0_, bf16[128,2048]{1,0:T(8,128)(2,1)} %collective-permute-done.9.refs_1_, f32[128,16]{1,0:T(8,128)S(1)} %bitcast.57, bf16[704,2048]{1,0:T(8,128)(2,1)S(1)} %bitcast.43, ...), custom_call_target="tpu_custom_call" | custom-call | flops 4429185024 | bytes 17301504 | tf_op jit(solution)/shard_map/pallas_call | solution.py:76
  121.9 0.0 copy-start.3
  121.9 0.1 add_convert_fusion.5
  122.0 1.8 %collective-permute-start.16 = (bf16[128,2048]{1,0:T(8,128)(2,1)S(1)}, bf16[128,2048]{1,0:T(8,128)(2,1)S(1)}, u32[]{:S(2)}, u32[]{:S(2)}) collective-permute-start(bf16[128,2048]{1,0:T(8,128)(2,1)S(1)} %add_convert_fusion.5), channel_id=1, source_target_pairs={{0,2},{1,3},{2,6},{3,7},{4,0},{5,1},{6,10},{7,11},{8,4},{9,5},{10,... | collective-permute-start | bytes 1572872 | tf_op jit(solution)/shard_map/ppermute | solution.py:152
  123.8 0.1 add_convert_fusion.2
  123.9 0.3 collective-permute-start.20
  124.3 13.7 %shard_map.131 = (f32[128,2048]{1,0:T(8,128)S(1)}, f32[128,2048]{1,0:T(8,128)S(1)}, f32[128,2048]{1,0:T(8,128)S(1)}) custom-call(bf16[128,2048]{1,0:T(8,128)(2,1)S(1)} %copy-done.8, bf16[128,2048]{1,0:T(8,128)(2,1)} %collective-permute-done.refs_1_, bf16[128,2048]{1,0:T(8,128)(2,1)} %collective-permute-done.1.refs_2_, f32[128,16]{1,0:T(8,128)S(1)} %bitcast.58, ...), custom_call_target="tpu_custom_call" | custom-call | flops 6643777536 | bytes 17301504 | tf_op jit(solution)/shard_map/pallas_call | solution.py:76
  138.0 1.0 copy-done.6
  138.9 0.1 add_convert_fusion.4
  139.1 1.8 %collective-permute-start.17 = (bf16[128,2048]{1,0:T(8,128)(2,1)S(1)}, bf16[128,2048]{1,0:T(8,128)(2,1)S(1)}, u32[]{:S(2)}, u32[]{:S(2)}) collective-permute-start(bf16[128,2048]{1,0:T(8,128)(2,1)S(1)} %add_convert_fusion.4), channel_id=1, source_target_pairs={{0,2},{1,3},{2,6},{3,7},{4,0},{5,1},{6,10},{7,11},{8,4},{9,5},{10,... | collective-permute-start | bytes 1572872 | tf_op jit(solution)/shard_map/ppermute | solution.py:152
  140.9 0.9 add_convert_fusion.1
  141.8 0.3 collective-permute-start.21
  142.0 2.4 %shard_map.135 = bf16[128,2048]{1,0:T(8,128)(2,1)} custom-call(bf16[128,2048]{1,0:T(8,128)(2,1)} %bitcast.24.arrived_ref, s32[16,16]{1,0:T(8,128)} %counts_ref.1, s32[1,16]{1,0:T(1,128)} %bitcast.60, s32[1]{0:T(128)} %bitcast.10.me_ref, bf16[128,2048]{1,0:T(8,128)(2,1)} %text_ref.1), custom_call_target="tpu_custom_call" | custom-call | tf_op jit(solution)/shard_map/pallas_call | solution.py:120
  144.4 5.3 %collective-permute-done.17 = bf16[128,2048]{1,0:T(8,128)(2,1)S(1)} collective-permute-done((bf16[128,2048]{1,0:T(8,128)(2,1)S(1)}, bf16[128,2048]{1,0:T(8,128)(2,1)S(1)}, u32[]{:S(2)}, u32[]{:S(2)}) %collective-permute-start.17) | collective-permute-done | bytes 524320 | tf_op jit(solution)/shard_map/ppermute | solution.py:152
  149.7 2.4 %collective-permute-done.21 = bf16[128,2048]{1,0:T(8,128)(2,1)S(1)} collective-permute-done((bf16[128,2048]{1,0:T(8,128)(2,1)}, bf16[128,2048]{1,0:T(8,128)(2,1)S(1)}, u32[]{:S(2)}, u32[]{:S(2)}) %collective-permute-start.21) | collective-permute-done | bytes 524320 | tf_op jit(solution)/shard_map/ppermute | solution.py:152
  152.1 1.0 add_convert_fusion
  (39 shorter events, 0.2 us)
Async XLA Ops:
  0.6 34.6 %copy-start = (bf16[1,16,8,2048]{3,2,1,0:T(8,128)(2,1)S(1)}, bf16[1,16,8,2048]{3,2,1,0:T(8,128)(2,1)}, u32[]{:S(2)}) copy-start(bf16[1,16,8,2048]{3,2,1,0:T(8,128)(2,1)} %param.18) | copy-start | bytes 1572868
  0.6 45.5 %copy-start.9 = (s32[8]{0:T(128)S(1)}, s32[8]{0:T(128)}, u32[]{:S(2)}) copy-start(s32[8]{0:T(128)} %constant.55.clone) | copy-start | bytes 100
  0.7 80.4 %copy-start.1 = (bf16[1,2048,704]{1,2,0:T(8,128)(2,1)S(1)}, bf16[1,2048,704]{1,2,0:T(8,128)(2,1)}, u32[]{:S(2)}) copy-start(bf16[1,2048,704]{1,2,0:T(8,128)(2,1)} %param.15) | copy-start | bytes 8650756
  0.7 80.3 %collective-permute-start.5 = (bf16[704,2048]{1,0:T(8,128)(2,1)}, bf16[704,2048]{1,0:T(8,128)(2,1)}, u32[]{:S(2)}, u32[]{:S(2)}) collective-permute-start(bf16[704,2048]{1,0:T(8,128)(2,1)} %bitcast.40), channel_id=1, source_target_pairs={{0,1},{1,0},{2,3},{3,2},{4,5},{5,4},{6,7},{7,6},{8,9},{9,8},{10,11... | collective-permute-start | bytes 8650760 | tf_op jit(solution)/shard_map/ppermute | solution.py:152
  1.2 79.8 %collective-permute-start.6 = (bf16[704,2048]{1,0:T(8,128)(2,1)}, bf16[704,2048]{1,0:T(8,128)(2,1)}, u32[]{:S(2)}, u32[]{:S(2)}) collective-permute-start(bf16[704,2048]{1,0:T(8,128)(2,1)} %bitcast.45), channel_id=1, source_target_pairs={{0,1},{1,0},{2,3},{3,2},{4,5},{5,4},{6,7},{7,6},{8,9},{9,8},{10,11... | collective-permute-start | bytes 8650760 | tf_op jit(solution)/shard_map/ppermute | solution.py:152
  1.3 79.7 %collective-permute-start.7 = (bf16[704,2048]{1,0:T(8,128)(2,1)}, bf16[704,2048]{1,0:T(8,128)(2,1)}, u32[]{:S(2)}, u32[]{:S(2)}) collective-permute-start(bf16[704,2048]{1,0:T(8,128)(2,1)} %bitcast.50), channel_id=1, source_target_pairs={{0,1},{1,0},{2,3},{3,2},{4,5},{5,4},{6,7},{7,6},{8,9},{9,8},{10,11... | collective-permute-start | bytes 8650760 | tf_op jit(solution)/shard_map/ppermute | solution.py:152
  4.0 4.5 %collective-permute-start.2 = (f32[1,16,128]{2,1,0:T(8,128)S(1)}, f32[1,16,128]{2,1,0:T(8,128)S(1)}, u32[]{:S(2)}, u32[]{:S(2)}) collective-permute-start(f32[1,16,128]{2,1,0:T(8,128)S(1)} %select_bitcast_fusion), channel_id=1, source_target_pairs={{0,2},{1,3},{2,0},{3,1},{4,6},{5,7},{6,4},{7,5},{8,10},{9,11},{10,... | collective-permute-start | bytes 24584 | tf_op jit(solution)/shard_map/ppermute | solution.py:152
  6.9 14.7 %collective-permute-start.1 = (bf16[128,2048]{1,0:T(8,128)(2,1)}, bf16[128,2048]{1,0:T(8,128)(2,1)}, u32[]{:S(2)}, u32[]{:S(2)}) collective-permute-start(bf16[128,2048]{1,0:T(8,128)(2,1)} %refs_0_.1), channel_id=1, source_target_pairs={{0,4},{1,5},{2,0},{3,1},{4,8},{5,9},{6,2},{7,3},{8,12},{9,13},{10,... | collective-permute-start | bytes 1572872 | tf_op jit(solution)/shard_map/ppermute | solution.py:152
  8.5 11.8 %collective-permute-start.3 = (f32[2,16,128]{2,1,0:T(8,128)S(1)}, f32[2,16,128]{2,1,0:T(8,128)S(1)}, u32[]{:S(2)}, u32[]{:S(2)}) collective-permute-start(f32[2,16,128]{2,1,0:T(8,128)S(1)} %pad_maximum_fusion.2), channel_id=1, source_target_pairs={{0,4},{1,5},{2,6},{3,7},{4,0},{5,1},{6,2},{7,3},{8,12},{9,13},{10,... | collective-permute-start | bytes 49160 | tf_op jit(solution)/shard_map/ppermute | solution.py:152
  20.3 14.1 %collective-permute-start = (bf16[128,2048]{1,0:T(8,128)(2,1)}, bf16[128,2048]{1,0:T(8,128)(2,1)}, u32[]{:S(2)}, u32[]{:S(2)}) collective-permute-start(bf16[128,2048]{1,0:T(8,128)(2,1)} %refs_0_.1), channel_id=1, source_target_pairs={{0,2},{1,3},{2,6},{3,7},{4,0},{5,1},{6,10},{7,11},{8,4},{9,5},{10,... | collective-permute-start | bytes 1572872 | tf_op jit(solution)/shard_map/ppermute | solution.py:152
  21.5 22.7 %collective-permute-start.9 = (bf16[128,2048]{1,0:T(8,128)(2,1)}, bf16[128,2048]{1,0:T(8,128)(2,1)}, u32[]{:S(2)}, u32[]{:S(2)}) collective-permute-start(bf16[128,2048]{1,0:T(8,128)(2,1)} %collective-permute-done.1.refs_2_), channel_id=1, source_target_pairs={{0,4},{1,5},{2,0},{3,1},{4,8},{5,9},{6,2},{7,3},{8,12},{9,13},{10,... | collective-permute-start | bytes 1572872 | tf_op jit(solution)/shard_map/ppermute | solution.py:152
  34.4 15.5 %collective-permute-start.8 = (bf16[128,2048]{1,0:T(8,128)(2,1)}, bf16[128,2048]{1,0:T(8,128)(2,1)}, u32[]{:S(2)}, u32[]{:S(2)}) collective-permute-start(bf16[128,2048]{1,0:T(8,128)(2,1)} %collective-permute-done.refs_1_), channel_id=1, source_target_pairs={{0,2},{1,3},{2,6},{3,7},{4,0},{5,1},{6,10},{7,11},{8,4},{9,5},{10,... | collective-permute-start | bytes 1572872 | tf_op jit(solution)/shard_map/ppermute | solution.py:152
  36.6 105.5 %all-to-all-start = ((bf16[16,8,2048]{2,1,0:T(8,128)(2,1)}), bf16[16,8,2048]{2,1,0:T(8,128)(2,1)}, u32[]{:S(2)}, u32[]{:S(2)}) async-start(bf16[16,8,2048]{2,1,0:T(8,128)(2,1)} %gather_fusion.2), calls=%async_computation | async-start | bytes 1048576 | tf_op jit(solution)/shard_map/all_to_all | solution.py:219
  44.3 18.9 %collective-permute-start.11 = (bf16[128,2048]{1,0:T(8,128)(2,1)}, bf16[128,2048]{1,0:T(8,128)(2,1)}, u32[]{:S(2)}, u32[]{:S(2)}) collective-permute-start(bf16[128,2048]{1,0:T(8,128)(2,1)} %collective-permute-done.9.refs_1_), channel_id=1, source_target_pairs={{0,4},{1,5},{2,0},{3,1},{4,8},{5,9},{6,2},{7,3},{8,12},{9,13},{10,... | collective-permute-start | bytes 1572872 | tf_op jit(solution)/shard_map/ppermute | solution.py:152
  49.8 21.6 %collective-permute-start.10 = (bf16[128,2048]{1,0:T(8,128)(2,1)}, bf16[128,2048]{1,0:T(8,128)(2,1)}, u32[]{:S(2)}, u32[]{:S(2)}) collective-permute-start(bf16[128,2048]{1,0:T(8,128)(2,1)} %collective-permute-done.8.refs_0_), channel_id=1, source_target_pairs={{0,2},{1,3},{2,6},{3,7},{4,0},{5,1},{6,10},{7,11},{8,4},{9,5},{10,... | collective-permute-start | bytes 1572872 | tf_op jit(solution)/shard_map/ppermute | solution.py:152
  63.2 9.9 %collective-permute-start.4 = (f32[4,16,128]{2,1,0:T(8,128)S(1)}, f32[4,16,128]{2,1,0:T(8,128)S(1)}, u32[]{:S(2)}, u32[]{:S(2)}) collective-permute-start(f32[4,16,128]{2,1,0:T(8,128)S(1)} %pad_maximum_fusion.1), channel_id=1, source_target_pairs={{0,8},{1,9},{2,10},{3,11},{4,12},{5,13},{6,14},{7,15},{8,0},{9,1},... | collective-permute-start | bytes 98312 | tf_op jit(solution)/shard_map/ppermute | solution.py:152
  71.4 7.9 %collective-permute-start.12 = (bf16[64,2048]{1,0:T(8,128)(2,1)}, bf16[64,2048]{1,0:T(8,128)(2,1)}, u32[]{:S(2)}, u32[]{:S(2)}) collective-permute-start(bf16[64,2048]{1,0:T(8,128)(2,1)} %slice.46), channel_id=1, source_target_pairs={{0,4},{1,5},{2,0},{3,1},{4,8},{5,9},{6,2},{7,3},{8,12},{9,13},{10,... | collective-permute-start | bytes 786440 | tf_op jit(solution)/shard_map/ppermute | solution.py:152
  73.2 7.8 %collective-permute-start.13 = (bf16[64,2048]{1,0:T(8,128)(2,1)}, bf16[64,2048]{1,0:T(8,128)(2,1)}, u32[]{:S(2)}, u32[]{:S(2)}) collective-permute-start(bf16[64,2048]{1,0:T(8,128)(2,1)} %slice.47), channel_id=1, source_target_pairs={{0,2},{1,3},{2,6},{3,7},{4,0},{5,1},{6,10},{7,11},{8,4},{9,5},{10,... | collective-permute-start | bytes 786440 | tf_op jit(solution)/shard_map/ppermute | solution.py:152
  81.0 1.8 %copy-start.2 = (bf16[1,2048,704]{1,2,0:T(8,128)(2,1)S(1)}, bf16[1,2048,704]{1,2,0:T(8,128)(2,1)}, u32[]{:S(2)}) copy-start(bf16[1,2048,704]{1,2,0:T(8,128)(2,1)} %param.16) | copy-start | bytes 8650756
  82.8 1.8 %copy-start.4 = (bf16[1,704,2048]{2,1,0:T(8,128)(2,1)S(1)}, bf16[1,704,2048]{2,1,0:T(8,128)(2,1)}, u32[]{:S(2)}) copy-start(bf16[1,704,2048]{2,1,0:T(8,128)(2,1)} %param.17) | copy-start | bytes 8650756
  95.0 13.2 %collective-permute-start.14 = (bf16[64,2048]{1,0:T(8,128)(2,1)S(1)}, bf16[64,2048]{1,0:T(8,128)(2,1)S(1)}, u32[]{:S(2)}, u32[]{:S(2)}) collective-permute-start(bf16[64,2048]{1,0:T(8,128)(2,1)S(1)} %get-tuple-element.16), channel_id=1, source_target_pairs={{0,2},{1,3},{2,6},{3,7},{4,0},{5,1},{6,10},{7,11},{8,4},{9,5},{10,... | collective-permute-start | bytes 786440 | tf_op jit(solution)/shard_map/ppermute | solution.py:152
  96.8 13.3 %collective-permute-start.18 = (bf16[64,2048]{1,0:T(8,128)(2,1)S(1)}, bf16[64,2048]{1,0:T(8,128)(2,1)S(1)}, u32[]{:S(2)}, u32[]{:S(2)}) collective-permute-start(bf16[64,2048]{1,0:T(8,128)(2,1)S(1)} %get-tuple-element.17), channel_id=1, source_target_pairs={{0,4},{1,5},{2,0},{3,1},{4,8},{5,9},{6,2},{7,3},{8,12},{9,13},{10,... | collective-permute-start | bytes 786440 | tf_op jit(solution)/shard_map/ppermute | solution.py:152
  108.2 13.7 %collective-permute-start.15 = (bf16[128,2048]{1,0:T(8,128)(2,1)S(1)}, bf16[128,2048]{1,0:T(8,128)(2,1)S(1)}, u32[]{:S(2)}, u32[]{:S(2)}) collective-permute-start(bf16[128,2048]{1,0:T(8,128)(2,1)S(1)} %add_convert_fusion.6), channel_id=1, source_target_pairs={{0,2},{1,3},{2,6},{3,7},{4,0},{5,1},{6,10},{7,11},{8,4},{9,5},{10,... | collective-permute-start | bytes 1572872 | tf_op jit(solution)/shard_map/ppermute | solution.py:152
  110.1 13.7 %collective-permute-start.19 = (bf16[128,2048]{1,0:T(8,128)(2,1)S(1)}, bf16[128,2048]{1,0:T(8,128)(2,1)S(1)}, u32[]{:S(2)}, u32[]{:S(2)}) collective-permute-start(bf16[128,2048]{1,0:T(8,128)(2,1)S(1)} %add_convert_fusion.3), channel_id=1, source_target_pairs={{0,4},{1,5},{2,0},{3,1},{4,8},{5,9},{6,2},{7,3},{8,12},{9,13},{10,... | collective-permute-start | bytes 1572872 | tf_op jit(solution)/shard_map/ppermute | solution.py:152
  110.6 13.6 %copy-start.5 = (bf16[1,704,2048]{2,1,0:T(8,128)(2,1)S(1)}, bf16[1,704,2048]{2,1,0:T(8,128)(2,1)}, u32[]{:S(2)}) copy-start(bf16[1,704,2048]{2,1,0:T(8,128)(2,1)} %param.17) | copy-start | bytes 8650756
  121.9 2.4 %copy-start.3 = (bf16[1,2048,704]{1,2,0:T(8,128)(2,1)S(1)}, bf16[1,2048,704]{1,2,0:T(8,128)(2,1)}, u32[]{:S(2)}) copy-start(bf16[1,2048,704]{1,2,0:T(8,128)(2,1)} %param.16) | copy-start | bytes 8650756
  121.9 2.4 %copy-start.8 = (bf16[128,2048]{1,0:T(8,128)(2,1)S(1)}, bf16[128,2048]{1,0:T(8,128)(2,1)}, u32[]{:S(2)}) copy-start(bf16[128,2048]{1,0:T(8,128)(2,1)} %refs_0_.1) | copy-start | bytes 1572868
  122.0 16.9 %collective-permute-start.16 = (bf16[128,2048]{1,0:T(8,128)(2,1)S(1)}, bf16[128,2048]{1,0:T(8,128)(2,1)S(1)}, u32[]{:S(2)}, u32[]{:S(2)}) collective-permute-start(bf16[128,2048]{1,0:T(8,128)(2,1)S(1)} %add_convert_fusion.5), channel_id=1, source_target_pairs={{0,2},{1,3},{2,6},{3,7},{4,0},{5,1},{6,10},{7,11},{8,4},{9,5},{10,... | collective-permute-start | bytes 1572872 | tf_op jit(solution)/shard_map/ppermute | solution.py:152
  123.9 16.9 %collective-permute-start.20 = (bf16[128,2048]{1,0:T(8,128)(2,1)S(1)}, bf16[128,2048]{1,0:T(8,128)(2,1)S(1)}, u32[]{:S(2)}, u32[]{:S(2)}) collective-permute-start(bf16[128,2048]{1,0:T(8,128)(2,1)S(1)} %add_convert_fusion.2), channel_id=1, source_target_pairs={{0,4},{1,5},{2,0},{3,1},{4,8},{5,9},{6,2},{7,3},{8,12},{9,13},{10,... | collective-permute-start | bytes 1572872 | tf_op jit(solution)/shard_map/ppermute | solution.py:152
  138.0 1.0 copy-start.6
  138.9 13.1 %copy-start.7 = (f32[128,2048]{1,0:T(8,128)S(1)}, f32[128,2048]{1,0:T(8,128)}, u32[]{:S(2)}) copy-start(f32[128,2048]{1,0:T(8,128)} %copy-done.6) | copy-start | bytes 3145732
  139.1 10.7 %collective-permute-start.17 = (bf16[128,2048]{1,0:T(8,128)(2,1)S(1)}, bf16[128,2048]{1,0:T(8,128)(2,1)S(1)}, u32[]{:S(2)}, u32[]{:S(2)}) collective-permute-start(bf16[128,2048]{1,0:T(8,128)(2,1)S(1)} %add_convert_fusion.4), channel_id=1, source_target_pairs={{0,2},{1,3},{2,6},{3,7},{4,0},{5,1},{6,10},{7,11},{8,4},{9,5},{10,... | collective-permute-start | bytes 1572872 | tf_op jit(solution)/shard_map/ppermute | solution.py:152
  141.8 10.3 %collective-permute-start.21 = (bf16[128,2048]{1,0:T(8,128)(2,1)}, bf16[128,2048]{1,0:T(8,128)(2,1)S(1)}, u32[]{:S(2)}, u32[]{:S(2)}) collective-permute-start(bf16[128,2048]{1,0:T(8,128)(2,1)} %add_convert_fusion.1), channel_id=1, source_target_pairs={{0,4},{1,5},{2,0},{3,1},{4,8},{5,9},{6,2},{7,3},{8,12},{9,13},{10,... | collective-permute-start | bytes 1572872 | tf_op jit(solution)/shard_map/ppermute | solution.py:152

commit v2 on v1

v2 whole, which is shorter than its diff:
```python
import functools

import jax
import jax.numpy as jnp
from jax import lax
from jax.experimental import pallas as pl
from jax.experimental.pallas import tpu as pltpu
from jax.sharding import PartitionSpec as P

route_scale = 2.446
NT = (((1,), (1,)), ((), ()))


def ring_of(chips):
    if chips <= 8:
        return list(range(0, chips, 2)) + list(range(chips - 1, 0, -2))
    return list(range(chips))


def payload_kernel(picks_ref, router_ref, tokens_ref, out_ref):
    rows, width = tokens_ref.shape
    experts = router_ref.shape[0]
    spare = out_ref.shape[1] - width
    tokens = tokens_ref[...]
    out_ref[:, :width] = tokens
    logits = lax.dot_general(router_ref[...], tokens, NT, preferred_element_type=jnp.float32)
    score = 1.0 / (1.0 + jnp.exp(-logits))
    expert = lax.broadcasted_iota(jnp.int32, (experts, rows), 0)
    picked = expert == picks_ref[0:1, :]
    for k in range(1, picks_ref.shape[0]):
        picked = jnp.logical_or(picked, expert == picks_ref[k : k + 1, :])
    total = jnp.sum(jnp.where(picked, score, 0.0), axis=0, keepdims=True)
    route = jnp.where(picked, route_scale * score / total, 0.0)
    parts = []
    for _ in range(3):
        part = route.astype(jnp.bfloat16)
        parts.append(part.astype(jnp.float32))
        route = route - parts[-1]
    parts = jnp.concatenate(parts + [jnp.zeros((spare - 3 * experts, rows), jnp.float32)], axis=0)
    square = (rows, rows)
    eye = lax.broadcasted_iota(jnp.int32, square, 0) == lax.broadcasted_iota(jnp.int32, square, 1)
    turned = lax.dot_general(
        eye.astype(jnp.bfloat16), parts.astype(jnp.bfloat16), NT, preferred_element_type=jnp.float32
    )
    out_ref[:, width:] = turned.astype(jnp.bfloat16)


def payload_of(tokens, expert_picks, router):
    rows, width = tokens.shape
    spare = -(-3 * router.shape[1] // 128) * 128
    vmem = pl.BlockSpec(memory_space=pltpu.VMEM)
    return pl.pallas_call(
        payload_kernel,
        out_shape=jax.ShapeDtypeStruct((rows, width + spare), tokens.dtype),
        in_specs=[vmem] * 3,
        out_specs=vmem,
    )(expert_picks.T, router.T, tokens)


def ffn_kernel(count, sizes, experts, me_ref, *refs):
    shards = refs[:count]
    weights = refs[count : count + 6]
    outs = refs[count + 6 : -3]
    x, hidden, total = refs[-3:]
    rows = sum(sizes)
    width = x.shape[1]
    block = rows // len(outs)
    tails = []
    at = 0
    for ref, m in zip(shards, sizes):
        x[pl.ds(at, m), :] = ref[:, :width]
        tails.append(ref[:, width:].astype(jnp.float32))
        at += m
    tail = jnp.concatenate(tails, axis=0)
    lane = lax.broadcasted_iota(jnp.int32, tail.shape, 1)
    lane = jnp.where(lane < 3 * experts, lane % experts, -1)
    for e in range(2):
        wg, wu, wd = weights[3 * e : 3 * e + 3]
        wanted = me_ref[0] if e == 0 else me_ref[0] + 1 - 2 * (me_ref[0] % 2)
        route = jnp.sum(jnp.where(lane == wanted, tail, 0.0), axis=1, keepdims=True)
        gate = lax.dot_general(x[...], wg[...], NT, preferred_element_type=jnp.float32)
        upward = lax.dot_general(x[...], wu[...], NT, preferred_element_type=jnp.float32)
        hidden[...] = (gate / (1.0 + jnp.exp(-gate)) * upward).astype(jnp.bfloat16)
        for a in range(0, width, 512):
            lanes = pl.ds(a, 512)
            row = jnp.dot(hidden[...], wd[:, lanes], preferred_element_type=jnp.float32)
            row = row.astype(jnp.bfloat16).astype(jnp.float32) * route
            if e == 0:
                total[:, lanes] = row
            else:
                row = total[:, lanes] + row
                for k, out in enumerate(outs):
                    out[:, lanes] = row[k * block : (k + 1) * block].astype(out.dtype)


def ffn(shards, results, me, weights, experts, dtype):
    sizes = [s.shape[0] for s in shards]
    rows = sum(sizes)
    ff, width = weights[0].shape
    block = rows // results
    vmem = pl.BlockSpec(memory_space=pltpu.VMEM)
    return pl.pallas_call(
        functools.partial(ffn_kernel, len(shards), sizes, experts),
        out_shape=[jax.ShapeDtypeStruct((block, width), dtype)] * results,
        in_specs=[pl.BlockSpec(memory_space=pltpu.SMEM)] + [vmem] * (len(shards) + 6),
        out_specs=[vmem] * results,
        scratch_shapes=[
            pltpu.VMEM((rows, width), jnp.bfloat16),
            pltpu.VMEM((rows, ff), jnp.bfloat16),
            pltpu.VMEM((rows, width), jnp.float32),
        ],
        compiler_params=pltpu.CompilerParams(vmem_limit_bytes=30 * 2**20),
        cost_estimate=pl.CostEstimate(
            flops=12 * rows * ff * width, bytes_accessed=12 * ff * width, transcendentals=2 * rows * ff
        ),
    )(me[None], *shards, *weights)


def place_kernel(slots, arrived_ref, counts_ref, owner_ref, me_ref, text_ref, out_ref):
    rows = text_ref.shape[0]
    devices = counts_ref.shape[0]
    held = arrived_ref.shape[0]
    mine = (owner_ref[...] == me_ref[0]).astype(jnp.int32)
    live = jnp.sum(counts_ref[...] * mine, axis=1, keepdims=True)
    total = jnp.sum(live)
    lane = lax.broadcasted_iota(jnp.int32, (devices, held), 1)
    holder = lane // slots
    which = lax.broadcasted_iota(jnp.int32, (devices, held), 0)
    own = jnp.sum(jnp.where(which == holder, live, 0), axis=0, keepdims=True)
    start = jnp.sum(jnp.where(which < holder, live, 0), axis=0, keepdims=True)
    offset = lane[:1] - holder[:1] * slots
    place = jnp.where(offset < own, start + offset, -1)
    row = lax.broadcasted_iota(jnp.int32, (rows, held), 0)
    pick = (row == place).astype(jnp.bfloat16)
    image = jnp.dot(pick, arrived_ref[...], preferred_element_type=jnp.float32).astype(jnp.bfloat16)
    position = lax.broadcasted_iota(jnp.int32, (rows, 1), 0)
    out_ref[...] = jnp.where(position < total, image, text_ref[...])


def place_images(arrived, counts, owner, me, text_block, slots):
    vmem = pl.BlockSpec(memory_space=pltpu.VMEM)
    return pl.pallas_call(
        functools.partial(place_kernel, slots),
        out_shape=jax.ShapeDtypeStruct(text_block.shape, text_block.dtype),
        in_specs=[vmem, vmem, vmem, pl.BlockSpec(memory_space=pltpu.SMEM), vmem],
        out_specs=vmem,
    )(arrived, counts, owner[None, :], me[None], text_block)


def local(
    tokens,
    expert_picks,
    router,
    gate_weight,
    up_weight,
    down_weight,
    image_rows,
    image_counts,
    span_owner,
    text_rows,
):
    devices = lax.axis_size("expert")
    me = lax.axis_index("expert")
    rows, width = tokens.shape
    half = rows // 2
    experts = gate_weight.shape[0] * devices
    slots = image_rows.shape[2]
    chips = devices // 2
    far = chips // 2
    ring = ring_of(chips)
    pos = {c: i for i, c in enumerate(ring)}

    def send(x, pairs):
        return lax.ppermute(x, "expert", pairs)

    def by_chip(target):
        return [(2 * c + k, 2 * target(c) + k) for c in range(chips) for k in range(2)]

    up = by_chip(lambda c: ring[(pos[c] + 1) % chips])
    down = by_chip(lambda c: ring[(pos[c] - 1) % chips])
    sibling = [(d, d ^ 1) for d in range(devices)]

    own = [gate_weight[0].T, up_weight[0].T, down_weight[0]]
    weights = own + [send(w, sibling) for w in own]
    weights = [pltpu.with_memory_space_constraint(w, pltpu.VMEM) for w in weights]

    mine = payload_of(tokens, expert_picks, router)
    from_below, from_above = [mine], [mine]
    for s in range(1, far):
        from_below.append(send(from_below[-1], up))
        from_above.append(send(from_above[-1], down))
    last = [send(from_below[-1][:half], up), send(from_above[-1][half:], down)]

    sums = {}
    for s in range(1, far):
        shards, columns = [from_above[s], from_below[s]], [s, chips - s]
        if s == 1:
            shards, columns = [mine] + shards, [0] + columns
        for c, value in zip(columns, ffn(shards, len(columns), me, weights, experts, jnp.float32)):
            sums[c] = value
    (farthest,) = ffn(last, 1, me, weights, experts, jnp.bfloat16)

    def low(x):
        return x.astype(jnp.bfloat16)

    def wide(x):
        return x.astype(jnp.float32)

    going_down = send(farthest[:half], down)
    going_up = send(farthest[half:], up)
    going_down = low(sums[chips - far + 1] + jnp.pad(wide(going_down), ((0, rows - half), (0, 0))))
    going_up = low(sums[far - 1] + jnp.pad(wide(going_up), ((half, 0), (0, 0))))
    for s in range(far - 1, 0, -1):
        going_down = send(going_down, down)
        going_up = send(going_up, up)
        if s > 1:
            going_down = low(sums[chips - s + 1] + wide(going_down))
            going_up = low(sums[s - 1] + wide(going_up))
    moe_out = low(sums[0] + wide(going_down) + wide(going_up))

    number = jnp.arange(devices, dtype=jnp.int32)
    span_of = jnp.sum(jnp.where(span_owner[:, None] == number[None, :], number[:, None], 0), axis=0)
    image_send, _ = lax.optimization_barrier((image_rows[0][span_of], from_below[-1]))
    arrived = lax.all_to_all(image_send, "expert", split_axis=0, concat_axis=0, tiled=True)
    next_span = place_images(
        arrived.reshape(devices * slots, width), image_counts, span_owner, me, text_rows, slots
    )
    return (moe_out, next_span)


def solution(mesh):
    return jax.shard_map(
        local,
        mesh=mesh,
        in_specs=(
            P(("groups", "expert"), None),
            P(("groups", "expert"), None),
            P(),
            P("expert", None, None),
            P("expert", None, None),
            P("expert", None, None),
            P(("groups", "expert"), None, None, None),
            P("groups", None),
            P("groups"),
            P(("groups", "expert"), None),
        ),
        out_specs=(P(("groups", "expert"), None), P(("groups", "expert"), None)),
        check_vma=False,
    )
```

time: 154 us -> 128 us (0.83)
  starting transfers between devices: 35.6 us -> 24.2 us
  Pallas kernels: 48.6 us -> 42.3 us
  waiting for transfers between devices: 49.8 us -> 45.6 us
  local copies, waits for them, and re-layouts: 12.9 us -> 11 us
    ppermute x22 -> x19, starting transfers between devices: 29.8 us -> 18.7 us  [send(): return lax.ppermute(x, 'expert', pairs)]
    pallas_call x4 -> x5, Pallas kernels: 46.2 us -> 39.9 us  [the longest x4 37.5 us: ffn(): pl.pallas_call(functools.partial(ffn_kernel, len(shards), sizes, experts)...]
    ppermute x22 -> x19, waiting for transfers between devices: 49.7 us -> 45.6 us  [send(): return lax.ppermute(x, 'expert', pairs)]
    unnamed x20 -> x26, local copies, waits for them, and re-layouts: 4.64 us -> 6.27 us
  transfers between devices with their start and end apart: 23 -> 20, of which waited for: 9 -> 7; matrix products, arithmetic and copies ran while one was open for 8% -> 5% of each run, Pallas kernels for 32% -> 33%
where the time goes in v2:
time: 128 us; the launch traced here: 127 us
  waiting for transfers between devices  45.6 us (36%)
  Pallas kernels  42.3 us (33%)
  starting transfers between devices  24.2 us (19%)
  local copies, waits for them, and re-layouts  11 us (9%)
  other arithmetic  3.18 us (2%)
    ppermute x19, waiting for transfers between devices, send(): return lax.ppermute(x, 'expert', pairs)  45.6 us
    pallas_call x4, Pallas kernels, ffn(): pl.pallas_call(functools.partial(ffn_kernel, len(shards), sizes, experts)...  37.5 us
    ppermute x19, starting transfers between devices, send(): return lax.ppermute(x, 'expert', pairs)  18.7 us
    unnamed x26, local copies, waits for them, and re-layouts  6.27 us
    all_to_all x1, starting transfers between devices, local(): lax.all_to_all(image_send, 'expert', split_axis=0, concat_axis=0, tiled=T...  5.56 us
    slice x2, local copies, waits for them, and re-layouts, local(): last = [send(from_below[-1][:half], up), send(from_above[-1][half:], down)]  3.36 us
  transfers between devices with their start and end apart: 20, of which 7 were waited for; matrix products, arithmetic and copies ran while one was open for 5% of the time, Pallas kernels for 33%

profile of v2, /device:TPU:0, one launch (start us, length us, event | category | flops | bytes accessed | tf_op | source)
XLA Modules:
  0.0 127.2 jit_solution(7713863772601543679)
XLA Ops:
  0.6 0.0 copy-start
  0.7 0.5 collective-permute-start.2
  1.2 0.1 collective-permute-start.3
  1.3 0.4 collective-permute-start.4
  1.7 2.4 %shard_map.113.refs_0_ = bf16[128,2176]{1,0:T(8,128)(2,1)} custom-call(s32[6,128]{1,0:T(8,128)} %bitcast.34, bf16[16,2048]{1,0:T(8,128)(2,1)} %bitcast.33, bf16[128,2048]{1,0:T(8,128)(2,1)} %tokens_ref.1), custom_call_target="tpu_custom_call" | custom-call | tf_op jit(solution)/shard_map/pallas_call | solution.py:52
  4.0 3.0 %collective-permute-start.1 = (bf16[128,2176]{1,0:T(8,128)(2,1)}, bf16[128,2176]{1,0:T(8,128)(2,1)S(1)}, u32[]{:S(2)}, u32[]{:S(2)}) collective-permute-start(bf16[128,2176]{1,0:T(8,128)(2,1)} %shard_map.113.refs_0_), channel_id=1, source_target_pairs={{0,4},{1,5},{2,0},{3,1},{4,8},{5,9},{6,2},{7,3},{8,12},{9,13},{10,... | collective-permute-start | bytes 1671176 | tf_op jit(solution)/shard_map/ppermute | solution.py:174
  7.0 0.0 collective-permute-start
  7.0 13.0 %collective-permute-done.1.refs_2_ = bf16[128,2176]{1,0:T(8,128)(2,1)S(1)} collective-permute-done((bf16[128,2176]{1,0:T(8,128)(2,1)}, bf16[128,2176]{1,0:T(8,128)(2,1)S(1)}, u32[]{:S(2)}, u32[]{:S(2)}) %collective-permute-start.1) | collective-permute-done | bytes 557088 | tf_op jit(solution)/shard_map/ppermute | solution.py:174
  20.1 1.8 %collective-permute-start.6 = (bf16[128,2176]{1,0:T(8,128)(2,1)S(1)}, bf16[128,2176]{1,0:T(8,128)(2,1)}, u32[]{:S(2)}, u32[]{:S(2)}) collective-permute-start(bf16[128,2176]{1,0:T(8,128)(2,1)S(1)} %collective-permute-done.1.refs_2_), channel_id=1, source_target_pairs={{0,4},{1,5},{2,0},{3,1},{4,8},{5,9},{6,2},{7,3},{8,12},{9,13},{10,... | collective-permute-start | bytes 1671176 | tf_op jit(solution)/shard_map/ppermute | solution.py:174
  21.9 0.8 copy-done.9
  22.7 0.0 collective-permute-done.refs_1_
  22.7 0.2 collective-permute-start.5
  22.9 0.8 copy-done.11
  23.7 10.6 %collective-permute-done.6.refs_1_ = bf16[128,2176]{1,0:T(8,128)(2,1)} collective-permute-done((bf16[128,2176]{1,0:T(8,128)(2,1)S(1)}, bf16[128,2176]{1,0:T(8,128)(2,1)}, u32[]{:S(2)}, u32[]{:S(2)}) %collective-permute-start.6) | collective-permute-done | bytes 557088 | tf_op jit(solution)/shard_map/ppermute | solution.py:174
  34.3 1.5 %collective-permute-start.8 = (bf16[128,2176]{1,0:T(8,128)(2,1)}, bf16[128,2176]{1,0:T(8,128)(2,1)}, u32[]{:S(2)}, u32[]{:S(2)}) collective-permute-start(bf16[128,2176]{1,0:T(8,128)(2,1)} %collective-permute-done.6.refs_1_), channel_id=1, source_target_pairs={{0,4},{1,5},{2,0},{3,1},{4,8},{5,9},{6,2},{7,3},{8,12},{9,13},{10,... | collective-permute-start | bytes 1671176 | tf_op jit(solution)/shard_map/ppermute | solution.py:174
  35.8 0.5 collective-permute-done.5.refs_0_
  36.3 0.5 collective-permute-start.7
  36.9 0.7 select_reduce_fusion
  37.6 10.2 %collective-permute-done.8.refs_1_ = bf16[128,2176]{1,0:T(8,128)(2,1)} collective-permute-done((bf16[128,2176]{1,0:T(8,128)(2,1)}, bf16[128,2176]{1,0:T(8,128)(2,1)}, u32[]{:S(2)}, u32[]{:S(2)}) %collective-permute-start.8) | collective-permute-done | bytes 557088 | tf_op jit(solution)/shard_map/ppermute | solution.py:174
  47.8 1.7 %slice.18 = bf16[64,2176]{1,0:T(8,128)(2,1)} slice(bf16[128,2176]{1,0:T(8,128)(2,1)} %collective-permute-done.8.refs_1_), slice={[0:64], [0:2176]} | slice | bytes 557056 | tf_op jit(solution)/shard_map/slice | solution.py:192
  49.5 1.1 collective-permute-start.9
  50.7 0.0 collective-permute-done.7.refs_0_
  50.7 1.7 %slice.19 = bf16[64,2176]{1,0:T(8,128)(2,1)} slice(bf16[128,2176]{1,0:T(8,128)(2,1)} %collective-permute-done.7.refs_0_), slice={[64:128], [0:2176]} | slice | bytes 557056 | tf_op jit(solution)/shard_map/slice | solution.py:192
  52.3 0.9 collective-permute-start.10
  53.2 1.4 %gather_fusion = bf16[16,8,2048]{2,1,0:T(8,128)(2,1)} fusion(bf16[16,8,2048]{2,1,0:T(8,128)(2,1)S(1)} %bitcast.17, s32[1024]{0:T(1024)S(1)} %pad_clamp_fusion), kind=kCustom, calls=%fused_computation | custom fusion | bytes 1048640 | tf_op jit(solution)/shard_map/gather | solution.py:223
  54.6 5.6 %all-to-all-start = ((bf16[16,8,2048]{2,1,0:T(8,128)(2,1)}), bf16[16,8,2048]{2,1,0:T(8,128)(2,1)}, u32[]{:S(2)}, u32[]{:S(2)}) async-start(bf16[16,8,2048]{2,1,0:T(8,128)(2,1)} %gather_fusion), calls=%async_computation | async-start | bytes 1048576 | tf_op jit(solution)/shard_map/all_to_all | solution.py:224
  60.2 0.0 collective-permute-done.9.refs_0_
  60.2 0.0 collective-permute-done.10.refs_1_
  60.2 0.0 collective-permute-done.2.refs_6_.refs_5_
  60.2 0.0 collective-permute-done.4.refs_8_.refs_7_
  60.2 0.0 copy-start.2
  60.3 1.8 %copy-done.2 = bf16[1,2048,704]{1,2,0:T(8,128)(2,1)S(1)} copy-done((bf16[1,2048,704]{1,2,0:T(8,128)(2,1)S(1)}, bf16[1,2048,704]{1,2,0:T(8,128)(2,1)}, u32[]{:S(2)}) %copy-start.2) | copy-done | bytes 2883608
  62.1 1.8 %copy-done.4 = bf16[1,704,2048]{2,1,0:T(8,128)(2,1)S(1)} copy-done((bf16[1,704,2048]{2,1,0:T(8,128)(2,1)S(1)}, bf16[1,704,2048]{2,1,0:T(8,128)(2,1)}, u32[]{:S(2)}) %copy-start.4) | copy-done | bytes 2883608
  63.9 8.3 %shard_map.117 = bf16[128,2048]{1,0:T(8,128)(2,1)S(1)} custom-call(s32[1]{0:T(128)} %bitcast.me_ref, bf16[64,2176]{1,0:T(8,128)(2,1)} %collective-permute-done.9.refs_0_, bf16[64,2176]{1,0:T(8,128)(2,1)} %collective-permute-done.10.refs_1_, bf16[704,2048]{1,0:T(8,128)(2,1)S(1)} %bitcast.19, bf16[704,2048]{1,0:T(8,128)(2,1)S(1)} %bitcast.24, ...), custom_call_target="tpu_custom_call" | custom-call | flops 2214592512 | bytes 17301504 | tf_op jit(solution)/shard_map/pallas_call | solution.py:102
  72.3 1.9 %collective-permute-start.11 = (bf16[64,2048]{1,0:T(8,128)(2,1)S(1)}, bf16[64,2048]{1,0:T(8,128)(2,1)S(1)}, u32[]{:S(2)}, u32[]{:S(2)}) collective-permute-start(bf16[64,2048]{1,0:T(8,128)(2,1)S(1)} %get-tuple-element.18), channel_id=1, source_target_pairs={{0,2},{1,3},{2,6},{3,7},{4,0},{5,1},{6,10},{7,11},{8,4},{9,5},{10,... | collective-permute-start | bytes 786440 | tf_op jit(solution)/shard_map/ppermute | solution.py:174
  74.2 0.2 collective-permute-start.15
  74.4 9.0 %shard_map.116 = (f32[128,2048]{1,0:T(8,128)S(1)}, f32[128,2048]{1,0:T(8,128)S(1)}) custom-call(s32[1]{0:T(128)} %bitcast.me_ref, bf16[128,2176]{1,0:T(8,128)(2,1)} %collective-permute-done.7.refs_0_, bf16[128,2176]{1,0:T(8,128)(2,1)} %collective-permute-done.8.refs_1_, bf16[704,2048]{1,0:T(8,128)(2,1)S(1)} %bitcast.20, bf16[704,2048]{1,0:T(8,128)(2,1)S(1)} %bitcast.25, ...), custom_call_target="tpu_custom_call" | custom-call | flops 4429185024 | bytes 17301504 | tf_op jit(solution)/shard_map/pallas_call | solution.py:102
  83.4 0.0 collective-permute-done.11
  83.4 0.1 add_convert_fusion.6
  83.5 1.9 %collective-permute-start.12 = (bf16[128,2048]{1,0:T(8,128)(2,1)S(1)}, bf16[128,2048]{1,0:T(8,128)(2,1)S(1)}, u32[]{:S(2)}, u32[]{:S(2)}) collective-permute-start(bf16[128,2048]{1,0:T(8,128)(2,1)S(1)} %add_convert_fusion.6), channel_id=1, source_target_pairs={{0,2},{1,3},{2,6},{3,7},{4,0},{5,1},{6,10},{7,11},{8,4},{9,5},{10,... | collective-permute-start | bytes 1572872 | tf_op jit(solution)/shard_map/ppermute | solution.py:174
  85.4 0.0 collective-permute-done.15
  85.4 0.1 add_convert_fusion.3
  85.5 0.4 collective-permute-start.16
  85.9 9.1 %shard_map.115 = (f32[128,2048]{1,0:T(8,128)S(1)}, f32[128,2048]{1,0:T(8,128)S(1)}) custom-call(s32[1]{0:T(128)} %bitcast.me_ref, bf16[128,2176]{1,0:T(8,128)(2,1)} %collective-permute-done.5.refs_0_, bf16[128,2176]{1,0:T(8,128)(2,1)} %collective-permute-done.6.refs_1_, bf16[704,2048]{1,0:T(8,128)(2,1)S(1)} %bitcast.21, bf16[704,2048]{1,0:T(8,128)(2,1)S(1)} %bitcast.26, ...), custom_call_target="tpu_custom_call" | custom-call | flops 4429185024 | bytes 17301504 | tf_op jit(solution)/shard_map/pallas_call | solution.py:102
  95.0 0.0 copy-start.3
  95.0 2.1 %collective-permute-done.12 = bf16[128,2048]{1,0:T(8,128)(2,1)S(1)} collective-permute-done((bf16[128,2048]{1,0:T(8,128)(2,1)S(1)}, bf16[128,2048]{1,0:T(8,128)(2,1)S(1)}, u32[]{:S(2)}, u32[]{:S(2)}) %collective-permute-start.12) | collective-permute-done | bytes 524320 | tf_op jit(solution)/shard_map/ppermute | solution.py:174
  97.1 0.1 add_convert_fusion.5
  97.3 1.7 %collective-permute-start.13 = (bf16[128,2048]{1,0:T(8,128)(2,1)S(1)}, bf16[128,2048]{1,0:T(8,128)(2,1)S(1)}, u32[]{:S(2)}, u32[]{:S(2)}) collective-permute-start(bf16[128,2048]{1,0:T(8,128)(2,1)S(1)} %add_convert_fusion.5), channel_id=1, source_target_pairs={{0,2},{1,3},{2,6},{3,7},{4,0},{5,1},{6,10},{7,11},{8,4},{9,5},{10,... | collective-permute-start | bytes 1572872 | tf_op jit(solution)/shard_map/ppermute | solution.py:174
  99.0 0.0 collective-permute-done.16
  99.0 0.1 add_convert_fusion.2
  99.1 0.4 collective-permute-start.17
  99.6 11.1 %shard_map.114 = (f32[128,2048]{1,0:T(8,128)S(1)}, f32[128,2048]{1,0:T(8,128)S(1)}, f32[128,2048]{1,0:T(8,128)S(1)}) custom-call(s32[1]{0:T(128)} %bitcast.me_ref, bf16[128,2176]{1,0:T(8,128)(2,1)S(1)} %copy-done.8, bf16[128,2176]{1,0:T(8,128)(2,1)S(1)} %copy-done.12, bf16[128,2176]{1,0:T(8,128)(2,1)S(1)} %copy-done.10, bf16[704,2048]{1,0:T(8,128)(2,1)S(1)} %bitcast.22, ...), custom_call_target="tpu_custom_call" | custom-call | flops 6643777536 | bytes 17301504 | tf_op jit(solution)/shard_map/pallas_call | solution.py:102
  110.7 1.0 copy-done.6
  111.6 0.0 collective-permute-done.13
  111.6 0.1 add_convert_fusion.4
  111.8 1.7 %collective-permute-start.14 = (bf16[128,2048]{1,0:T(8,128)(2,1)S(1)}, bf16[128,2048]{1,0:T(8,128)(2,1)S(1)}, u32[]{:S(2)}, u32[]{:S(2)}) collective-permute-start(bf16[128,2048]{1,0:T(8,128)(2,1)S(1)} %add_convert_fusion.4), channel_id=1, source_target_pairs={{0,2},{1,3},{2,6},{3,7},{4,0},{5,1},{6,10},{7,11},{8,4},{9,5},{10,... | collective-permute-start | bytes 1572872 | tf_op jit(solution)/shard_map/ppermute | solution.py:174
  113.5 0.0 collective-permute-done.17
  113.5 0.9 add_convert_fusion.1
  114.4 0.4 collective-permute-start.18
  114.7 0.0 all-to-all-done
  114.7 2.4 %shard_map.118 = bf16[128,2048]{1,0:T(8,128)(2,1)} custom-call(bf16[128,2048]{1,0:T(8,128)(2,1)} %bitcast.13.arrived_ref, s32[16,16]{1,0:T(8,128)} %counts_ref.1, s32[1,16]{1,0:T(1,128)} %bitcast.35, s32[1]{0:T(128)} %bitcast.me_ref, bf16[128,2048]{1,0:T(8,128)(2,1)} %text_ref.1), custom_call_target="tpu_custom_call" | custom-call | tf_op jit(solution)/shard_map/pallas_call | solution.py:142
  117.1 6.9 %collective-permute-done.14 = bf16[128,2048]{1,0:T(8,128)(2,1)S(1)} collective-permute-done((bf16[128,2048]{1,0:T(8,128)(2,1)S(1)}, bf16[128,2048]{1,0:T(8,128)(2,1)S(1)}, u32[]{:S(2)}, u32[]{:S(2)}) %collective-permute-start.14) | collective-permute-done | bytes 524320 | tf_op jit(solution)/shard_map/ppermute | solution.py:174
  124.0 2.3 %collective-permute-done.18 = bf16[128,2048]{1,0:T(8,128)(2,1)S(1)} collective-permute-done((bf16[128,2048]{1,0:T(8,128)(2,1)}, bf16[128,2048]{1,0:T(8,128)(2,1)S(1)}, u32[]{:S(2)}, u32[]{:S(2)}) %collective-permute-start.18) | collective-permute-done | bytes 524320 | tf_op jit(solution)/shard_map/ppermute | solution.py:174
  126.3 1.0 add_convert_fusion
  (22 shorter events, 0.1 us)
Async XLA Ops:
  0.6 52.6 %copy-start = (bf16[1,16,8,2048]{3,2,1,0:T(8,128)(2,1)S(1)}, bf16[1,16,8,2048]{3,2,1,0:T(8,128)(2,1)}, u32[]{:S(2)}) copy-start(bf16[1,16,8,2048]{3,2,1,0:T(8,128)(2,1)} %param.16) | copy-start | bytes 1572868
  0.6 59.6 %copy-start.1 = (bf16[1,2048,704]{1,2,0:T(8,128)(2,1)S(1)}, bf16[1,2048,704]{1,2,0:T(8,128)(2,1)}, u32[]{:S(2)}) copy-start(bf16[1,2048,704]{1,2,0:T(8,128)(2,1)} %param.13) | copy-start | bytes 8650756
  0.7 59.5 %collective-permute-start.2 = (bf16[704,2048]{1,0:T(8,128)(2,1)}, bf16[704,2048]{1,0:T(8,128)(2,1)}, u32[]{:S(2)}, u32[]{:S(2)}) collective-permute-start(bf16[704,2048]{1,0:T(8,128)(2,1)} %bitcast.18), channel_id=1, source_target_pairs={{0,1},{1,0},{2,3},{3,2},{4,5},{5,4},{6,7},{7,6},{8,9},{9,8},{10,11... | collective-permute-start | bytes 8650760 | tf_op jit(solution)/shard_map/ppermute | solution.py:174
  1.2 59.0 %collective-permute-start.3 = (bf16[704,2048]{1,0:T(8,128)(2,1)}, bf16[704,2048]{1,0:T(8,128)(2,1)}, u32[]{:S(2)}, u32[]{:S(2)}) collective-permute-start(bf16[704,2048]{1,0:T(8,128)(2,1)} %bitcast.23), channel_id=1, source_target_pairs={{0,1},{1,0},{2,3},{3,2},{4,5},{5,4},{6,7},{7,6},{8,9},{9,8},{10,11... | collective-permute-start | bytes 8650760 | tf_op jit(solution)/shard_map/ppermute | solution.py:174
  1.3 59.0 %collective-permute-start.4 = (bf16[704,2048]{1,0:T(8,128)(2,1)}, bf16[704,2048]{1,0:T(8,128)(2,1)}, u32[]{:S(2)}, u32[]{:S(2)}) collective-permute-start(bf16[704,2048]{1,0:T(8,128)(2,1)} %bitcast.28), channel_id=1, source_target_pairs={{0,1},{1,0},{2,3},{3,2},{4,5},{5,4},{6,7},{7,6},{8,9},{9,8},{10,11... | collective-permute-start | bytes 8650760 | tf_op jit(solution)/shard_map/ppermute | solution.py:174
  4.0 16.0 %collective-permute-start.1 = (bf16[128,2176]{1,0:T(8,128)(2,1)}, bf16[128,2176]{1,0:T(8,128)(2,1)S(1)}, u32[]{:S(2)}, u32[]{:S(2)}) collective-permute-start(bf16[128,2176]{1,0:T(8,128)(2,1)} %shard_map.113.refs_0_), channel_id=1, source_target_pairs={{0,4},{1,5},{2,0},{3,1},{4,8},{5,9},{6,2},{7,3},{8,12},{9,13},{10,... | collective-permute-start | bytes 1671176 | tf_op jit(solution)/shard_map/ppermute | solution.py:174
  7.0 15.7 %collective-permute-start = (bf16[128,2176]{1,0:T(8,128)(2,1)}, bf16[128,2176]{1,0:T(8,128)(2,1)S(1)}, u32[]{:S(2)}, u32[]{:S(2)}) collective-permute-start(bf16[128,2176]{1,0:T(8,128)(2,1)} %shard_map.113.refs_0_), channel_id=1, source_target_pairs={{0,2},{1,3},{2,6},{3,7},{4,0},{5,1},{6,10},{7,11},{8,4},{9,5},{10,... | collective-permute-start | bytes 1671176 | tf_op jit(solution)/shard_map/ppermute | solution.py:174
  20.1 14.2 %collective-permute-start.6 = (bf16[128,2176]{1,0:T(8,128)(2,1)S(1)}, bf16[128,2176]{1,0:T(8,128)(2,1)}, u32[]{:S(2)}, u32[]{:S(2)}) collective-permute-start(bf16[128,2176]{1,0:T(8,128)(2,1)S(1)} %collective-permute-done.1.refs_2_), channel_id=1, source_target_pairs={{0,4},{1,5},{2,0},{3,1},{4,8},{5,9},{6,2},{7,3},{8,12},{9,13},{10,... | collective-permute-start | bytes 1671176 | tf_op jit(solution)/shard_map/ppermute | solution.py:174
  21.9 0.8 copy-start.9
  22.7 13.6 %collective-permute-start.5 = (bf16[128,2176]{1,0:T(8,128)(2,1)S(1)}, bf16[128,2176]{1,0:T(8,128)(2,1)}, u32[]{:S(2)}, u32[]{:S(2)}) collective-permute-start(bf16[128,2176]{1,0:T(8,128)(2,1)S(1)} %collective-permute-done.refs_1_), channel_id=1, source_target_pairs={{0,2},{1,3},{2,6},{3,7},{4,0},{5,1},{6,10},{7,11},{8,4},{9,5},{10,... | collective-permute-start | bytes 1671176 | tf_op jit(solution)/shard_map/ppermute | solution.py:174
  22.9 0.8 copy-start.11
  34.3 13.5 %collective-permute-start.8 = (bf16[128,2176]{1,0:T(8,128)(2,1)}, bf16[128,2176]{1,0:T(8,128)(2,1)}, u32[]{:S(2)}, u32[]{:S(2)}) collective-permute-start(bf16[128,2176]{1,0:T(8,128)(2,1)} %collective-permute-done.6.refs_1_), channel_id=1, source_target_pairs={{0,4},{1,5},{2,0},{3,1},{4,8},{5,9},{6,2},{7,3},{8,12},{9,13},{10,... | collective-permute-start | bytes 1671176 | tf_op jit(solution)/shard_map/ppermute | solution.py:174
  36.3 14.4 %collective-permute-start.7 = (bf16[128,2176]{1,0:T(8,128)(2,1)}, bf16[128,2176]{1,0:T(8,128)(2,1)}, u32[]{:S(2)}, u32[]{:S(2)}) collective-permute-start(bf16[128,2176]{1,0:T(8,128)(2,1)} %collective-permute-done.5.refs_0_), channel_id=1, source_target_pairs={{0,2},{1,3},{2,6},{3,7},{4,0},{5,1},{6,10},{7,11},{8,4},{9,5},{10,... | collective-permute-start | bytes 1671176 | tf_op jit(solution)/shard_map/ppermute | solution.py:174
  49.5 10.7 %collective-permute-start.9 = (bf16[64,2176]{1,0:T(8,128)(2,1)}, bf16[64,2176]{1,0:T(8,128)(2,1)}, u32[]{:S(2)}, u32[]{:S(2)}) collective-permute-start(bf16[64,2176]{1,0:T(8,128)(2,1)} %slice.18), channel_id=1, source_target_pairs={{0,4},{1,5},{2,0},{3,1},{4,8},{5,9},{6,2},{7,3},{8,12},{9,13},{10,... | collective-permute-start | bytes 835592 | tf_op jit(solution)/shard_map/ppermute | solution.py:174
  52.3 7.9 %collective-permute-start.10 = (bf16[64,2176]{1,0:T(8,128)(2,1)}, bf16[64,2176]{1,0:T(8,128)(2,1)}, u32[]{:S(2)}, u32[]{:S(2)}) collective-permute-start(bf16[64,2176]{1,0:T(8,128)(2,1)} %slice.19), channel_id=1, source_target_pairs={{0,2},{1,3},{2,6},{3,7},{4,0},{5,1},{6,10},{7,11},{8,4},{9,5},{10,... | collective-permute-start | bytes 835592 | tf_op jit(solution)/shard_map/ppermute | solution.py:174
  54.6 60.1 %all-to-all-start = ((bf16[16,8,2048]{2,1,0:T(8,128)(2,1)}), bf16[16,8,2048]{2,1,0:T(8,128)(2,1)}, u32[]{:S(2)}, u32[]{:S(2)}) async-start(bf16[16,8,2048]{2,1,0:T(8,128)(2,1)} %gather_fusion), calls=%async_computation | async-start | bytes 1048576 | tf_op jit(solution)/shard_map/all_to_all | solution.py:224
  60.2 1.8 %copy-start.2 = (bf16[1,2048,704]{1,2,0:T(8,128)(2,1)S(1)}, bf16[1,2048,704]{1,2,0:T(8,128)(2,1)}, u32[]{:S(2)}) copy-start(bf16[1,2048,704]{1,2,0:T(8,128)(2,1)} %param.14) | copy-start | bytes 8650756
  62.1 1.8 %copy-start.4 = (bf16[1,704,2048]{2,1,0:T(8,128)(2,1)S(1)}, bf16[1,704,2048]{2,1,0:T(8,128)(2,1)}, u32[]{:S(2)}) copy-start(bf16[1,704,2048]{2,1,0:T(8,128)(2,1)} %param.15) | copy-start | bytes 8650756
  72.3 11.1 %collective-permute-start.11 = (bf16[64,2048]{1,0:T(8,128)(2,1)S(1)}, bf16[64,2048]{1,0:T(8,128)(2,1)S(1)}, u32[]{:S(2)}, u32[]{:S(2)}) collective-permute-start(bf16[64,2048]{1,0:T(8,128)(2,1)S(1)} %get-tuple-element.18), channel_id=1, source_target_pairs={{0,2},{1,3},{2,6},{3,7},{4,0},{5,1},{6,10},{7,11},{8,4},{9,5},{10,... | collective-permute-start | bytes 786440 | tf_op jit(solution)/shard_map/ppermute | solution.py:174
  74.2 11.2 %collective-permute-start.15 = (bf16[64,2048]{1,0:T(8,128)(2,1)S(1)}, bf16[64,2048]{1,0:T(8,128)(2,1)S(1)}, u32[]{:S(2)}, u32[]{:S(2)}) collective-permute-start(bf16[64,2048]{1,0:T(8,128)(2,1)S(1)} %get-tuple-element.19), channel_id=1, source_target_pairs={{0,4},{1,5},{2,0},{3,1},{4,8},{5,9},{6,2},{7,3},{8,12},{9,13},{10,... | collective-permute-start | bytes 786440 | tf_op jit(solution)/shard_map/ppermute | solution.py:174
  83.5 13.7 %collective-permute-start.12 = (bf16[128,2048]{1,0:T(8,128)(2,1)S(1)}, bf16[128,2048]{1,0:T(8,128)(2,1)S(1)}, u32[]{:S(2)}, u32[]{:S(2)}) collective-permute-start(bf16[128,2048]{1,0:T(8,128)(2,1)S(1)} %add_convert_fusion.6), channel_id=1, source_target_pairs={{0,2},{1,3},{2,6},{3,7},{4,0},{5,1},{6,10},{7,11},{8,4},{9,5},{10,... | collective-permute-start | bytes 1572872 | tf_op jit(solution)/shard_map/ppermute | solution.py:174
  85.5 13.5 %collective-permute-start.16 = (bf16[128,2048]{1,0:T(8,128)(2,1)S(1)}, bf16[128,2048]{1,0:T(8,128)(2,1)S(1)}, u32[]{:S(2)}, u32[]{:S(2)}) collective-permute-start(bf16[128,2048]{1,0:T(8,128)(2,1)S(1)} %add_convert_fusion.3), channel_id=1, source_target_pairs={{0,4},{1,5},{2,0},{3,1},{4,8},{5,9},{6,2},{7,3},{8,12},{9,13},{10,... | collective-permute-start | bytes 1572872 | tf_op jit(solution)/shard_map/ppermute | solution.py:174
  85.9 13.7 %copy-start.5 = (bf16[1,704,2048]{2,1,0:T(8,128)(2,1)S(1)}, bf16[1,704,2048]{2,1,0:T(8,128)(2,1)}, u32[]{:S(2)}) copy-start(bf16[1,704,2048]{2,1,0:T(8,128)(2,1)} %param.15) | copy-start | bytes 8650756
  85.9 13.7 %copy-start.12 = (bf16[128,2176]{1,0:T(8,128)(2,1)S(1)}, bf16[128,2176]{1,0:T(8,128)(2,1)}, u32[]{:S(2)}) copy-start(bf16[128,2176]{1,0:T(8,128)(2,1)} %copy-done.11) | copy-start | bytes 1671172
  95.0 4.5 %copy-start.3 = (bf16[1,2048,704]{1,2,0:T(8,128)(2,1)S(1)}, bf16[1,2048,704]{1,2,0:T(8,128)(2,1)}, u32[]{:S(2)}) copy-start(bf16[1,2048,704]{1,2,0:T(8,128)(2,1)} %param.14) | copy-start | bytes 8650756
  95.0 4.5 %copy-start.8 = (bf16[128,2176]{1,0:T(8,128)(2,1)S(1)}, bf16[128,2176]{1,0:T(8,128)(2,1)}, u32[]{:S(2)}) copy-start(bf16[128,2176]{1,0:T(8,128)(2,1)} %shard_map.113.refs_0_) | copy-start | bytes 1671172
  95.0 4.5 %copy-start.10 = (bf16[128,2176]{1,0:T(8,128)(2,1)S(1)}, bf16[128,2176]{1,0:T(8,128)(2,1)}, u32[]{:S(2)}) copy-start(bf16[128,2176]{1,0:T(8,128)(2,1)} %copy-done.9) | copy-start | bytes 1671172
  97.3 14.4 %collective-permute-start.13 = (bf16[128,2048]{1,0:T(8,128)(2,1)S(1)}, bf16[128,2048]{1,0:T(8,128)(2,1)S(1)}, u32[]{:S(2)}, u32[]{:S(2)}) collective-permute-start(bf16[128,2048]{1,0:T(8,128)(2,1)S(1)} %add_convert_fusion.5), channel_id=1, source_target_pairs={{0,2},{1,3},{2,6},{3,7},{4,0},{5,1},{6,10},{7,11},{8,4},{9,5},{10,... | collective-permute-start | bytes 1572872 | tf_op jit(solution)/shard_map/ppermute | solution.py:174
  99.1 14.3 %collective-permute-start.17 = (bf16[128,2048]{1,0:T(8,128)(2,1)S(1)}, bf16[128,2048]{1,0:T(8,128)(2,1)S(1)}, u32[]{:S(2)}, u32[]{:S(2)}) collective-permute-start(bf16[128,2048]{1,0:T(8,128)(2,1)S(1)} %add_convert_fusion.2), channel_id=1, source_target_pairs={{0,4},{1,5},{2,0},{3,1},{4,8},{5,9},{6,2},{7,3},{8,12},{9,13},{10,... | collective-permute-start | bytes 1572872 | tf_op jit(solution)/shard_map/ppermute | solution.py:174
  110.7 1.0 copy-start.6
  111.6 14.6 %copy-start.7 = (f32[128,2048]{1,0:T(8,128)S(1)}, f32[128,2048]{1,0:T(8,128)}, u32[]{:S(2)}) copy-start(f32[128,2048]{1,0:T(8,128)} %copy-done.6) | copy-start | bytes 3145732
  111.8 12.2 %collective-permute-start.14 = (bf16[128,2048]{1,0:T(8,128)(2,1)S(1)}, bf16[128,2048]{1,0:T(8,128)(2,1)S(1)}, u32[]{:S(2)}, u32[]{:S(2)}) collective-permute-start(bf16[128,2048]{1,0:T(8,128)(2,1)S(1)} %add_convert_fusion.4), channel_id=1, source_target_pairs={{0,2},{1,3},{2,6},{3,7},{4,0},{5,1},{6,10},{7,11},{8,4},{9,5},{10,... | collective-permute-start | bytes 1572872 | tf_op jit(solution)/shard_map/ppermute | solution.py:174
  114.4 11.9 %collective-permute-start.18 = (bf16[128,2048]{1,0:T(8,128)(2,1)}, bf16[128,2048]{1,0:T(8,128)(2,1)S(1)}, u32[]{:S(2)}, u32[]{:S(2)}) collective-permute-start(bf16[128,2048]{1,0:T(8,128)(2,1)} %add_convert_fusion.1), channel_id=1, source_target_pairs={{0,4},{1,5},{2,0},{3,1},{4,8},{5,9},{6,2},{7,3},{8,12},{9,13},{10,... | collective-permute-start | bytes 1572872 | tf_op jit(solution)/shard_map/ppermute | solution.py:174

commit v3 on v2

v3 whole, which is shorter than its diff:
```python
import functools
import math

import jax
import jax.numpy as jnp
from jax import lax
from jax.experimental import pallas as pl
from jax.experimental.pallas import tpu as pltpu
from jax.sharding import PartitionSpec as P

route_scale = 2.446
NT = (((1,), (1,)), ((), ()))


def ring_of(chips):
    if chips <= 8:
        return list(range(0, chips, 2)) + list(range(chips - 1, 0, -2))
    return list(range(chips))


def route_kernel(slots, picks_ref, router_hbm, tokens_hbm, out_ref, router_ref, tokens_ref, sems):
    rows = tokens_ref.shape[0]
    experts = router_ref.shape[0]
    take_tokens = pltpu.make_async_copy(tokens_hbm, tokens_ref, sems.at[0])
    take_router = pltpu.make_async_copy(router_hbm, router_ref, sems.at[1])
    take_tokens.start()
    take_router.start()
    take_tokens.wait()
    take_router.wait()
    logits = lax.dot_general(router_ref[...], tokens_ref[...], NT, preferred_element_type=jnp.float32)
    score = 1.0 / (1.0 + jnp.exp(-logits))
    expert = lax.broadcasted_iota(jnp.int32, (experts, rows), 0)
    picked = expert == picks_ref[0:1, :]
    for k in range(1, picks_ref.shape[0]):
        picked = jnp.logical_or(picked, expert == picks_ref[k : k + 1, :])
    total = jnp.sum(jnp.where(picked, score, 0.0), axis=0, keepdims=True)
    route = jnp.where(picked, route_scale * score / total, 0.0)
    parts = []
    for _ in range(3):
        part = route.astype(jnp.bfloat16)
        parts.append(part.astype(jnp.float32))
        route = route - parts[-1]
    parts = jnp.concatenate(parts, axis=0).astype(jnp.bfloat16)
    shape = (out_ref.shape[0], 3 * experts)
    target = lax.broadcasted_iota(jnp.int32, shape, 0)
    source = lax.broadcasted_iota(jnp.int32, shape, 1)
    for block in range(out_ref.shape[1] // rows):
        line = block * slots + target % slots
        wanted = (line % 3) * experts + ((target // slots) ^ (line // 3))
        pick = jnp.logical_and(line < 6, source == wanted).astype(jnp.bfloat16)
        out_ref[:, block * rows : (block + 1) * rows] = jnp.dot(
            pick, parts, preferred_element_type=jnp.float32
        ).astype(jnp.bfloat16)


def in_hbm(x):
    return pltpu.with_memory_space_constraint(x, pltpu.HBM)


def route_of(tokens, expert_picks, router, slots):
    rows, width = tokens.shape
    experts = router.shape[1]
    vmem = pl.BlockSpec(memory_space=pltpu.VMEM)
    hbm = pl.BlockSpec(memory_space=pl.ANY)
    return pl.pallas_call(
        functools.partial(route_kernel, slots),
        out_shape=jax.ShapeDtypeStruct((experts * slots, -(-6 // slots) * rows), jnp.bfloat16),
        in_specs=[vmem, hbm, hbm],
        out_specs=vmem,
        scratch_shapes=[
            pltpu.VMEM((experts, width), router.dtype),
            pltpu.VMEM((rows, width), tokens.dtype),
            pltpu.SemaphoreType.DMA((2,)),
        ],
        compiler_params=pltpu.CompilerParams(vmem_limit_bytes=8 * 2**20),
    )(expert_picks.T, in_hbm(router.T), in_hbm(tokens))


def lines_kernel(width, slots, arrived_hbm, out_ref, taken_ref, sem):
    copy = pltpu.make_async_copy(arrived_hbm.at[:, pl.ds(width, taken_ref.shape[1])], taken_ref, sem)
    copy.start()
    copy.wait()
    lines, rows = out_ref.shape
    shape = (lines, taken_ref.shape[0])
    target = lax.broadcasted_iota(jnp.int32, shape, 0)
    source = lax.broadcasted_iota(jnp.int32, shape, 1)
    total = jnp.zeros(out_ref.shape, jnp.float32)
    for block in range(taken_ref.shape[1] // rows):
        line = target % 8 - block * slots
        wanted = jnp.where(jnp.logical_and(line >= 0, line < slots), target // 8 * slots + line, -1)
        pick = (source == wanted).astype(jnp.bfloat16)
        total = total + jnp.dot(
            pick, taken_ref[:, block * rows : (block + 1) * rows], preferred_element_type=jnp.float32
        )
    out_ref[...] = total


def lines_of(arrived, width, slots, rows):
    devices = arrived.shape[0] // slots
    return pl.pallas_call(
        functools.partial(lines_kernel, width, slots),
        out_shape=jax.ShapeDtypeStruct((8 * devices, rows), jnp.float32),
        in_specs=[pl.BlockSpec(memory_space=pl.ANY)],
        out_specs=pl.BlockSpec(memory_space=pltpu.VMEM),
        scratch_shapes=[
            pltpu.VMEM((arrived.shape[0], arrived.shape[1] - width), arrived.dtype),
            pltpu.SemaphoreType.DMA,
        ],
        compiler_params=pltpu.CompilerParams(vmem_limit_bytes=4 * 2**20),
    )(arrived)


def spans_kernel(span_of_ref, rows_hbm, out_ref, sems):
    copies = [
        pltpu.make_async_copy(rows_hbm.at[span_of_ref[d]], out_ref.at[d], sems.at[d]) for d in range(rows_hbm.shape[0])
    ]
    for copy in copies:
        copy.start()
    for copy in copies:
        copy.wait()


def by_owner(image_rows, span_of):
    return pl.pallas_call(
        spans_kernel,
        out_shape=jax.ShapeDtypeStruct(image_rows.shape, image_rows.dtype),
        in_specs=[pl.BlockSpec(memory_space=pltpu.SMEM), pl.BlockSpec(memory_space=pl.ANY)],
        out_specs=pl.BlockSpec(memory_space=pltpu.VMEM),
        scratch_shapes=[pltpu.SemaphoreType.DMA((image_rows.shape[0],))],
        compiler_params=pltpu.CompilerParams(vmem_limit_bytes=4 * 2**20),
    )(span_of, in_hbm(image_rows))


def ffn_kernel(count, results, sizes, offsets, chips, holds, me_ref, order_ref, *refs):
    shards = refs[:count]
    table = refs[count]
    weights = refs[count + 1 : count + 7]
    outs = refs[count + 7 : count + 7 + results]
    kept = refs[count + 7 + results : count + 7 + results + holds]
    x, hidden, total = refs[count + 7 + results + holds :][:3]
    copies = []
    if holds:
        sems = refs[-1]
        for i in range(6):
            copies.append(pltpu.make_async_copy(weights[i], kept[i], sems.at[i]))
            copies[i].start()
        weights = kept
    rows = sum(sizes)
    width = x.shape[1]
    block = rows // results
    at = 0
    for ref, m in zip(shards, sizes):
        x[pl.ds(at, m), :] = ref[...]
        at += m
    me = me_ref[0]
    tokens = rows // len(offsets)
    square = (tokens, tokens)
    eye = lax.broadcasted_iota(jnp.int32, square, 0) == lax.broadcasted_iota(jnp.int32, square, 1)
    routes = [[], []]
    for offset in offsets:
        source = 2 * order_ref[(me // 2) * chips + offset] + me % 2
        lines = table[pl.ds(pl.multiple_of(source * 8, 8), 8), :]
        for e in range(2):
            line = lines[3 * e : 3 * e + 1] + lines[3 * e + 1 : 3 * e + 2] + lines[3 * e + 2 : 3 * e + 3]
            routes[e].append(jnp.sum(jnp.where(eye, line, 0.0), axis=1, keepdims=True))
    for e in range(2):
        wg, wu, wd = weights[3 * e : 3 * e + 3]
        route = jnp.concatenate(routes[e], axis=0)
        if holds:
            copies[3 * e].wait()
            copies[3 * e + 1].wait()
        gate = lax.dot_general(x[...], wg[...], NT, preferred_element_type=jnp.float32)
        upward = lax.dot_general(x[...], wu[...], NT, preferred_element_type=jnp.float32)
        hidden[...] = (gate / (1.0 + jnp.exp(-gate)) * upward).astype(jnp.bfloat16)
        if holds:
            copies[3 * e + 2].wait()
        for a in range(0, width, 512):
            lanes = pl.ds(a, 512)
            row = jnp.dot(hidden[...], wd[:, lanes], preferred_element_type=jnp.float32)
            row = row.astype(jnp.bfloat16).astype(jnp.float32) * route
            if e == 0:
                total[:, lanes] = row
            else:
                row = total[:, lanes] + row
                for k, out in enumerate(outs):
                    out[:, lanes] = row[k * block : (k + 1) * block].astype(out.dtype)


def ffn(shards, offsets, results, me, order, table, weights, holds):
    sizes = [s.shape[0] for s in shards]
    rows = sum(sizes)
    ff, width = weights[0].shape
    block = rows // results
    vmem = pl.BlockSpec(memory_space=pltpu.VMEM)
    smem = pl.BlockSpec(memory_space=pltpu.SMEM)
    hbm = pl.BlockSpec(memory_space=pl.ANY)
    chips = math.isqrt(order.shape[0])
    kept = 6 if holds else 0
    if holds:
        weights = [in_hbm(w) for w in weights]
    return pl.pallas_call(
        functools.partial(ffn_kernel, len(shards), results, sizes, offsets, chips, kept),
        out_shape=[jax.ShapeDtypeStruct((block, width), jnp.float32)] * results
        + [pltpu.VMEM(w.shape, w.dtype) for w in weights[:kept]],
        in_specs=[smem] * 2 + [vmem] * (len(shards) + 1) + [hbm if holds else vmem] * 6,
        out_specs=[vmem] * (results + kept),
        scratch_shapes=[
            pltpu.VMEM((rows, width), jnp.bfloat16),
            pltpu.VMEM((rows, ff), jnp.bfloat16),
            pltpu.VMEM((rows, width), jnp.float32),
        ]
        + [pltpu.SemaphoreType.DMA((6,))] * holds,
        compiler_params=pltpu.CompilerParams(vmem_limit_bytes=10 * 2**20),
        cost_estimate=pl.CostEstimate(
            flops=12 * rows * ff * width, bytes_accessed=12 * ff * width, transcendentals=2 * rows * ff
        ),
    )(me[None], order, *shards, table, *weights)


def place_kernel(slots, arrived_ref, counts_ref, owner_ref, me_ref, text_ref, out_ref):
    rows = text_ref.shape[0]
    devices = counts_ref.shape[0]
    held = arrived_ref.shape[0]
    mine = (owner_ref[...] == me_ref[0]).astype(jnp.int32)
    live = jnp.sum(counts_ref[...] * mine, axis=1, keepdims=True)
    total = jnp.sum(live)
    lane = lax.broadcasted_iota(jnp.int32, (devices, held), 1)
    holder = lane // slots
    which = lax.broadcasted_iota(jnp.int32, (devices, held), 0)
    own = jnp.sum(jnp.where(which == holder, live, 0), axis=0, keepdims=True)
    start = jnp.sum(jnp.where(which < holder, live, 0), axis=0, keepdims=True)
    offset = lane[:1] - holder[:1] * slots
    place = jnp.where(offset < own, start + offset, -1)
    row = lax.broadcasted_iota(jnp.int32, (rows, held), 0)
    pick = (row == place).astype(jnp.bfloat16)
    image = jnp.dot(pick, arrived_ref[:, : text_ref.shape[1]], preferred_element_type=jnp.float32).astype(jnp.bfloat16)
    position = lax.broadcasted_iota(jnp.int32, (rows, 1), 0)
    out_ref[...] = jnp.where(position < total, image, text_ref[...])


def place_images(arrived, counts, owner, me, text_block, slots):
    vmem = pl.BlockSpec(memory_space=pltpu.VMEM)
    return pl.pallas_call(
        functools.partial(place_kernel, slots),
        out_shape=jax.ShapeDtypeStruct(text_block.shape, text_block.dtype),
        in_specs=[vmem, vmem, vmem, pl.BlockSpec(memory_space=pltpu.SMEM), vmem],
        out_specs=vmem,
        compiler_params=pltpu.CompilerParams(vmem_limit_bytes=8 * 2**20),
    )(arrived, counts, owner[None, :], me[None], text_block)


def cut_kernel(below_ref, above_ref, first_ref, second_ref, sems):
    half = first_ref.shape[0]
    copies = [
        pltpu.make_async_copy(below_ref.at[pl.ds(0, half)], first_ref, sems.at[0]),
        pltpu.make_async_copy(above_ref.at[pl.ds(half, half)], second_ref, sems.at[1]),
    ]
    for copy in copies:
        copy.start()
    for copy in copies:
        copy.wait()


def cut(below, above):
    rows, width = below.shape
    vmem = pl.BlockSpec(memory_space=pltpu.VMEM)
    return pl.pallas_call(
        cut_kernel,
        out_shape=[jax.ShapeDtypeStruct((rows // 2, width), below.dtype)] * 2,
        in_specs=[pl.BlockSpec(memory_space=pl.ANY)] * 2,
        out_specs=[vmem] * 2,
        scratch_shapes=[pltpu.SemaphoreType.DMA((2,))],
        compiler_params=pltpu.CompilerParams(vmem_limit_bytes=2 * 2**20),
    )(below, above)


def merge_kernel(above_ref, below_ref, up_first, up_second, down_first, down_second, up_ref, down_ref):
    half = up_first.shape[0]
    for out, total, first, second in (
        (up_ref, above_ref, up_first, up_second),
        (down_ref, below_ref, down_first, down_second),
    ):
        for i, came in enumerate((first, second)):
            part = pl.ds(i * half, half)
            out[part, :] = (total[part, :] + came[...].astype(jnp.float32)).astype(out.dtype)


def merge(above, below, *came):
    vmem = pl.BlockSpec(memory_space=pltpu.VMEM)
    return pl.pallas_call(
        merge_kernel,
        out_shape=[jax.ShapeDtypeStruct(above.shape, jnp.bfloat16)] * 2,
        in_specs=[vmem] * 6,
        out_specs=[vmem] * 2,
        compiler_params=pltpu.CompilerParams(vmem_limit_bytes=8 * 2**20),
    )(above, below, *came)


def tie(*arrays):
    return lax.optimization_barrier(arrays)


def local(
    tokens,
    expert_picks,
    router,
    gate_weight,
    up_weight,
    down_weight,
    image_rows,
    image_counts,
    span_owner,
    text_rows,
):
    devices = lax.axis_size("expert")
    me = lax.axis_index("expert")
    width = tokens.shape[1]
    experts = gate_weight.shape[0] * devices
    slots = image_rows.shape[2]
    chips = devices // 2
    far = chips // 2
    ring = ring_of(chips)
    pos = {c: i for i, c in enumerate(ring)}

    def send(x, pairs):
        return lax.ppermute(x, "expert", pairs)

    up = [(2 * c + k, 2 * ring[(pos[c] + 1) % chips] + k) for c in range(chips) for k in range(2)]
    down = [(target, source) for source, target in up]
    sibling = [(d, d ^ 1) for d in range(devices)]

    own = [gate_weight[0].T, up_weight[0].T, down_weight[0]]
    others = [send(w, sibling) for w in own]

    order = jnp.array([ring[(pos[c] + offset) % chips] for c in range(chips) for offset in range(chips)], jnp.int32)

    def run(shards, offsets, results=None, holds=False):
        return ffn(shards, offsets, results or len(shards), me, order, table, weights, holds)

    def run_both(s):
        return run([below[s], above[s]], [chips - s, s])

    number = jnp.arange(devices, dtype=jnp.int32)
    span_of = jnp.sum(jnp.where(span_owner[:, None] == number[None, :], number[:, None], 0), axis=0)
    span_of, expert_picks, swapped = tie(span_of, expert_picks, others[0])
    lines = route_of(tokens, expert_picks, router, slots)
    image_send = jnp.concatenate([by_owner(image_rows[0], span_of), lines.reshape(devices, slots, -1)], axis=2)
    arrived = lax.all_to_all(image_send, "expert", split_axis=0, concat_axis=0, tiled=True)
    arrived = arrived.reshape(devices * slots, -1)

    below, above = [tokens], [tokens]
    from_below, from_above = {}, {}
    for s in range(1, far):
        below.append(send(below[-1], up))
        above.append(send(above[-1], down))
        below[s], above[s] = tie(below[s], above[s])
    table = lines_of(arrived, width, slots, tokens.shape[0])
    weights = own + others

    first, second = cut(below[-1], above[-1])
    first, second = send(first, up), send(second, down)
    *done, w0, w1, w2, w3, w4, w5 = run([below[-1], above[-1]], [chips - far + 1, far - 1], 4, True)
    weights = [w0, w1, w2, w3, w4, w5]
    first, second, *done = tie(first, second, *done)

    def low(x):
        return x.astype(jnp.bfloat16)

    def add(mine, came):
        return low(mine + came.astype(jnp.float32))

    below_first, below_second, above_first, above_second = done
    short_up, short_down = send(low(above_first), up), send(low(below_second), down)
    far_first, far_second, result_first, result_second = run([first, second, tokens], [far, 0], 4)
    short_up, short_down, far_first, far_second = tie(short_up, short_down, far_first, far_second)
    long_up, long_down = send(low(far_second), up), send(low(far_first), down)
    from_below[far - 2], from_above[far - 2] = run_both(far - 2)
    long_up, long_down, from_below[far - 2], from_above[far - 2] = tie(
        long_up, long_down, from_below[far - 2], from_above[far - 2]
    )
    long_up, long_down = send(add(above_second, long_up), up), send(add(below_first, long_down), down)
    from_below[1], from_above[1] = run_both(1)
    long_up, long_down, from_below[1], from_above[1] = tie(long_up, long_down, from_below[1], from_above[1])
    going_up, going_down = merge(
        from_above[far - 2], from_below[far - 2], short_up, long_up, long_down, short_down
    )
    for s in range(2, far - 2):
        if s not in from_below:
            from_below[s], from_above[s] = run_both(s)
    for s in range(far - 2, 0, -1):
        going_up, going_down = tie(send(going_up, up), send(going_down, down))
        if s > 1:
            going_up, going_down = add(from_above[s - 1], going_up), add(from_below[s - 1], going_down)
    result = jnp.concatenate([result_first, result_second], axis=0)
    moe_out = low(result + going_up.astype(jnp.float32) + going_down.astype(jnp.float32))

    next_span = place_images(
        arrived, image_counts, span_owner, me, text_rows, slots
    )
    return (moe_out, next_span)


def solution(mesh):
    return jax.shard_map(
        local,
        mesh=mesh,
        in_specs=(
            P(("groups", "expert"), None),
            P(("groups", "expert"), None),
            P(),
            P("expert", None, None),
            P("expert", None, None),
            P("expert", None, None),
            P(("groups", "expert"), None, None, None),
            P("groups", None),
            P("groups"),
            P(("groups", "expert"), None),
        ),
        out_specs=(P(("groups", "expert"), None), P(("groups", "expert"), None)),
        check_vma=False,
    )
```

time: 128 us -> 120 us (0.938)
  local copies, waits for them, and re-layouts: 11 us -> 0.72 us
  Pallas kernels: 42.3 us -> 33.6 us
  waiting for transfers between devices: 45.6 us -> 53.4 us
  starting transfers between devices: 24.2 us -> 28 us
    ppermute x19 -> x21, waiting for transfers between devices: 45.6 us -> 53.4 us  [send(): return lax.ppermute(x, 'expert', pairs)]
    pallas_call x5 -> x9, Pallas kernels: 39.9 us -> 32.4 us  [the longest x4 27.6 us: ffn(): pl.pallas_call(functools.partial(ffn_kernel, len(shards), results, sizes,...]
    unnamed x26 -> x14, local copies, waits for them, and re-layouts: 6.27 us -> 0.72 us
    ppermute x19 -> x21, starting transfers between devices: 18.7 us -> 23.1 us  [send(): return lax.ppermute(x, 'expert', pairs)]
    slice x3 -> x0, local copies, waits for them, and re-layouts: 3.4 us -> none  [the longest x2 3.36 us: local(): last = [send(from_below[-1][:half], up), send(from_above[-1][half:], down)]]
    gather x1 -> x0, local copies, waits for them, and re-layouts: 1.37 us -> none  [local(): image_rows[0][span_of]]
  transfers between devices with their start and end apart: 20 -> 22, of which waited for: 7 -> 10; matrix products, arithmetic and copies ran while one was open for 5% -> 2% of each run, Pallas kernels for 33% -> 28%
where the time goes in v3:
time: 120 us
  waiting for transfers between devices  53.4 us (44%)
  Pallas kernels  33.6 us (28%)
  starting transfers between devices  28 us (23%)
  other arithmetic  3.11 us (3%)
    ppermute x21, waiting for transfers between devices, send(): return lax.ppermute(x, 'expert', pairs)  53.4 us
    pallas_call x4, Pallas kernels, ffn(): pl.pallas_call(functools.partial(ffn_kernel, len(shards), results, sizes,...  27.6 us
    ppermute x21, starting transfers between devices, send(): return lax.ppermute(x, 'expert', pairs)  23.1 us
    all_to_all x1, starting transfers between devices, local(): lax.all_to_all(image_send, 'expert', split_axis=0, concat_axis=0, tiled=T...  4.93 us
  transfers between devices with their start and end apart: 22, of which 10 were waited for; matrix products, arithmetic and copies ran while one was open for 2% of the time, Pallas kernels for 28%

profile of v3, /device:TPU:0, one launch (start us, length us, event | category | flops | bytes accessed | tf_op | source)
XLA Modules:
  0.0 119.7 jit_solution(15667330198816689661)
XLA Ops:
  0.6 0.0 copy-start.2
  0.6 0.5 collective-permute-start.8
  1.2 0.1 collective-permute-start.10
  1.2 0.4 collective-permute-start.9
  1.7 2.7 %collective-permute-start = (bf16[128,2048]{1,0:T(8,128)(2,1)}, bf16[128,2048]{1,0:T(8,128)(2,1)S(1)}, u32[]{:S(2)}, u32[]{:S(2)}) collective-permute-start(bf16[128,2048]{1,0:T(8,128)(2,1)} %refs_2_.1), channel_id=1, source_target_pairs={{0,4},{1,5},{2,0},{3,1},{4,8},{5,9},{6,2},{7,3},{8,12},{9,13},{10,... | collective-permute-start | bytes 1572872 | tf_op jit(solution)/shard_map/ppermute | solution.py:326
  4.3 0.0 collective-permute-start.1
  4.3 0.7 select_reduce_fusion.span_of_ref
  5.1 11.9 %collective-permute-done.refs_0_ = bf16[128,2048]{1,0:T(8,128)(2,1)S(1)} collective-permute-done((bf16[128,2048]{1,0:T(8,128)(2,1)}, bf16[128,2048]{1,0:T(8,128)(2,1)S(1)}, u32[]{:S(2)}, u32[]{:S(2)}) %collective-permute-start) | collective-permute-done | bytes 524320 | tf_op jit(solution)/shard_map/ppermute | solution.py:326
  17.0 1.5 %collective-permute-done.1.refs_1_ = bf16[128,2048]{1,0:T(8,128)(2,1)S(1)} collective-permute-done((bf16[128,2048]{1,0:T(8,128)(2,1)}, bf16[128,2048]{1,0:T(8,128)(2,1)S(1)}, u32[]{:S(2)}, u32[]{:S(2)}) %collective-permute-start.1) | collective-permute-done | bytes 524320 | tf_op jit(solution)/shard_map/ppermute | solution.py:326
  18.5 1.6 %collective-permute-start.2 = (bf16[128,2048]{1,0:T(8,128)(2,1)S(1)}, bf16[128,2048]{1,0:T(8,128)(2,1)S(1)}, u32[]{:S(2)}, u32[]{:S(2)}) collective-permute-start(bf16[128,2048]{1,0:T(8,128)(2,1)S(1)} %collective-permute-done.refs_0_), channel_id=1, source_target_pairs={{0,4},{1,5},{2,0},{3,1},{4,8},{5,9},{6,2},{7,3},{8,12},{9,13},{10,... | collective-permute-start | bytes 1572872 | tf_op jit(solution)/shard_map/ppermute | solution.py:326
  20.1 0.4 collective-permute-start.3
  20.6 0.0 collective-permute-done.8.refs_6_
  20.6 2.1 %shard_map.123 = bf16[16,8,2048]{2,1,0:T(8,128)(2,1)S(1)} custom-call(s32[16]{0:T(128)S(1)} %select_reduce_fusion.span_of_ref, bf16[16,8,2048]{2,1,0:T(8,128)(2,1)} %bitcast.25), custom_call_target="tpu_custom_call" | custom-call | tf_op jit(solution)/shard_map/pallas_call | solution.py:124
  22.7 0.0 copy-start.4
  22.7 0.7 copy-done.4
  23.4 1.5 %shard_map.124 = bf16[128,128]{1,0:T(8,128)(2,1)S(1)} custom-call(s32[6,128]{1,0:T(8,128)S(1)} %bitcast.17, bf16[16,2048]{1,0:T(8,128)(2,1)} %bitcast.26, bf16[128,2048]{1,0:T(8,128)(2,1)} %refs_2_.1), custom_call_target="tpu_custom_call" | custom-call | tf_op jit(solution)/shard_map/pallas_call | solution.py:65
  24.9 0.9 pad_maximum_fusion
  25.8 4.9 %all-to-all-start = ((bf16[16,8,2176]{2,1,0:T(8,128)(2,1)}), bf16[16,8,2176]{2,1,0:T(8,128)(2,1)S(1)}, u32[]{:S(2)}, u32[]{:S(2)}) async-start(bf16[16,8,2176]{2,1,0:T(8,128)(2,1)} %pad_maximum_fusion), calls=%async_computation | async-start | bytes 1114112 | tf_op jit(solution)/shard_map/all_to_all | solution.py:348
  30.7 1.0 collective-permute-done.2.refs_0_
  31.7 1.4 %collective-permute-done.3.refs_1_ = bf16[128,2048]{1,0:T(8,128)(2,1)} collective-permute-done((bf16[128,2048]{1,0:T(8,128)(2,1)S(1)}, bf16[128,2048]{1,0:T(8,128)(2,1)}, u32[]{:S(2)}, u32[]{:S(2)}) %collective-permute-start.3) | collective-permute-done | bytes 524320 | tf_op jit(solution)/shard_map/ppermute | solution.py:326
  33.1 1.6 %collective-permute-start.4 = (bf16[128,2048]{1,0:T(8,128)(2,1)S(1)}, bf16[128,2048]{1,0:T(8,128)(2,1)S(1)}, u32[]{:S(2)}, u32[]{:S(2)}) collective-permute-start(bf16[128,2048]{1,0:T(8,128)(2,1)S(1)} %collective-permute-done.2.refs_0_), channel_id=1, source_target_pairs={{0,4},{1,5},{2,0},{3,1},{4,8},{5,9},{6,2},{7,3},{8,12},{9,13},{10,... | collective-permute-start | bytes 1572872 | tf_op jit(solution)/shard_map/ppermute | solution.py:326
  34.7 0.4 collective-permute-start.5
  35.1 16.9 %collective-permute-done.4.below_ref.refs_0_ = bf16[128,2048]{1,0:T(8,128)(2,1)S(1)} collective-permute-done((bf16[128,2048]{1,0:T(8,128)(2,1)S(1)}, bf16[128,2048]{1,0:T(8,128)(2,1)S(1)}, u32[]{:S(2)}, u32[]{:S(2)}) %collective-permute-start.4) | collective-permute-done | bytes 524320 | tf_op jit(solution)/shard_map/ppermute | solution.py:326
  52.0 2.0 %collective-permute-done.5.above_ref.refs_1_ = bf16[128,2048]{1,0:T(8,128)(2,1)S(1)} collective-permute-done((bf16[128,2048]{1,0:T(8,128)(2,1)}, bf16[128,2048]{1,0:T(8,128)(2,1)S(1)}, u32[]{:S(2)}, u32[]{:S(2)}) %collective-permute-start.5) | collective-permute-done | bytes 524320 | tf_op jit(solution)/shard_map/ppermute | solution.py:326
  54.0 0.8 shard_map.122
  54.9 4.5 %collective-permute-start.6 = (bf16[64,2048]{1,0:T(8,128)(2,1)}, bf16[64,2048]{1,0:T(8,128)(2,1)S(1)}, u32[]{:S(2)}, u32[]{:S(2)}) collective-permute-start(bf16[64,2048]{1,0:T(8,128)(2,1)} %get-tuple-element.60), channel_id=1, source_target_pairs={{0,4},{1,5},{2,0},{3,1},{4,8},{5,9},{6,2},{7,3},{8,12},{9,13},{10,... | collective-permute-start | bytes 786440 | tf_op jit(solution)/shard_map/ppermute | solution.py:326
  59.4 0.0 collective-permute-start.7
  59.4 0.0 all-to-all-done
  59.4 0.2 shard_map.125.refs_2_.refs_3_
  59.6 0.0 collective-permute-done.10.refs_8_
  59.6 0.0 collective-permute-done.9.refs_7_
  59.6 0.0 copy-start
  59.6 9.1 %shard_map.126 = (f32[64,2048]{1,0:T(8,128)S(1)}, f32[64,2048]{1,0:T(8,128)S(1)}, f32[64,2048]{1,0:T(8,128)S(1)}, f32[64,2048]{1,0:T(8,128)S(1)}, bf16[704,2048]...) custom-call(s32[1]{0:T(128)} %bitcast.me_ref, ...), custom_call_target="tpu_custom_call" | custom-call | flops 4429185024 | bytes 17301504 | tf_op jit(solution)/shard_map/pallas_call | solution.py:201
  68.7 0.0 collective-permute-done.6.refs_0_
  68.7 0.0 collective-permute-done.7.refs_1_
  68.8 2.1 %collective-permute-start.11 = (bf16[64,2048]{1,0:T(8,128)(2,1)S(1)}, bf16[64,2048]{1,0:T(8,128)(2,1)S(1)}, u32[]{:S(2)}, u32[]{:S(2)}) collective-permute-start(bf16[64,2048]{1,0:T(8,128)(2,1)S(1)} %convert_element_type.45), channel_id=1, source_target_pairs={{0,4},{1,5},{2,0},{3,1},{4,8},{5,9},{6,2},{7,3},{8,12},{9,13},{10,... | collective-permute-start | bytes 786440 | tf_op jit(solution)/shard_map/ppermute | solution.py:326
  70.9 0.1 collective-permute-start.12
  71.0 6.3 %shard_map.127 = (f32[64,2048]{1,0:T(8,128)S(1)}, f32[64,2048]{1,0:T(8,128)S(1)}, f32[64,2048]{1,0:T(8,128)S(1)}, f32[64,2048]{1,0:T(8,128)S(1)}) custom-call(s32[1]{0:T(128)} %bitcast.me_ref, s32[64]{0:T(128)S(1)} %copy-done.2, bf16[64,2048]{1,0:T(8,128)(2,1)S(1)} %collective-permute-done.6.refs_0_, bf16[64,2048]{1,0:T(8,128)(2,1)} %collective-permute-done.7.refs_1_, ...), custom_call_target="tpu_custom_call" | custom-call | flops 4429185024 | bytes 17301504 | tf_op jit(solution)/shard_map/pallas_call | solution.py:201
  77.3 0.0 collective-permute-done.11.up_first
  77.3 0.7 collective-permute-done.12.down_second
  78.0 1.4 %collective-permute-start.13 = (bf16[64,2048]{1,0:T(8,128)(2,1)S(1)}, bf16[64,2048]{1,0:T(8,128)(2,1)S(1)}, u32[]{:S(2)}, u32[]{:S(2)}) collective-permute-start(bf16[64,2048]{1,0:T(8,128)(2,1)S(1)} %convert_element_type.47), channel_id=1, source_target_pairs={{0,4},{1,5},{2,0},{3,1},{4,8},{5,9},{6,2},{7,3},{8,12},{9,13},{10,... | collective-permute-start | bytes 786440 | tf_op jit(solution)/shard_map/ppermute | solution.py:326
  79.4 0.9 collective-permute-start.14
  80.3 6.4 %shard_map.128 = (f32[128,2048]{1,0:T(8,128)S(1)}, f32[128,2048]{1,0:T(8,128)S(1)}) custom-call(s32[1]{0:T(128)} %bitcast.me_ref, s32[64]{0:T(128)S(1)} %copy-done.2, bf16[128,2048]{1,0:T(8,128)(2,1)S(1)} %collective-permute-done.2.refs_0_, bf16[128,2048]{1,0:T(8,128)(2,1)} %collective-permute-done.3.refs_1_, f32[128,128]{1,0:T(8,128)S(1)} %shard_map.125.refs_2_.refs_3_, ...), custom_call_target="tpu_custom_call" | custom-call | flops 4429185024 | bytes 17301504 | tf_op jit(solution)/shard_map/pallas_call | solution.py:201
  86.8 0.9 collective-permute-start.16
  87.7 0.1 add_convert_fusion.3
  87.7 1.2 %collective-permute-start.15 = (bf16[64,2048]{1,0:T(8,128)(2,1)S(1)}, bf16[64,2048]{1,0:T(8,128)(2,1)S(1)}, u32[]{:S(2)}, u32[]{:S(2)}) collective-permute-start(bf16[64,2048]{1,0:T(8,128)(2,1)S(1)} %add_convert_fusion.3), channel_id=1, source_target_pairs={{0,4},{1,5},{2,0},{3,1},{4,8},{5,9},{6,2},{7,3},{8,12},{9,13},{10,... | collective-permute-start | bytes 786440 | tf_op jit(solution)/shard_map/ppermute | solution.py:326
  89.0 5.9 %shard_map.129 = (f32[128,2048]{1,0:T(8,128)S(1)}, f32[128,2048]{1,0:T(8,128)S(1)}) custom-call(s32[1]{0:T(128)} %bitcast.me_ref, s32[64]{0:T(128)S(1)} %copy-done.2, bf16[128,2048]{1,0:T(8,128)(2,1)S(1)} %collective-permute-done.refs_0_, bf16[128,2048]{1,0:T(8,128)(2,1)S(1)} %collective-permute-done.1.refs_1_, f32[128,128]{1,0:T(8,128)S(1)} %shard_map.125.refs_2_.refs_3_, ...), custom_call_target="tpu_custom_call" | custom-call | flops 4429185024 | bytes 17301504 | tf_op jit(solution)/shard_map/pallas_call | solution.py:201
  94.9 0.0 collective-permute-done.15.up_second
  94.9 0.2 shard_map.130
  95.1 0.0 copy-start.1
  95.1 0.0 copy-start.3
  95.1 0.0 copy-start.5
  95.1 1.4 %collective-permute-start.17 = (bf16[128,2048]{1,0:T(8,128)(2,1)S(1)}, bf16[128,2048]{1,0:T(8,128)(2,1)S(1)}, u32[]{:S(2)}, u32[]{:S(2)}) collective-permute-start(bf16[128,2048]{1,0:T(8,128)(2,1)S(1)} %get-tuple-element.99), channel_id=1, source_target_pairs={{0,4},{1,5},{2,0},{3,1},{4,8},{5,9},{6,2},{7,3},{8,12},{9,13},{10,... | collective-permute-start | bytes 1572872 | tf_op jit(solution)/shard_map/ppermute | solution.py:326
  96.5 0.7 collective-permute-start.18
  97.2 8.8 %collective-permute-done.17 = bf16[128,2048]{1,0:T(8,128)(2,1)S(1)} collective-permute-done((bf16[128,2048]{1,0:T(8,128)(2,1)S(1)}, bf16[128,2048]{1,0:T(8,128)(2,1)S(1)}, u32[]{:S(2)}, u32[]{:S(2)}) %collective-permute-start.17) | collective-permute-done | bytes 524320 | tf_op jit(solution)/shard_map/ppermute | solution.py:326
  106.0 2.4 %collective-permute-done.18 = bf16[128,2048]{1,0:T(8,128)(2,1)S(1)} collective-permute-done((bf16[128,2048]{1,0:T(8,128)(2,1)S(1)}, bf16[128,2048]{1,0:T(8,128)(2,1)S(1)}, u32[]{:S(2)}, u32[]{:S(2)}) %collective-permute-start.18) | collective-permute-done | bytes 524320 | tf_op jit(solution)/shard_map/ppermute | solution.py:326
  108.4 0.1 add_convert_fusion
  108.5 0.4 collective-permute-start.20
  108.9 0.1 add_convert_fusion.1
  109.1 1.8 %collective-permute-start.19 = (bf16[128,2048]{1,0:T(8,128)(2,1)S(1)}, bf16[128,2048]{1,0:T(8,128)(2,1)S(1)}, u32[]{:S(2)}, u32[]{:S(2)}) collective-permute-start(bf16[128,2048]{1,0:T(8,128)(2,1)S(1)} %add_convert_fusion.1), channel_id=1, source_target_pairs={{0,4},{1,5},{2,0},{3,1},{4,8},{5,9},{6,2},{7,3},{8,12},{9,13},{10,... | collective-permute-start | bytes 1572872 | tf_op jit(solution)/shard_map/ppermute | solution.py:326
  110.8 1.2 shard_map.131
  112.0 6.7 %collective-permute-done.20 = bf16[128,2048]{1,0:T(8,128)(2,1)S(1)} collective-permute-done((bf16[128,2048]{1,0:T(8,128)(2,1)S(1)}, bf16[128,2048]{1,0:T(8,128)(2,1)S(1)}, u32[]{:S(2)}, u32[]{:S(2)}) %collective-permute-start.20) | collective-permute-done | bytes 524320 | tf_op jit(solution)/shard_map/ppermute | solution.py:326
  118.7 0.0 collective-permute-done.19
  118.7 1.0 fusion.1
  (15 shorter events, 0.2 us)
Async XLA Ops:
  0.6 59.0 %copy-start.2 = (s32[64]{0:T(128)S(1)}, s32[64]{0:T(128)}, u32[]{:S(2)}) copy-start(s32[64]{0:T(128)} %constant.8.clone.order_ref) | copy-start | bytes 772
  0.6 19.9 %collective-permute-start.8 = (bf16[704,2048]{1,0:T(8,128)(2,1)}, bf16[704,2048]{1,0:T(8,128)(2,1)S(1)}, u32[]{:S(2)}, u32[]{:S(2)}) collective-permute-start(bf16[704,2048]{1,0:T(8,128)(2,1)} %bitcast.19), channel_id=1, source_target_pairs={{0,1},{1,0},{2,3},{3,2},{4,5},{5,4},{6,7},{7,6},{8,9},{9,8},{10,11... | collective-permute-start | bytes 8650760 | tf_op jit(solution)/shard_map/ppermute | solution.py:326
  1.2 58.4 %collective-permute-start.10 = (bf16[704,2048]{1,0:T(8,128)(2,1)}, bf16[704,2048]{1,0:T(8,128)(2,1)}, u32[]{:S(2)}, u32[]{:S(2)}) collective-permute-start(bf16[704,2048]{1,0:T(8,128)(2,1)} %bitcast.23), channel_id=1, source_target_pairs={{0,1},{1,0},{2,3},{3,2},{4,5},{5,4},{6,7},{7,6},{8,9},{9,8},{10,11... | collective-permute-start | bytes 8650760 | tf_op jit(solution)/shard_map/ppermute | solution.py:326
  1.2 58.4 %collective-permute-start.9 = (bf16[704,2048]{1,0:T(8,128)(2,1)}, bf16[704,2048]{1,0:T(8,128)(2,1)}, u32[]{:S(2)}, u32[]{:S(2)}) collective-permute-start(bf16[704,2048]{1,0:T(8,128)(2,1)} %bitcast.21), channel_id=1, source_target_pairs={{0,1},{1,0},{2,3},{3,2},{4,5},{5,4},{6,7},{7,6},{8,9},{9,8},{10,11... | collective-permute-start | bytes 8650760 | tf_op jit(solution)/shard_map/ppermute | solution.py:326
  1.7 15.3 %collective-permute-start = (bf16[128,2048]{1,0:T(8,128)(2,1)}, bf16[128,2048]{1,0:T(8,128)(2,1)S(1)}, u32[]{:S(2)}, u32[]{:S(2)}) collective-permute-start(bf16[128,2048]{1,0:T(8,128)(2,1)} %refs_2_.1), channel_id=1, source_target_pairs={{0,4},{1,5},{2,0},{3,1},{4,8},{5,9},{6,2},{7,3},{8,12},{9,13},{10,... | collective-permute-start | bytes 1572872 | tf_op jit(solution)/shard_map/ppermute | solution.py:326
  4.3 14.2 %collective-permute-start.1 = (bf16[128,2048]{1,0:T(8,128)(2,1)}, bf16[128,2048]{1,0:T(8,128)(2,1)S(1)}, u32[]{:S(2)}, u32[]{:S(2)}) collective-permute-start(bf16[128,2048]{1,0:T(8,128)(2,1)} %refs_2_.1), channel_id=1, source_target_pairs={{4,0},{5,1},{0,2},{1,3},{8,4},{9,5},{2,6},{3,7},{12,8},{13,9},{6,1... | collective-permute-start | bytes 1572872 | tf_op jit(solution)/shard_map/ppermute | solution.py:326
  18.5 13.2 %collective-permute-start.2 = (bf16[128,2048]{1,0:T(8,128)(2,1)S(1)}, bf16[128,2048]{1,0:T(8,128)(2,1)S(1)}, u32[]{:S(2)}, u32[]{:S(2)}) collective-permute-start(bf16[128,2048]{1,0:T(8,128)(2,1)S(1)} %collective-permute-done.refs_0_), channel_id=1, source_target_pairs={{0,4},{1,5},{2,0},{3,1},{4,8},{5,9},{6,2},{7,3},{8,12},{9,13},{10,... | collective-permute-start | bytes 1572872 | tf_op jit(solution)/shard_map/ppermute | solution.py:326
  20.1 13.0 %collective-permute-start.3 = (bf16[128,2048]{1,0:T(8,128)(2,1)S(1)}, bf16[128,2048]{1,0:T(8,128)(2,1)}, u32[]{:S(2)}, u32[]{:S(2)}) collective-permute-start(bf16[128,2048]{1,0:T(8,128)(2,1)S(1)} %collective-permute-done.1.refs_1_), channel_id=1, source_target_pairs={{4,0},{5,1},{0,2},{1,3},{8,4},{9,5},{2,6},{3,7},{12,8},{13,9},{6,1... | collective-permute-start | bytes 1572872 | tf_op jit(solution)/shard_map/ppermute | solution.py:326
  20.6 4.3 %copy-start.6 = (bf16[704,2048]{1,0:T(8,128)(2,1)}, bf16[704,2048]{1,0:T(8,128)(2,1)S(1)}, u32[]{:S(2)}) copy-start(bf16[704,2048]{1,0:T(8,128)(2,1)S(1)} %collective-permute-done.8.refs_6_) | copy-start | bytes 8650756
  22.7 0.7 copy-start.4
  25.8 33.7 %all-to-all-start = ((bf16[16,8,2176]{2,1,0:T(8,128)(2,1)}), bf16[16,8,2176]{2,1,0:T(8,128)(2,1)S(1)}, u32[]{:S(2)}, u32[]{:S(2)}) async-start(bf16[16,8,2176]{2,1,0:T(8,128)(2,1)} %pad_maximum_fusion), calls=%async_computation | async-start | bytes 1114112 | tf_op jit(solution)/shard_map/all_to_all | solution.py:348
  33.1 18.9 %collective-permute-start.4 = (bf16[128,2048]{1,0:T(8,128)(2,1)S(1)}, bf16[128,2048]{1,0:T(8,128)(2,1)S(1)}, u32[]{:S(2)}, u32[]{:S(2)}) collective-permute-start(bf16[128,2048]{1,0:T(8,128)(2,1)S(1)} %collective-permute-done.2.refs_0_), channel_id=1, source_target_pairs={{0,4},{1,5},{2,0},{3,1},{4,8},{5,9},{6,2},{7,3},{8,12},{9,13},{10,... | collective-permute-start | bytes 1572872 | tf_op jit(solution)/shard_map/ppermute | solution.py:326
  34.7 19.3 %collective-permute-start.5 = (bf16[128,2048]{1,0:T(8,128)(2,1)}, bf16[128,2048]{1,0:T(8,128)(2,1)S(1)}, u32[]{:S(2)}, u32[]{:S(2)}) collective-permute-start(bf16[128,2048]{1,0:T(8,128)(2,1)} %collective-permute-done.3.refs_1_), channel_id=1, source_target_pairs={{4,0},{5,1},{0,2},{1,3},{8,4},{9,5},{2,6},{3,7},{12,8},{13,9},{6,1... | collective-permute-start | bytes 1572872 | tf_op jit(solution)/shard_map/ppermute | solution.py:326
  54.9 13.9 %collective-permute-start.6 = (bf16[64,2048]{1,0:T(8,128)(2,1)}, bf16[64,2048]{1,0:T(8,128)(2,1)S(1)}, u32[]{:S(2)}, u32[]{:S(2)}) collective-permute-start(bf16[64,2048]{1,0:T(8,128)(2,1)} %get-tuple-element.60), channel_id=1, source_target_pairs={{0,4},{1,5},{2,0},{3,1},{4,8},{5,9},{6,2},{7,3},{8,12},{9,13},{10,... | collective-permute-start | bytes 786440 | tf_op jit(solution)/shard_map/ppermute | solution.py:326
  59.4 9.3 %collective-permute-start.7 = (bf16[64,2048]{1,0:T(8,128)(2,1)}, bf16[64,2048]{1,0:T(8,128)(2,1)}, u32[]{:S(2)}, u32[]{:S(2)}) collective-permute-start(bf16[64,2048]{1,0:T(8,128)(2,1)} %get-tuple-element.61), channel_id=1, source_target_pairs={{4,0},{5,1},{0,2},{1,3},{8,4},{9,5},{2,6},{3,7},{12,8},{13,9},{6,1... | collective-permute-start | bytes 786440 | tf_op jit(solution)/shard_map/ppermute | solution.py:326
  59.6 11.3 %copy-start = (bf16[128,2048]{1,0:T(8,128)(2,1)S(1)}, bf16[128,2048]{1,0:T(8,128)(2,1)}, u32[]{:S(2)}) copy-start(bf16[128,2048]{1,0:T(8,128)(2,1)} %refs_2_.1) | copy-start | bytes 1572868
  68.8 8.5 %collective-permute-start.11 = (bf16[64,2048]{1,0:T(8,128)(2,1)S(1)}, bf16[64,2048]{1,0:T(8,128)(2,1)S(1)}, u32[]{:S(2)}, u32[]{:S(2)}) collective-permute-start(bf16[64,2048]{1,0:T(8,128)(2,1)S(1)} %convert_element_type.45), channel_id=1, source_target_pairs={{0,4},{1,5},{2,0},{3,1},{4,8},{5,9},{6,2},{7,3},{8,12},{9,13},{10,... | collective-permute-start | bytes 786440 | tf_op jit(solution)/shard_map/ppermute | solution.py:326
  70.9 7.1 %collective-permute-start.12 = (bf16[64,2048]{1,0:T(8,128)(2,1)S(1)}, bf16[64,2048]{1,0:T(8,128)(2,1)S(1)}, u32[]{:S(2)}, u32[]{:S(2)}) collective-permute-start(bf16[64,2048]{1,0:T(8,128)(2,1)S(1)} %convert_element_type.46), channel_id=1, source_target_pairs={{4,0},{5,1},{0,2},{1,3},{8,4},{9,5},{2,6},{3,7},{12,8},{13,9},{6,1... | collective-permute-start | bytes 786440 | tf_op jit(solution)/shard_map/ppermute | solution.py:326
  78.0 8.7 %collective-permute-start.13 = (bf16[64,2048]{1,0:T(8,128)(2,1)S(1)}, bf16[64,2048]{1,0:T(8,128)(2,1)S(1)}, u32[]{:S(2)}, u32[]{:S(2)}) collective-permute-start(bf16[64,2048]{1,0:T(8,128)(2,1)S(1)} %convert_element_type.47), channel_id=1, source_target_pairs={{0,4},{1,5},{2,0},{3,1},{4,8},{5,9},{6,2},{7,3},{8,12},{9,13},{10,... | collective-permute-start | bytes 786440 | tf_op jit(solution)/shard_map/ppermute | solution.py:326
  79.4 7.3 %collective-permute-start.14 = (bf16[64,2048]{1,0:T(8,128)(2,1)S(1)}, bf16[64,2048]{1,0:T(8,128)(2,1)S(1)}, u32[]{:S(2)}, u32[]{:S(2)}) collective-permute-start(bf16[64,2048]{1,0:T(8,128)(2,1)S(1)} %convert_element_type.48), channel_id=1, source_target_pairs={{4,0},{5,1},{0,2},{1,3},{8,4},{9,5},{2,6},{3,7},{12,8},{13,9},{6,1... | collective-permute-start | bytes 786440 | tf_op jit(solution)/shard_map/ppermute | solution.py:326
  86.8 8.1 %collective-permute-start.16 = (bf16[64,2048]{1,0:T(8,128)(2,1)S(1)}, bf16[64,2048]{1,0:T(8,128)(2,1)S(1)}, u32[]{:S(2)}, u32[]{:S(2)}) collective-permute-start(bf16[64,2048]{1,0:T(8,128)(2,1)S(1)} %add_convert_fusion.2), channel_id=1, source_target_pairs={{4,0},{5,1},{0,2},{1,3},{8,4},{9,5},{2,6},{3,7},{12,8},{13,9},{6,1... | collective-permute-start | bytes 786440 | tf_op jit(solution)/shard_map/ppermute | solution.py:326
  87.7 7.1 %collective-permute-start.15 = (bf16[64,2048]{1,0:T(8,128)(2,1)S(1)}, bf16[64,2048]{1,0:T(8,128)(2,1)S(1)}, u32[]{:S(2)}, u32[]{:S(2)}) collective-permute-start(bf16[64,2048]{1,0:T(8,128)(2,1)S(1)} %add_convert_fusion.3), channel_id=1, source_target_pairs={{0,4},{1,5},{2,0},{3,1},{4,8},{5,9},{6,2},{7,3},{8,12},{9,13},{10,... | collective-permute-start | bytes 786440 | tf_op jit(solution)/shard_map/ppermute | solution.py:326
  95.1 15.7 %copy-start.1 = (bf16[128,2048]{1,0:T(8,128)(2,1)S(1)}, bf16[128,2048]{1,0:T(8,128)(2,1)}, u32[]{:S(2)}) copy-start(bf16[128,2048]{1,0:T(8,128)(2,1)} %text_ref.1) | copy-start | bytes 1572868
  95.1 15.7 %copy-start.3 = (s32[16,16]{1,0:T(8,128)S(1)}, s32[16,16]{1,0:T(8,128)}, u32[]{:S(2)}) copy-start(s32[16,16]{1,0:T(8,128)} %counts_ref.1) | copy-start | bytes 3076
  95.1 15.7 %copy-start.5 = (s32[16]{0:T(128)S(1)}, s32[16]{0:T(128)}, u32[]{:S(2)}) copy-start(s32[16]{0:T(128)} %param.19) | copy-start | bytes 196
  95.1 10.9 %collective-permute-start.17 = (bf16[128,2048]{1,0:T(8,128)(2,1)S(1)}, bf16[128,2048]{1,0:T(8,128)(2,1)S(1)}, u32[]{:S(2)}, u32[]{:S(2)}) collective-permute-start(bf16[128,2048]{1,0:T(8,128)(2,1)S(1)} %get-tuple-element.99), channel_id=1, source_target_pairs={{0,4},{1,5},{2,0},{3,1},{4,8},{5,9},{6,2},{7,3},{8,12},{9,13},{10,... | collective-permute-start | bytes 1572872 | tf_op jit(solution)/shard_map/ppermute | solution.py:326
  96.5 11.9 %collective-permute-start.18 = (bf16[128,2048]{1,0:T(8,128)(2,1)S(1)}, bf16[128,2048]{1,0:T(8,128)(2,1)S(1)}, u32[]{:S(2)}, u32[]{:S(2)}) collective-permute-start(bf16[128,2048]{1,0:T(8,128)(2,1)S(1)} %get-tuple-element.100), channel_id=1, source_target_pairs={{4,0},{5,1},{0,2},{1,3},{8,4},{9,5},{2,6},{3,7},{12,8},{13,9},{6,1... | collective-permute-start | bytes 1572872 | tf_op jit(solution)/shard_map/ppermute | solution.py:326
  108.5 10.1 %collective-permute-start.20 = (bf16[128,2048]{1,0:T(8,128)(2,1)S(1)}, bf16[128,2048]{1,0:T(8,128)(2,1)S(1)}, u32[]{:S(2)}, u32[]{:S(2)}) collective-permute-start(bf16[128,2048]{1,0:T(8,128)(2,1)S(1)} %add_convert_fusion), channel_id=1, source_target_pairs={{4,0},{5,1},{0,2},{1,3},{8,4},{9,5},{2,6},{3,7},{12,8},{13,9},{6,1... | collective-permute-start | bytes 1572872 | tf_op jit(solution)/shard_map/ppermute | solution.py:326
  109.1 9.6 %collective-permute-start.19 = (bf16[128,2048]{1,0:T(8,128)(2,1)S(1)}, bf16[128,2048]{1,0:T(8,128)(2,1)S(1)}, u32[]{:S(2)}, u32[]{:S(2)}) collective-permute-start(bf16[128,2048]{1,0:T(8,128)(2,1)S(1)} %add_convert_fusion.1), channel_id=1, source_target_pairs={{0,4},{1,5},{2,0},{3,1},{4,8},{5,9},{6,2},{7,3},{8,12},{9,13},{10,... | collective-permute-start | bytes 1572872 | tf_op jit(solution)/shard_map/ppermute | solution.py:326

commit v4 on v3

--- a/solution.py
+++ b/solution.py
@@ -18,9 +18,9 @@
     return list(range(chips))
 
 
-def route_kernel(slots, picks_ref, router_hbm, tokens_hbm, out_ref, router_ref, tokens_ref, sems):
+def route_kernel(picks_ref, router_hbm, tokens_hbm, out_ref, router_ref, tokens_ref, sems):
+    experts = router_ref.shape[0]
     rows = tokens_ref.shape[0]
-    experts = router_ref.shape[0]
     take_tokens = pltpu.make_async_copy(tokens_hbm, tokens_ref, sems.at[0])
     take_router = pltpu.make_async_copy(router_hbm, router_ref, sems.at[1])
     take_tokens.start()
@@ -34,37 +34,30 @@
     for k in range(1, picks_ref.shape[0]):
         picked = jnp.logical_or(picked, expert == picks_ref[k : k + 1, :])
     total = jnp.sum(jnp.where(picked, score, 0.0), axis=0, keepdims=True)
-    route = jnp.where(picked, route_scale * score / total, 0.0)
-    parts = []
+    rest = jnp.where(picked, route_scale * score / total, 0.0)
+    target = lax.broadcasted_iota(jnp.int32, (out_ref.shape[0], experts), 0)
+    source = lax.broadcasted_iota(jnp.int32, (out_ref.shape[0], experts), 1)
+    pick = jnp.logical_and(target % 8 < 2, source == ((target // 8) ^ (target % 8))).astype(jnp.bfloat16)
+    lines = jnp.zeros(out_ref.shape, jnp.float32)
     for _ in range(3):
-        part = route.astype(jnp.bfloat16)
-        parts.append(part.astype(jnp.float32))
-        route = route - parts[-1]
-    parts = jnp.concatenate(parts, axis=0).astype(jnp.bfloat16)
-    shape = (out_ref.shape[0], 3 * experts)
-    target = lax.broadcasted_iota(jnp.int32, shape, 0)
-    source = lax.broadcasted_iota(jnp.int32, shape, 1)
-    for block in range(out_ref.shape[1] // rows):
-        line = block * slots + target % slots
-        wanted = (line % 3) * experts + ((target // slots) ^ (line // 3))
-        pick = jnp.logical_and(line < 6, source == wanted).astype(jnp.bfloat16)
-        out_ref[:, block * rows : (block + 1) * rows] = jnp.dot(
-            pick, parts, preferred_element_type=jnp.float32
-        ).astype(jnp.bfloat16)
+        part = rest.astype(jnp.bfloat16)
+        rest = rest - part.astype(jnp.float32)
+        lines = lines + jnp.dot(pick, part, preferred_element_type=jnp.float32)
+    out_ref[...] = lines
 
 
 def in_hbm(x):
     return pltpu.with_memory_space_constraint(x, pltpu.HBM)
 
 
-def route_of(tokens, expert_picks, router, slots):
+def route_of(tokens, expert_picks, router):
     rows, width = tokens.shape
     experts = router.shape[1]
     vmem = pl.BlockSpec(memory_space=pltpu.VMEM)
     hbm = pl.BlockSpec(memory_space=pl.ANY)
     return pl.pallas_call(
-        functools.partial(route_kernel, slots),
-        out_shape=jax.ShapeDtypeStruct((experts * slots, -(-6 // slots) * rows), jnp.bfloat16),
+        route_kernel,
+        out_shape=jax.ShapeDtypeStruct((8 * experts, rows), jnp.float32),
         in_specs=[vmem, hbm, hbm],
         out_specs=vmem,
         scratch_shapes=[
@@ -74,40 +67,6 @@
         ],
         compiler_params=pltpu.CompilerParams(vmem_limit_bytes=8 * 2**20),
     )(expert_picks.T, in_hbm(router.T), in_hbm(tokens))
-
-
-def lines_kernel(width, slots, arrived_hbm, out_ref, taken_ref, sem):
-    copy = pltpu.make_async_copy(arrived_hbm.at[:, pl.ds(width, taken_ref.shape[1])], taken_ref, sem)
-    copy.start()
-    copy.wait()
-    lines, rows = out_ref.shape
-    shape = (lines, taken_ref.shape[0])
-    target = lax.broadcasted_iota(jnp.int32, shape, 0)
-    source = lax.broadcasted_iota(jnp.int32, shape, 1)
-    total = jnp.zeros(out_ref.shape, jnp.float32)
-    for block in range(taken_ref.shape[1] // rows):
-        line = target % 8 - block * slots
-        wanted = jnp.where(jnp.logical_and(line >= 0, line < slots), target // 8 * slots + line, -1)
-        pick = (source == wanted).astype(jnp.bfloat16)
-        total = total + jnp.dot(
-            pick, taken_ref[:, block * rows : (block + 1) * rows], preferred_element_type=jnp.float32
-        )
-    out_ref[...] = total
-
-
-def lines_of(arrived, width, slots, rows):
-    devices = arrived.shape[0] // slots
-    return pl.pallas_call(
-        functools.partial(lines_kernel, width, slots),
-        out_shape=jax.ShapeDtypeStruct((8 * devices, rows), jnp.float32),
-        in_specs=[pl.BlockSpec(memory_space=pl.ANY)],
-        out_specs=pl.BlockSpec(memory_space=pltpu.VMEM),
-        scratch_shapes=[
-            pltpu.VMEM((arrived.shape[0], arrived.shape[1] - width), arrived.dtype),
-            pltpu.SemaphoreType.DMA,
-        ],
-        compiler_params=pltpu.CompilerParams(vmem_limit_bytes=4 * 2**20),
-    )(arrived)
 
 
 def spans_kernel(span_of_ref, rows_hbm, out_ref, sems):
@@ -161,15 +120,15 @@
         source = 2 * order_ref[(me // 2) * chips + offset] + me % 2
         lines = table[pl.ds(pl.multiple_of(source * 8, 8), 8), :]
         for e in range(2):
-            line = lines[3 * e : 3 * e + 1] + lines[3 * e + 1 : 3 * e + 2] + lines[3 * e + 2 : 3 * e + 3]
-            routes[e].append(jnp.sum(jnp.where(eye, line, 0.0), axis=1, keepdims=True))
+            routes[e].append(jnp.sum(jnp.where(eye, lines[e : e + 1], 0.0), axis=1, keepdims=True))
     for e in range(2):
         wg, wu, wd = weights[3 * e : 3 * e + 3]
         route = jnp.concatenate(routes[e], axis=0)
         if holds:
             copies[3 * e].wait()
+        gate = lax.dot_general(x[...], wg[...], NT, preferred_element_type=jnp.float32)
+        if holds:
             copies[3 * e + 1].wait()
-        gate = lax.dot_general(x[...], wg[...], NT, preferred_element_type=jnp.float32)
         upward = lax.dot_general(x[...], wu[...], NT, preferred_element_type=jnp.float32)
         hidden[...] = (gate / (1.0 + jnp.exp(-gate)) * upward).astype(jnp.bfloat16)
         if holds:
@@ -233,7 +192,7 @@
     place = jnp.where(offset < own, start + offset, -1)
     row = lax.broadcasted_iota(jnp.int32, (rows, held), 0)
     pick = (row == place).astype(jnp.bfloat16)
-    image = jnp.dot(pick, arrived_ref[:, : text_ref.shape[1]], preferred_element_type=jnp.float32).astype(jnp.bfloat16)
+    image = jnp.dot(pick, arrived_ref[...], preferred_element_type=jnp.float32).astype(jnp.bfloat16)
     position = lax.broadcasted_iota(jnp.int32, (rows, 1), 0)
     out_ref[...] = jnp.where(position < total, image, text_ref[...])
 
@@ -274,26 +233,26 @@
     )(below, above)
 
 
-def merge_kernel(above_ref, below_ref, up_first, up_second, down_first, down_second, up_ref, down_ref):
-    half = up_first.shape[0]
-    for out, total, first, second in (
-        (up_ref, above_ref, up_first, up_second),
-        (down_ref, below_ref, down_first, down_second),
-    ):
-        for i, came in enumerate((first, second)):
-            part = pl.ds(i * half, half)
+def merge_kernel(parts, *refs):
+    for i in range(2):
+        total, out = refs[i], refs[2 + 2 * parts + i]
+        at = 0
+        for came in refs[2 + i * parts : 2 + (i + 1) * parts]:
+            part = pl.ds(at, came.shape[0])
             out[part, :] = (total[part, :] + came[...].astype(jnp.float32)).astype(out.dtype)
-
-
-def merge(above, below, *came):
-    vmem = pl.BlockSpec(memory_space=pltpu.VMEM)
-    return pl.pallas_call(
-        merge_kernel,
+            at += came.shape[0]
+
+
+def merge(above, below, up_parts, down_parts):
+    parts = len(up_parts)
+    vmem = pl.BlockSpec(memory_space=pltpu.VMEM)
+    return pl.pallas_call(
+        functools.partial(merge_kernel, parts),
         out_shape=[jax.ShapeDtypeStruct(above.shape, jnp.bfloat16)] * 2,
-        in_specs=[vmem] * 6,
+        in_specs=[vmem] * (2 + 2 * parts),
         out_specs=[vmem] * 2,
         compiler_params=pltpu.CompilerParams(vmem_limit_bytes=8 * 2**20),
-    )(above, below, *came)
+    )(above, below, *up_parts, *down_parts)
 
 
 def tie(*arrays):
@@ -340,27 +299,35 @@
     def run_both(s):
         return run([below[s], above[s]], [chips - s, s])
 
+    expert_picks, _ = tie(expert_picks, others[0])
+    table = route_of(tokens, expert_picks, router)
+    table = lax.all_to_all(table.reshape(devices, 8, -1), "expert", split_axis=0, concat_axis=0, tiled=True)
+    table = table.reshape(8 * devices, -1)
+
     number = jnp.arange(devices, dtype=jnp.int32)
     span_of = jnp.sum(jnp.where(span_owner[:, None] == number[None, :], number[:, None], 0), axis=0)
-    span_of, expert_picks, swapped = tie(span_of, expert_picks, others[0])
-    lines = route_of(tokens, expert_picks, router, slots)
-    image_send = jnp.concatenate([by_owner(image_rows[0], span_of), lines.reshape(devices, slots, -1)], axis=2)
+    span_of, _ = tie(span_of, others[1])
+    image_send = by_owner(image_rows[0], span_of)
     arrived = lax.all_to_all(image_send, "expert", split_axis=0, concat_axis=0, tiled=True)
-    arrived = arrived.reshape(devices * slots, -1)
 
     below, above = [tokens], [tokens]
     from_below, from_above = {}, {}
     for s in range(1, far):
         below.append(send(below[-1], up))
         above.append(send(above[-1], down))
-        below[s], above[s] = tie(below[s], above[s])
-    table = lines_of(arrived, width, slots, tokens.shape[0])
-    weights = own + others
+        if s == far - 1:
+            weights = own + others
+            table, image_send = tie(table, image_send)
+            from_below[s - 1], from_above[s - 1], *weights = run([below[s - 1], above[s - 1]], [chips - s + 1, s - 1], 2, True)
+            below[s], above[s], from_below[s - 1], from_above[s - 1] = tie(
+                below[s], above[s], from_below[s - 1], from_above[s - 1]
+            )
+        else:
+            below[s], above[s], image_send = tie(below[s], above[s], image_send)
 
     first, second = cut(below[-1], above[-1])
     first, second = send(first, up), send(second, down)
-    *done, w0, w1, w2, w3, w4, w5 = run([below[-1], above[-1]], [chips - far + 1, far - 1], 4, True)
-    weights = [w0, w1, w2, w3, w4, w5]
+    done = run([below[-1], above[-1]], [chips - far + 1, far - 1], 4)
     first, second, *done = tie(first, second, *done)
 
     def low(x):
@@ -374,15 +341,13 @@
     far_first, far_second, result_first, result_second = run([first, second, tokens], [far, 0], 4)
     short_up, short_down, far_first, far_second = tie(short_up, short_down, far_first, far_second)
     long_up, long_down = send(low(far_second), up), send(low(far_first), down)
-    from_below[far - 2], from_above[far - 2] = run_both(far - 2)
-    long_up, long_down, from_below[far - 2], from_above[far - 2] = tie(
-        long_up, long_down, from_below[far - 2], from_above[far - 2]
+    from_below[1], from_above[1] = run_both(1)
+    long_up, long_down, short_up, short_down, from_below[1], from_above[1] = tie(
+        long_up, long_down, short_up, short_down, from_below[1], from_above[1]
     )
     long_up, long_down = send(add(above_second, long_up), up), send(add(below_first, long_down), down)
-    from_below[1], from_above[1] = run_both(1)
-    long_up, long_down, from_below[1], from_above[1] = tie(long_up, long_down, from_below[1], from_above[1])
     going_up, going_down = merge(
-        from_above[far - 2], from_below[far - 2], short_up, long_up, long_down, short_down
+        from_above[far - 2], from_below[far - 2], [short_up, long_up], [long_down, short_down]
     )
     for s in range(2, far - 2):
         if s not in from_below:
@@ -390,10 +355,11 @@
     for s in range(far - 2, 0, -1):
         going_up, going_down = tie(send(going_up, up), send(going_down, down))
         if s > 1:
-            going_up, going_down = add(from_above[s - 1], going_up), add(from_below[s - 1], going_down)
+            going_up, going_down = merge(from_above[s - 1], from_below[s - 1], [going_up], [going_down])
     result = jnp.concatenate([result_first, result_second], axis=0)
     moe_out = low(result + going_up.astype(jnp.float32) + going_down.astype(jnp.float32))
 
+    arrived = arrived.reshape(devices * slots, width)
     next_span = place_images(
         arrived, image_counts, span_owner, me, text_rows, slots
     )

time: 120 us -> 115 us (0.958)
  waiting for transfers between devices: 53.4 us -> 40.1 us
  Pallas kernels: 33.6 us -> 37.3 us
  local copies, waits for them, and re-layouts: 0.72 us -> 3.99 us
    ppermute x21, waiting for transfers between devices: 53.4 us -> 38.4 us  [send(): return lax.ppermute(x, 'expert', pairs)]
    all_to_all x0 -> x1, starting transfers between devices: none -> 4.94 us  [local(): lax.all_to_all(table.reshape(devices, 8, -1), 'expert', split_axis=0, con...]
    pallas_call x3, Pallas kernels: 1.83 us -> 5.9 us  [the longest x2 3.43 us: merge(): pl.pallas_call(functools.partial(merge_kernel, parts), out_shape=[jax.Sha...]
    unnamed x14 -> x28, local copies, waits for them, and re-layouts: 0.72 us -> 3.99 us
    ppermute x21, starting transfers between devices: 23.1 us -> 20.4 us  [send(): return lax.ppermute(x, 'expert', pairs)]
    all_to_all x0 -> x1, waiting for transfers between devices: none -> 1.66 us  [local(): lax.all_to_all(table.reshape(devices, 8, -1), 'expert', split_axis=0, con...]
  transfers between devices with their start and end apart: 22 -> 23, of which waited for: 10 -> 13; matrix products, arithmetic and copies ran while one was open for 2% -> 1% of each run, Pallas kernels for 28% -> 32%
where the time goes in v4:
time: 115 us
  waiting for transfers between devices  40.1 us (35%)
  Pallas kernels  37.3 us (32%)
  starting transfers between devices  29.2 us (25%)
  local copies, waits for them, and re-layouts  3.99 us (3%)
  other arithmetic  3.04 us (3%)
    ppermute x21, waiting for transfers between devices, send(): return lax.ppermute(x, 'expert', pairs)  38.4 us
    pallas_call x4, Pallas kernels, ffn(): pl.pallas_call(functools.partial(ffn_kernel, len(shards), results, sizes,...  27.3 us
    ppermute x21, starting transfers between devices, send(): return lax.ppermute(x, 'expert', pairs)  20.4 us
    all_to_all x1, starting transfers between devices, local(): lax.all_to_all(table.reshape(devices, 8, -1), 'expert', split_axis=0, con...  4.94 us
    unnamed x28, local copies, waits for them, and re-layouts  3.99 us
    all_to_all x1, starting transfers between devices, local(): lax.all_to_all(image_send, 'expert', split_axis=0, concat_axis=0, tiled=T...  3.87 us
    pallas_call x2, Pallas kernels, merge(): pl.pallas_call(functools.partial(merge_kernel, parts), out_shape=[jax.Sha...  3.43 us
    pallas_call x1, Pallas kernels, by_owner(): pl.pallas_call(spans_kernel, out_shape=jax.ShapeDtypeStruct(image_rows.sh...  2.94 us
  transfers between devices with their start and end apart: 23, of which 13 were waited for; matrix products, arithmetic and copies ran while one was open for 1% of the time, Pallas kernels for 32%

profile of v4, /device:TPU:0, one launch (start us, length us, event | category | flops | bytes accessed | tf_op | source)
XLA Modules:
  0.0 114.5 jit_solution(9237354006734686264)
XLA Ops:
  0.6 0.5 collective-permute-start.2
  1.1 0.1 collective-permute-start.7
  1.2 0.4 collective-permute-start.8
  1.7 2.7 %collective-permute-start = (bf16[128,2048]{1,0:T(8,128)(2,1)}, bf16[128,2048]{1,0:T(8,128)(2,1)S(1)}, u32[]{:S(2)}, u32[]{:S(2)}) collective-permute-start(bf16[128,2048]{1,0:T(8,128)(2,1)} %refs_2_.1), channel_id=1, source_target_pairs={{0,4},{1,5},{2,0},{3,1},{4,8},{5,9},{6,2},{7,3},{8,12},{9,13},{10,... | collective-permute-start | bytes 1572872 | tf_op jit(solution)/shard_map/ppermute | solution.py:285
  4.3 0.0 collective-permute-start.1
  4.3 0.7 select_reduce_fusion.span_of_ref
  5.1 1.2 %collective-permute-done.2.refs_7_ = bf16[704,2048]{1,0:T(8,128)(2,1)S(1)} collective-permute-done((bf16[704,2048]{1,0:T(8,128)(2,1)}, bf16[704,2048]{1,0:T(8,128)(2,1)S(1)}, u32[]{:S(2)}, u32[]{:S(2)}) %collective-permute-start.2) | collective-permute-done | bytes 2883616 | tf_op jit(solution)/shard_map/ppermute | solution.py:285
  6.3 2.9 %shard_map.122 = bf16[16,8,2048]{2,1,0:T(8,128)(2,1)} custom-call(s32[16]{0:T(128)S(1)} %select_reduce_fusion.span_of_ref, bf16[16,8,2048]{2,1,0:T(8,128)(2,1)} %bitcast.28), custom_call_target="tpu_custom_call" | custom-call | tf_op jit(solution)/shard_map/pallas_call | solution.py:83
  9.2 7.8 %collective-permute-done.refs_0_ = bf16[128,2048]{1,0:T(8,128)(2,1)S(1)} collective-permute-done((bf16[128,2048]{1,0:T(8,128)(2,1)}, bf16[128,2048]{1,0:T(8,128)(2,1)S(1)}, u32[]{:S(2)}, u32[]{:S(2)}) %collective-permute-start) | collective-permute-done | bytes 524320 | tf_op jit(solution)/shard_map/ppermute | solution.py:285
  17.0 1.5 %collective-permute-done.1.refs_1_ = bf16[128,2048]{1,0:T(8,128)(2,1)S(1)} collective-permute-done((bf16[128,2048]{1,0:T(8,128)(2,1)}, bf16[128,2048]{1,0:T(8,128)(2,1)S(1)}, u32[]{:S(2)}, u32[]{:S(2)}) %collective-permute-start.1) | collective-permute-done | bytes 524320 | tf_op jit(solution)/shard_map/ppermute | solution.py:285
  18.5 1.6 %collective-permute-start.3 = (bf16[128,2048]{1,0:T(8,128)(2,1)S(1)}, bf16[128,2048]{1,0:T(8,128)(2,1)S(1)}, u32[]{:S(2)}, u32[]{:S(2)}) collective-permute-start(bf16[128,2048]{1,0:T(8,128)(2,1)S(1)} %collective-permute-done.refs_0_), channel_id=1, source_target_pairs={{0,4},{1,5},{2,0},{3,1},{4,8},{5,9},{6,2},{7,3},{8,12},{9,13},{10,... | collective-permute-start | bytes 1572872 | tf_op jit(solution)/shard_map/ppermute | solution.py:285
  20.1 0.4 collective-permute-start.4
  20.5 0.8 copy-done.3
  21.3 0.0 collective-permute-done.7.refs_6_
  21.3 0.7 copy-done.10
  22.0 2.5 %shard_map.123 = f32[128,128]{1,0:T(8,128)} custom-call(s32[6,128]{1,0:T(8,128)S(1)} %bitcast.20, bf16[16,2048]{1,0:T(8,128)(2,1)} %bitcast.29, bf16[128,2048]{1,0:T(8,128)(2,1)} %refs_2_.1), custom_call_target="tpu_custom_call" | custom-call | tf_op jit(solution)/shard_map/pallas_call | solution.py:58
  24.5 4.9 %all-to-all-start = ((f32[16,8,128]{2,1,0:T(8,128)}), f32[16,8,128]{2,1,0:T(8,128)S(1)}, u32[]{:S(2)}, u32[]{:S(2)}) async-start(f32[16,8,128]{2,1,0:T(8,128)} %bitcast.8), calls=%async_computation | async-start | bytes 131072 | tf_op jit(solution)/shard_map/all_to_all | solution.py:304
  29.5 2.2 %collective-permute-done.3.refs_0_ = bf16[128,2048]{1,0:T(8,128)(2,1)S(1)} collective-permute-done((bf16[128,2048]{1,0:T(8,128)(2,1)S(1)}, bf16[128,2048]{1,0:T(8,128)(2,1)S(1)}, u32[]{:S(2)}, u32[]{:S(2)}) %collective-permute-start.3) | collective-permute-done | bytes 524320 | tf_op jit(solution)/shard_map/ppermute | solution.py:285
  31.7 1.5 %collective-permute-done.4.refs_1_ = bf16[128,2048]{1,0:T(8,128)(2,1)S(1)} collective-permute-done((bf16[128,2048]{1,0:T(8,128)(2,1)S(1)}, bf16[128,2048]{1,0:T(8,128)(2,1)S(1)}, u32[]{:S(2)}, u32[]{:S(2)}) %collective-permute-start.4) | collective-permute-done | bytes 524320 | tf_op jit(solution)/shard_map/ppermute | solution.py:285
  33.2 1.8 %collective-permute-start.5 = (bf16[128,2048]{1,0:T(8,128)(2,1)S(1)}, bf16[128,2048]{1,0:T(8,128)(2,1)S(1)}, u32[]{:S(2)}, u32[]{:S(2)}) collective-permute-start(bf16[128,2048]{1,0:T(8,128)(2,1)S(1)} %collective-permute-done.3.refs_0_), channel_id=1, source_target_pairs={{0,4},{1,5},{2,0},{3,1},{4,8},{5,9},{6,2},{7,3},{8,12},{9,13},{10,... | collective-permute-start | bytes 1572872 | tf_op jit(solution)/shard_map/ppermute | solution.py:285
  34.9 0.3 collective-permute-start.6
  35.2 1.7 %all-to-all-done = f32[16,8,128]{2,1,0:T(8,128)S(1)} async-done(((f32[16,8,128]{2,1,0:T(8,128)}), f32[16,8,128]{2,1,0:T(8,128)S(1)}, u32[]{:S(2)}, u32[]{:S(2)}) %all-to-all-start) | async-done | bytes 65568 | tf_op jit(solution)/shard_map/all_to_all | solution.py:304
  36.8 0.7 copy-done.7
  37.5 9.7 %shard_map.124 = (f32[128,2048]{1,0:T(8,128)S(1)}, f32[128,2048]{1,0:T(8,128)S(1)}, bf16[704,2048]{1,0:T(8,128)(2,1)S(1)}, bf16[704,2048]{1,0:T(8,128)(2,1)S(1)}...) custom-call(s32[1]{0:T(128)} %bitcast.me_ref, ...), custom_call_target="tpu_custom_call" | custom-call | flops 4429185024 | bytes 17301504 | tf_op jit(solution)/shard_map/pallas_call | solution.py:160
  47.2 0.0 collective-permute-done.6.above_ref.refs_1_
  47.2 0.1 shard_map.125
  47.3 0.3 collective-permute-start.10
  47.6 1.7 %collective-permute-start.9 = (bf16[64,2048]{1,0:T(8,128)(2,1)S(1)}, bf16[64,2048]{1,0:T(8,128)(2,1)S(1)}, u32[]{:S(2)}, u32[]{:S(2)}) collective-permute-start(bf16[64,2048]{1,0:T(8,128)(2,1)S(1)} %get-tuple-element.66), channel_id=1, source_target_pairs={{0,4},{1,5},{2,0},{3,1},{4,8},{5,9},{6,2},{7,3},{8,12},{9,13},{10,... | collective-permute-start | bytes 786440 | tf_op jit(solution)/shard_map/ppermute | solution.py:285
  49.3 5.9 %shard_map.126 = (f32[64,2048]{1,0:T(8,128)S(1)}, f32[64,2048]{1,0:T(8,128)S(1)}, f32[64,2048]{1,0:T(8,128)S(1)}, f32[64,2048]{1,0:T(8,128)S(1)}) custom-call(s32[1]{0:T(128)} %bitcast.me_ref, s32[64]{0:T(128)S(1)} %copy-done.7, bf16[128,2048]{1,0:T(8,128)(2,1)S(1)} %collective-permute-done.5.below_ref.refs_0_, ...), custom_call_target="tpu_custom_call" | custom-call | flops 4429185024 | bytes 17301504 | tf_op jit(solution)/shard_map/pallas_call | solution.py:160
  55.2 0.0 collective-permute-done.10.refs_1_
  55.2 0.3 collective-permute-done.9.refs_0_
  55.6 1.1 collective-permute-start.11
  56.7 0.0 copy-start.2
  56.7 0.0 copy-start.4
  56.7 1.2 %collective-permute-start.12 = (bf16[64,2048]{1,0:T(8,128)(2,1)S(1)}, bf16[64,2048]{1,0:T(8,128)(2,1)S(1)}, u32[]{:S(2)}, u32[]{:S(2)}) collective-permute-start(bf16[64,2048]{1,0:T(8,128)(2,1)S(1)} %convert_element_type.34), channel_id=1, source_target_pairs={{4,0},{5,1},{0,2},{1,3},{8,4},{9,5},{2,6},{3,7},{12,8},{13,9},{6,1... | collective-permute-start | bytes 786440 | tf_op jit(solution)/shard_map/ppermute | solution.py:285
  57.9 5.9 %shard_map.127 = (f32[64,2048]{1,0:T(8,128)S(1)}, f32[64,2048]{1,0:T(8,128)S(1)}, f32[64,2048]{1,0:T(8,128)S(1)}, f32[64,2048]{1,0:T(8,128)S(1)}) custom-call(s32[1]{0:T(128)} %bitcast.me_ref, s32[64]{0:T(128)S(1)} %copy-done.8, bf16[64,2048]{1,0:T(8,128)(2,1)S(1)} %collective-permute-done.9.refs_0_, bf16[64,2048]{1,0:T(8,128)(2,1)S(1)} %collective-permute-done.10.refs_1_, ...), custom_call_target="tpu_custom_call" | custom-call | flops 4429185024 | bytes 17301504 | tf_op jit(solution)/shard_map/pallas_call | solution.py:160
  63.8 0.8 copy-done.5
  64.6 0.0 collective-permute-done.12.refs_5_
  64.6 1.1 collective-permute-start.13
  65.8 1.1 collective-permute-start.14
  66.8 5.9 %shard_map.128 = (f32[128,2048]{1,0:T(8,128)S(1)}, f32[128,2048]{1,0:T(8,128)S(1)}) custom-call(s32[1]{0:T(128)} %bitcast.me_ref, s32[64]{0:T(128)S(1)} %copy-done.8, bf16[128,2048]{1,0:T(8,128)(2,1)S(1)} %copy-done.2, bf16[128,2048]{1,0:T(8,128)(2,1)S(1)} %copy-done.4, f32[128,128]{1,0:T(8,128)S(1)} %bitcast.19, ...), custom_call_target="tpu_custom_call" | custom-call | flops 4429185024 | bytes 17301504 | tf_op jit(solution)/shard_map/pallas_call | solution.py:160
  72.7 0.0 collective-permute-done.13
  72.7 0.0 collective-permute-done.14
  72.8 0.7 collective-permute-start.16
  73.5 0.1 add_convert_fusion.1
  73.5 1.4 %collective-permute-start.15 = (bf16[64,2048]{1,0:T(8,128)(2,1)S(1)}, bf16[64,2048]{1,0:T(8,128)(2,1)S(1)}, u32[]{:S(2)}, u32[]{:S(2)}) collective-permute-start(bf16[64,2048]{1,0:T(8,128)(2,1)S(1)} %add_convert_fusion.1), channel_id=1, source_target_pairs={{0,4},{1,5},{2,0},{3,1},{4,8},{5,9},{6,2},{7,3},{8,12},{9,13},{10,... | collective-permute-start | bytes 786440 | tf_op jit(solution)/shard_map/ppermute | solution.py:285
  75.0 4.2 %collective-permute-done.16.refs_4_ = bf16[64,2048]{1,0:T(8,128)(2,1)S(1)} collective-permute-done((bf16[64,2048]{1,0:T(8,128)(2,1)S(1)}, bf16[64,2048]{1,0:T(8,128)(2,1)S(1)}, u32[]{:S(2)}, u32[]{:S(2)}) %collective-permute-start.16) | collective-permute-done | bytes 262176 | tf_op jit(solution)/shard_map/ppermute | solution.py:285
  79.2 0.8 collective-permute-done.15.refs_3_
  80.0 1.1 shard_map.129
  81.1 1.4 %collective-permute-start.17 = (bf16[128,2048]{1,0:T(8,128)(2,1)}, bf16[128,2048]{1,0:T(8,128)(2,1)}, u32[]{:S(2)}, u32[]{:S(2)}) collective-permute-start(bf16[128,2048]{1,0:T(8,128)(2,1)} %get-tuple-element.102), channel_id=1, source_target_pairs={{0,4},{1,5},{2,0},{3,1},{4,8},{5,9},{6,2},{7,3},{8,12},{9,13},{10,... | collective-permute-start | bytes 1572872 | tf_op jit(solution)/shard_map/ppermute | solution.py:285
  82.5 0.6 collective-permute-start.18
  83.1 3.9 %all-to-all-start.1 = ((bf16[16,8,2048]{2,1,0:T(8,128)(2,1)}), bf16[16,8,2048]{2,1,0:T(8,128)(2,1)S(1)}, u32[]{:S(2)}, u32[]{:S(2)}) async-start(bf16[16,8,2048]{2,1,0:T(8,128)(2,1)} %shard_map.122), calls=%async_computation.1 | async-start | bytes 1048576 | tf_op jit(solution)/shard_map/all_to_all | solution.py:311
  87.0 6.5 %collective-permute-done.17.refs_2_ = bf16[128,2048]{1,0:T(8,128)(2,1)} collective-permute-done((bf16[128,2048]{1,0:T(8,128)(2,1)}, bf16[128,2048]{1,0:T(8,128)(2,1)}, u32[]{:S(2)}, u32[]{:S(2)}) %collective-permute-start.17) | collective-permute-done | bytes 524320 | tf_op jit(solution)/shard_map/ppermute | solution.py:285
  93.4 6.0 %collective-permute-done.18.refs_3_ = bf16[128,2048]{1,0:T(8,128)(2,1)} collective-permute-done((bf16[128,2048]{1,0:T(8,128)(2,1)}, bf16[128,2048]{1,0:T(8,128)(2,1)}, u32[]{:S(2)}, u32[]{:S(2)}) %collective-permute-start.18) | collective-permute-done | bytes 524320 | tf_op jit(solution)/shard_map/ppermute | solution.py:285
  99.4 2.3 %shard_map.130 = (bf16[128,2048]{1,0:T(8,128)(2,1)}, bf16[128,2048]{1,0:T(8,128)(2,1)}) custom-call(f32[128,2048]{1,0:T(8,128)S(1)} %get-tuple-element.92.refs_0_, f32[128,2048]{1,0:T(8,128)S(1)} %get-tuple-element.93.refs_1_, bf16[128,2048]{1,0:T(8,128)(2,1)} %collective-permute-done.17.refs_2_, bf16[128,2048]{1,0:T(8,128)(2,1)} %collective-permute-done.18.refs_3_), custom_call_target="tpu_custom_call" | custom-call | tf_op jit(solution)/shard_map/pallas_call | solution.py:249
  101.7 0.0 collective-permute-start.19
  101.7 2.0 %collective-permute-start.20 = (bf16[128,2048]{1,0:T(8,128)(2,1)}, bf16[128,2048]{1,0:T(8,128)(2,1)S(1)}, u32[]{:S(2)}, u32[]{:S(2)}) collective-permute-start(bf16[128,2048]{1,0:T(8,128)(2,1)} %get-tuple-element.107), channel_id=1, source_target_pairs={{4,0},{5,1},{0,2},{1,3},{8,4},{9,5},{2,6},{3,7},{12,8},{13,9},{6,1... | collective-permute-start | bytes 1572872 | tf_op jit(solution)/shard_map/ppermute | solution.py:285
  103.8 0.0 all-to-all-done.1
  103.8 0.0 copy-start.6
  103.8 1.0 copy-done.6
  104.8 1.2 %shard_map.131 = bf16[128,2048]{1,0:T(8,128)(2,1)} custom-call(bf16[128,2048]{1,0:T(8,128)(2,1)S(1)} %bitcast.15, s32[16,16]{1,0:T(8,128)S(1)} %copy-done.9, s32[1,16]{1,0:T(1,128)S(1)} %bitcast.21, s32[1]{0:T(128)} %bitcast.me_ref, bf16[128,2048]{1,0:T(8,128)(2,1)S(1)} %copy-done.6), custom_call_target="tpu_custom_call" | custom-call | tf_op jit(solution)/shard_map/pallas_call | solution.py:202
  106.0 5.1 %collective-permute-done.19 = bf16[128,2048]{1,0:T(8,128)(2,1)S(1)} collective-permute-done((bf16[128,2048]{1,0:T(8,128)(2,1)}, bf16[128,2048]{1,0:T(8,128)(2,1)S(1)}, u32[]{:S(2)}, u32[]{:S(2)}) %collective-permute-start.19) | collective-permute-done | bytes 524320 | tf_op jit(solution)/shard_map/ppermute | solution.py:285
  111.1 1.3 %collective-permute-done.20 = bf16[128,2048]{1,0:T(8,128)(2,1)S(1)} collective-permute-done((bf16[128,2048]{1,0:T(8,128)(2,1)}, bf16[128,2048]{1,0:T(8,128)(2,1)S(1)}, u32[]{:S(2)}, u32[]{:S(2)}) %collective-permute-start.20) | collective-permute-done | bytes 524320 | tf_op jit(solution)/shard_map/ppermute | solution.py:285
  112.5 2.1 %fusion.1 = bf16[128,2048]{1,0:T(8,128)(2,1)} fusion(f32[64,2048]{1,0:T(8,128)} %copy-done.5, f32[64,2048]{1,0:T(8,128)S(1)} %get-tuple-element.80, bf16[128,2048]{1,0:T(8,128)(2,1)S(1)} %collective-permute-done.20, bf16[128,2048]{1,0:T(8,128)(2,1)S(1)} %collective-permute-done.19), kind=kLoop, calls=%fused_computation.2 | loop fusion | flops 1572864 | bytes 2621440 | tf_op jit(solution)/shard_map/convert_element_type | solution.py:334
  (28 shorter events, 0.2 us)
Async XLA Ops:
  0.6 5.6 %collective-permute-start.2 = (bf16[704,2048]{1,0:T(8,128)(2,1)}, bf16[704,2048]{1,0:T(8,128)(2,1)S(1)}, u32[]{:S(2)}, u32[]{:S(2)}) collective-permute-start(bf16[704,2048]{1,0:T(8,128)(2,1)} %bitcast.24), channel_id=1, source_target_pairs={{0,1},{1,0},{2,3},{3,2},{4,5},{5,4},{6,7},{7,6},{8,9},{9,8},{10,11... | collective-permute-start | bytes 8650760 | tf_op jit(solution)/shard_map/ppermute | solution.py:285
  1.1 20.2 %collective-permute-start.7 = (bf16[704,2048]{1,0:T(8,128)(2,1)}, bf16[704,2048]{1,0:T(8,128)(2,1)S(1)}, u32[]{:S(2)}, u32[]{:S(2)}) collective-permute-start(bf16[704,2048]{1,0:T(8,128)(2,1)} %bitcast.22), channel_id=1, source_target_pairs={{0,1},{1,0},{2,3},{3,2},{4,5},{5,4},{6,7},{7,6},{8,9},{9,8},{10,11... | collective-permute-start | bytes 8650760 | tf_op jit(solution)/shard_map/ppermute | solution.py:285
  1.2 35.6 %collective-permute-start.8 = (bf16[704,2048]{1,0:T(8,128)(2,1)}, bf16[704,2048]{1,0:T(8,128)(2,1)}, u32[]{:S(2)}, u32[]{:S(2)}) collective-permute-start(bf16[704,2048]{1,0:T(8,128)(2,1)} %bitcast.26), channel_id=1, source_target_pairs={{0,1},{1,0},{2,3},{3,2},{4,5},{5,4},{6,7},{7,6},{8,9},{9,8},{10,11... | collective-permute-start | bytes 8650760 | tf_op jit(solution)/shard_map/ppermute | solution.py:285
  1.7 15.3 %collective-permute-start = (bf16[128,2048]{1,0:T(8,128)(2,1)}, bf16[128,2048]{1,0:T(8,128)(2,1)S(1)}, u32[]{:S(2)}, u32[]{:S(2)}) collective-permute-start(bf16[128,2048]{1,0:T(8,128)(2,1)} %refs_2_.1), channel_id=1, source_target_pairs={{0,4},{1,5},{2,0},{3,1},{4,8},{5,9},{6,2},{7,3},{8,12},{9,13},{10,... | collective-permute-start | bytes 1572872 | tf_op jit(solution)/shard_map/ppermute | solution.py:285
  4.3 14.2 %collective-permute-start.1 = (bf16[128,2048]{1,0:T(8,128)(2,1)}, bf16[128,2048]{1,0:T(8,128)(2,1)S(1)}, u32[]{:S(2)}, u32[]{:S(2)}) collective-permute-start(bf16[128,2048]{1,0:T(8,128)(2,1)} %refs_2_.1), channel_id=1, source_target_pairs={{4,0},{5,1},{0,2},{1,3},{8,4},{9,5},{2,6},{3,7},{12,8},{13,9},{6,1... | collective-permute-start | bytes 1572872 | tf_op jit(solution)/shard_map/ppermute | solution.py:285
  6.3 18.2 %copy-start.12 = (bf16[704,2048]{1,0:T(8,128)(2,1)}, bf16[704,2048]{1,0:T(8,128)(2,1)S(1)}, u32[]{:S(2)}) copy-start(bf16[704,2048]{1,0:T(8,128)(2,1)S(1)} %collective-permute-done.2.refs_7_) | copy-start | bytes 8650756
  17.0 14.7 %copy-start.1 = (bf16[128,2048]{1,0:T(8,128)(2,1)}, bf16[128,2048]{1,0:T(8,128)(2,1)S(1)}, u32[]{:S(2)}) copy-start(bf16[128,2048]{1,0:T(8,128)(2,1)S(1)} %collective-permute-done.refs_0_) | copy-start | bytes 1572868
  18.5 13.2 %collective-permute-start.3 = (bf16[128,2048]{1,0:T(8,128)(2,1)S(1)}, bf16[128,2048]{1,0:T(8,128)(2,1)S(1)}, u32[]{:S(2)}, u32[]{:S(2)}) collective-permute-start(bf16[128,2048]{1,0:T(8,128)(2,1)S(1)} %collective-permute-done.refs_0_), channel_id=1, source_target_pairs={{0,4},{1,5},{2,0},{3,1},{4,8},{5,9},{6,2},{7,3},{8,12},{9,13},{10,... | collective-permute-start | bytes 1572872 | tf_op jit(solution)/shard_map/ppermute | solution.py:285
  20.1 13.1 %collective-permute-start.4 = (bf16[128,2048]{1,0:T(8,128)(2,1)S(1)}, bf16[128,2048]{1,0:T(8,128)(2,1)S(1)}, u32[]{:S(2)}, u32[]{:S(2)}) collective-permute-start(bf16[128,2048]{1,0:T(8,128)(2,1)S(1)} %collective-permute-done.1.refs_1_), channel_id=1, source_target_pairs={{4,0},{5,1},{0,2},{1,3},{8,4},{9,5},{2,6},{3,7},{12,8},{13,9},{6,1... | collective-permute-start | bytes 1572872 | tf_op jit(solution)/shard_map/ppermute | solution.py:285
  20.5 0.8 copy-start.3
  21.3 3.2 %copy-start.13 = (bf16[704,2048]{1,0:T(8,128)(2,1)}, bf16[704,2048]{1,0:T(8,128)(2,1)S(1)}, u32[]{:S(2)}) copy-start(bf16[704,2048]{1,0:T(8,128)(2,1)S(1)} %collective-permute-done.7.refs_6_) | copy-start | bytes 8650756
  21.3 0.7 copy-start.10
  24.5 12.3 %all-to-all-start = ((f32[16,8,128]{2,1,0:T(8,128)}), f32[16,8,128]{2,1,0:T(8,128)S(1)}, u32[]{:S(2)}, u32[]{:S(2)}) async-start(f32[16,8,128]{2,1,0:T(8,128)} %bitcast.8), calls=%async_computation | async-start | bytes 131072 | tf_op jit(solution)/shard_map/all_to_all | solution.py:304
  33.2 14.0 %collective-permute-start.5 = (bf16[128,2048]{1,0:T(8,128)(2,1)S(1)}, bf16[128,2048]{1,0:T(8,128)(2,1)S(1)}, u32[]{:S(2)}, u32[]{:S(2)}) collective-permute-start(bf16[128,2048]{1,0:T(8,128)(2,1)S(1)} %collective-permute-done.3.refs_0_), channel_id=1, source_target_pairs={{0,4},{1,5},{2,0},{3,1},{4,8},{5,9},{6,2},{7,3},{8,12},{9,13},{10,... | collective-permute-start | bytes 1572872 | tf_op jit(solution)/shard_map/ppermute | solution.py:285
  34.9 12.3 %collective-permute-start.6 = (bf16[128,2048]{1,0:T(8,128)(2,1)S(1)}, bf16[128,2048]{1,0:T(8,128)(2,1)S(1)}, u32[]{:S(2)}, u32[]{:S(2)}) collective-permute-start(bf16[128,2048]{1,0:T(8,128)(2,1)S(1)} %collective-permute-done.4.refs_1_), channel_id=1, source_target_pairs={{4,0},{5,1},{0,2},{1,3},{8,4},{9,5},{2,6},{3,7},{12,8},{13,9},{6,1... | collective-permute-start | bytes 1572872 | tf_op jit(solution)/shard_map/ppermute | solution.py:285
  36.8 0.7 copy-start.7
  47.3 8.0 %collective-permute-start.10 = (bf16[64,2048]{1,0:T(8,128)(2,1)S(1)}, bf16[64,2048]{1,0:T(8,128)(2,1)S(1)}, u32[]{:S(2)}, u32[]{:S(2)}) collective-permute-start(bf16[64,2048]{1,0:T(8,128)(2,1)S(1)} %get-tuple-element.67), channel_id=1, source_target_pairs={{4,0},{5,1},{0,2},{1,3},{8,4},{9,5},{2,6},{3,7},{12,8},{13,9},{6,1... | collective-permute-start | bytes 786440 | tf_op jit(solution)/shard_map/ppermute | solution.py:285
  47.6 7.9 %collective-permute-start.9 = (bf16[64,2048]{1,0:T(8,128)(2,1)S(1)}, bf16[64,2048]{1,0:T(8,128)(2,1)S(1)}, u32[]{:S(2)}, u32[]{:S(2)}) collective-permute-start(bf16[64,2048]{1,0:T(8,128)(2,1)S(1)} %get-tuple-element.66), channel_id=1, source_target_pairs={{0,4},{1,5},{2,0},{3,1},{4,8},{5,9},{6,2},{7,3},{8,12},{9,13},{10,... | collective-permute-start | bytes 786440 | tf_op jit(solution)/shard_map/ppermute | solution.py:285
  49.3 8.6 %copy-start = (bf16[128,2048]{1,0:T(8,128)(2,1)S(1)}, bf16[128,2048]{1,0:T(8,128)(2,1)}, u32[]{:S(2)}) copy-start(bf16[128,2048]{1,0:T(8,128)(2,1)} %refs_2_.1) | copy-start | bytes 1572868
  49.3 8.6 %copy-start.8 = (s32[64]{0:T(128)S(1)}, s32[64]{0:T(128)}, u32[]{:S(2)}) copy-start(s32[64]{0:T(128)} %constant.8.clone.order_ref) | copy-start | bytes 772
  55.6 9.0 %collective-permute-start.11 = (bf16[64,2048]{1,0:T(8,128)(2,1)S(1)}, bf16[64,2048]{1,0:T(8,128)(2,1)S(1)}, u32[]{:S(2)}, u32[]{:S(2)}) collective-permute-start(bf16[64,2048]{1,0:T(8,128)(2,1)S(1)} %convert_element_type.33), channel_id=1, source_target_pairs={{0,4},{1,5},{2,0},{3,1},{4,8},{5,9},{6,2},{7,3},{8,12},{9,13},{10,... | collective-permute-start | bytes 786440 | tf_op jit(solution)/shard_map/ppermute | solution.py:285
  56.7 10.1 %copy-start.2 = (bf16[128,2048]{1,0:T(8,128)(2,1)S(1)}, bf16[128,2048]{1,0:T(8,128)(2,1)}, u32[]{:S(2)}) copy-start(bf16[128,2048]{1,0:T(8,128)(2,1)} %copy-done.1) | copy-start | bytes 1572868
  56.7 10.1 %copy-start.4 = (bf16[128,2048]{1,0:T(8,128)(2,1)S(1)}, bf16[128,2048]{1,0:T(8,128)(2,1)}, u32[]{:S(2)}) copy-start(bf16[128,2048]{1,0:T(8,128)(2,1)} %copy-done.3) | copy-start | bytes 1572868
  56.7 7.9 %collective-permute-start.12 = (bf16[64,2048]{1,0:T(8,128)(2,1)S(1)}, bf16[64,2048]{1,0:T(8,128)(2,1)S(1)}, u32[]{:S(2)}, u32[]{:S(2)}) collective-permute-start(bf16[64,2048]{1,0:T(8,128)(2,1)S(1)} %convert_element_type.34), channel_id=1, source_target_pairs={{4,0},{5,1},{0,2},{1,3},{8,4},{9,5},{2,6},{3,7},{12,8},{13,9},{6,1... | collective-permute-start | bytes 786440 | tf_op jit(solution)/shard_map/ppermute | solution.py:285
  63.8 0.8 copy-start.5
  64.6 8.1 %collective-permute-start.13 = (bf16[64,2048]{1,0:T(8,128)(2,1)S(1)}, bf16[64,2048]{1,0:T(8,128)(2,1)S(1)}, u32[]{:S(2)}, u32[]{:S(2)}) collective-permute-start(bf16[64,2048]{1,0:T(8,128)(2,1)S(1)} %convert_element_type.35), channel_id=1, source_target_pairs={{0,4},{1,5},{2,0},{3,1},{4,8},{5,9},{6,2},{7,3},{8,12},{9,13},{10,... | collective-permute-start | bytes 786440 | tf_op jit(solution)/shard_map/ppermute | solution.py:285
  65.8 7.0 %collective-permute-start.14 = (bf16[64,2048]{1,0:T(8,128)(2,1)S(1)}, bf16[64,2048]{1,0:T(8,128)(2,1)S(1)}, u32[]{:S(2)}, u32[]{:S(2)}) collective-permute-start(bf16[64,2048]{1,0:T(8,128)(2,1)S(1)} %convert_element_type.36), channel_id=1, source_target_pairs={{4,0},{5,1},{0,2},{1,3},{8,4},{9,5},{2,6},{3,7},{12,8},{13,9},{6,1... | collective-permute-start | bytes 786440 | tf_op jit(solution)/shard_map/ppermute | solution.py:285
  72.8 6.4 %collective-permute-start.16 = (bf16[64,2048]{1,0:T(8,128)(2,1)S(1)}, bf16[64,2048]{1,0:T(8,128)(2,1)S(1)}, u32[]{:S(2)}, u32[]{:S(2)}) collective-permute-start(bf16[64,2048]{1,0:T(8,128)(2,1)S(1)} %add_convert_fusion), channel_id=1, source_target_pairs={{4,0},{5,1},{0,2},{1,3},{8,4},{9,5},{2,6},{3,7},{12,8},{13,9},{6,1... | collective-permute-start | bytes 786440 | tf_op jit(solution)/shard_map/ppermute | solution.py:285
  73.5 6.4 %collective-permute-start.15 = (bf16[64,2048]{1,0:T(8,128)(2,1)S(1)}, bf16[64,2048]{1,0:T(8,128)(2,1)S(1)}, u32[]{:S(2)}, u32[]{:S(2)}) collective-permute-start(bf16[64,2048]{1,0:T(8,128)(2,1)S(1)} %add_convert_fusion.1), channel_id=1, source_target_pairs={{0,4},{1,5},{2,0},{3,1},{4,8},{5,9},{6,2},{7,3},{8,12},{9,13},{10,... | collective-permute-start | bytes 786440 | tf_op jit(solution)/shard_map/ppermute | solution.py:285
  81.1 22.7 %copy-start.9 = (s32[16,16]{1,0:T(8,128)S(1)}, s32[16,16]{1,0:T(8,128)}, u32[]{:S(2)}) copy-start(s32[16,16]{1,0:T(8,128)} %counts_ref.1) | copy-start | bytes 3076
  81.1 22.7 %copy-start.11 = (s32[16]{0:T(128)S(1)}, s32[16]{0:T(128)}, u32[]{:S(2)}) copy-start(s32[16]{0:T(128)} %param.19) | copy-start | bytes 196
  81.1 12.4 %collective-permute-start.17 = (bf16[128,2048]{1,0:T(8,128)(2,1)}, bf16[128,2048]{1,0:T(8,128)(2,1)}, u32[]{:S(2)}, u32[]{:S(2)}) collective-permute-start(bf16[128,2048]{1,0:T(8,128)(2,1)} %get-tuple-element.102), channel_id=1, source_target_pairs={{0,4},{1,5},{2,0},{3,1},{4,8},{5,9},{6,2},{7,3},{8,12},{9,13},{10,... | collective-permute-start | bytes 1572872 | tf_op jit(solution)/shard_map/ppermute | solution.py:285
  82.5 17.0 %collective-permute-start.18 = (bf16[128,2048]{1,0:T(8,128)(2,1)}, bf16[128,2048]{1,0:T(8,128)(2,1)}, u32[]{:S(2)}, u32[]{:S(2)}) collective-permute-start(bf16[128,2048]{1,0:T(8,128)(2,1)} %get-tuple-element.103), channel_id=1, source_target_pairs={{4,0},{5,1},{0,2},{1,3},{8,4},{9,5},{2,6},{3,7},{12,8},{13,9},{6,1... | collective-permute-start | bytes 1572872 | tf_op jit(solution)/shard_map/ppermute | solution.py:285
  83.1 20.7 %all-to-all-start.1 = ((bf16[16,8,2048]{2,1,0:T(8,128)(2,1)}), bf16[16,8,2048]{2,1,0:T(8,128)(2,1)S(1)}, u32[]{:S(2)}, u32[]{:S(2)}) async-start(bf16[16,8,2048]{2,1,0:T(8,128)(2,1)} %shard_map.122), calls=%async_computation.1 | async-start | bytes 1048576 | tf_op jit(solution)/shard_map/all_to_all | solution.py:311
  101.7 9.4 %collective-permute-start.19 = (bf16[128,2048]{1,0:T(8,128)(2,1)}, bf16[128,2048]{1,0:T(8,128)(2,1)S(1)}, u32[]{:S(2)}, u32[]{:S(2)}) collective-permute-start(bf16[128,2048]{1,0:T(8,128)(2,1)} %get-tuple-element.106), channel_id=1, source_target_pairs={{0,4},{1,5},{2,0},{3,1},{4,8},{5,9},{6,2},{7,3},{8,12},{9,13},{10,... | collective-permute-start | bytes 1572872 | tf_op jit(solution)/shard_map/ppermute | solution.py:285
  101.7 10.7 %collective-permute-start.20 = (bf16[128,2048]{1,0:T(8,128)(2,1)}, bf16[128,2048]{1,0:T(8,128)(2,1)S(1)}, u32[]{:S(2)}, u32[]{:S(2)}) collective-permute-start(bf16[128,2048]{1,0:T(8,128)(2,1)} %get-tuple-element.107), channel_id=1, source_target_pairs={{4,0},{5,1},{0,2},{1,3},{8,4},{9,5},{2,6},{3,7},{12,8},{13,9},{6,1... | collective-permute-start | bytes 1572872 | tf_op jit(solution)/shard_map/ppermute | solution.py:285
  103.8 1.0 copy-start.6

commit v5 on v4

--- a/solution.py
+++ b/solution.py
@@ -69,25 +69,29 @@
     )(expert_picks.T, in_hbm(router.T), in_hbm(tokens))
 
 
-def spans_kernel(span_of_ref, rows_hbm, out_ref, sems):
-    copies = [
-        pltpu.make_async_copy(rows_hbm.at[span_of_ref[d]], out_ref.at[d], sems.at[d]) for d in range(rows_hbm.shape[0])
-    ]
+def spans_kernel(me_ref, span_of_ref, rows_hbm, keep_ref, give_ref, sems):
+    copies = []
+    for c in range(keep_ref.shape[0]):
+        for j, out in enumerate((keep_ref, give_ref)):
+            owner = 2 * c + (me_ref[0] + j) % 2
+            copies.append(pltpu.make_async_copy(rows_hbm.at[span_of_ref[owner]], out.at[c], sems.at[c, j]))
     for copy in copies:
         copy.start()
     for copy in copies:
         copy.wait()
 
 
-def by_owner(image_rows, span_of):
+def by_owner(me, image_rows, span_of):
+    devices, slots, width = image_rows.shape
+    smem = pl.BlockSpec(memory_space=pltpu.SMEM)
     return pl.pallas_call(
         spans_kernel,
-        out_shape=jax.ShapeDtypeStruct(image_rows.shape, image_rows.dtype),
-        in_specs=[pl.BlockSpec(memory_space=pltpu.SMEM), pl.BlockSpec(memory_space=pl.ANY)],
-        out_specs=pl.BlockSpec(memory_space=pltpu.VMEM),
-        scratch_shapes=[pltpu.SemaphoreType.DMA((image_rows.shape[0],))],
+        out_shape=[jax.ShapeDtypeStruct((devices // 2, slots, width), image_rows.dtype)] * 2,
+        in_specs=[smem, smem, pl.BlockSpec(memory_space=pl.ANY)],
+        out_specs=[pl.BlockSpec(memory_space=pltpu.VMEM)] * 2,
+        scratch_shapes=[pltpu.SemaphoreType.DMA((devices // 2, 2))],
         compiler_params=pltpu.CompilerParams(vmem_limit_bytes=4 * 2**20),
-    )(span_of, in_hbm(image_rows))
+    )(me[None], span_of, in_hbm(image_rows))
 
 
 def ffn_kernel(count, results, sizes, offsets, chips, holds, me_ref, order_ref, *refs):
@@ -159,7 +163,7 @@
         weights = [in_hbm(w) for w in weights]
     return pl.pallas_call(
         functools.partial(ffn_kernel, len(shards), results, sizes, offsets, chips, kept),
-        out_shape=[jax.ShapeDtypeStruct((block, width), jnp.float32)] * results
+        out_shape=[jax.ShapeDtypeStruct((block, width), jnp.bfloat16)] * results
         + [pltpu.VMEM(w.shape, w.dtype) for w in weights[:kept]],
         in_specs=[smem] * 2 + [vmem] * (len(shards) + 1) + [hbm if holds else vmem] * 6,
         out_specs=[vmem] * (results + kept),
@@ -184,11 +188,12 @@
     live = jnp.sum(counts_ref[...] * mine, axis=1, keepdims=True)
     total = jnp.sum(live)
     lane = lax.broadcasted_iota(jnp.int32, (devices, held), 1)
-    holder = lane // slots
+    group = lane // slots
+    holder = 2 * (group // 2) + (me_ref[0] + group) % 2
     which = lax.broadcasted_iota(jnp.int32, (devices, held), 0)
     own = jnp.sum(jnp.where(which == holder, live, 0), axis=0, keepdims=True)
     start = jnp.sum(jnp.where(which < holder, live, 0), axis=0, keepdims=True)
-    offset = lane[:1] - holder[:1] * slots
+    offset = lane[:1] - group[:1] * slots
     place = jnp.where(offset < own, start + offset, -1)
     row = lax.broadcasted_iota(jnp.int32, (rows, held), 0)
     pick = (row == place).astype(jnp.bfloat16)
@@ -239,7 +244,7 @@
         at = 0
         for came in refs[2 + i * parts : 2 + (i + 1) * parts]:
             part = pl.ds(at, came.shape[0])
-            out[part, :] = (total[part, :] + came[...].astype(jnp.float32)).astype(out.dtype)
+            out[part, :] = (total[part, :].astype(jnp.float32) + came[...].astype(jnp.float32)).astype(out.dtype)
             at += came.shape[0]
 
 
@@ -253,6 +258,25 @@
         out_specs=[vmem] * 2,
         compiler_params=pltpu.CompilerParams(vmem_limit_bytes=8 * 2**20),
     )(above, below, *up_parts, *down_parts)
+
+
+def finish_kernel(first_ref, second_ref, up_ref, down_ref, out_ref):
+    half = first_ref.shape[0]
+    for i, mine in enumerate((first_ref, second_ref)):
+        part = pl.ds(i * half, half)
+        total = mine[...].astype(jnp.float32) + up_ref[part, :].astype(jnp.float32)
+        out_ref[part, :] = (total + down_ref[part, :].astype(jnp.float32)).astype(out_ref.dtype)
+
+
+def finish(first, second, came_up, came_down):
+    vmem = pl.BlockSpec(memory_space=pltpu.VMEM)
+    return pl.pallas_call(
+        finish_kernel,
+        out_shape=jax.ShapeDtypeStruct(came_up.shape, came_up.dtype),
+        in_specs=[vmem] * 4,
+        out_specs=vmem,
+        compiler_params=pltpu.CompilerParams(vmem_limit_bytes=8 * 2**20),
+    )(first, second, came_up, came_down)
 
 
 def tie(*arrays):
@@ -299,6 +323,11 @@
     def run_both(s):
         return run([below[s], above[s]], [chips - s, s])
 
+    parity = [[2 * c + k for c in range(chips)] for k in range(2)]
+
+    def exchange(x):
+        return lax.all_to_all(x, "expert", split_axis=0, concat_axis=0, tiled=True, axis_index_groups=parity)
+
     expert_picks, _ = tie(expert_picks, others[0])
     table = route_of(tokens, expert_picks, router)
     table = lax.all_to_all(table.reshape(devices, 8, -1), "expert", split_axis=0, concat_axis=0, tiled=True)
@@ -307,8 +336,7 @@
     number = jnp.arange(devices, dtype=jnp.int32)
     span_of = jnp.sum(jnp.where(span_owner[:, None] == number[None, :], number[:, None], 0), axis=0)
     span_of, _ = tie(span_of, others[1])
-    image_send = by_owner(image_rows[0], span_of)
-    arrived = lax.all_to_all(image_send, "expert", split_axis=0, concat_axis=0, tiled=True)
+    keep, give = by_owner(me, image_rows[0], span_of)
 
     below, above = [tokens], [tokens]
     from_below, from_above = {}, {}
@@ -323,24 +351,27 @@
                 below[s], above[s], from_below[s - 1], from_above[s - 1]
             )
         else:
-            below[s], above[s], image_send = tie(below[s], above[s], image_send)
+            if s == 1:
+                below[s], above[s], keep, give = tie(below[s], above[s], keep, give)
+                image_send = jnp.stack([keep, send(give, sibling)], axis=1)
+            else:
+                below[s], above[s], image_send = tie(below[s], above[s], image_send)
+
+    arrived = exchange(image_send)
 
     first, second = cut(below[-1], above[-1])
     first, second = send(first, up), send(second, down)
     done = run([below[-1], above[-1]], [chips - far + 1, far - 1], 4)
     first, second, *done = tie(first, second, *done)
 
-    def low(x):
-        return x.astype(jnp.bfloat16)
-
-    def add(mine, came):
-        return low(mine + came.astype(jnp.float32))
+    def add(mine, *came):
+        return sum([c.astype(jnp.float32) for c in came], mine.astype(jnp.float32)).astype(jnp.bfloat16)
 
     below_first, below_second, above_first, above_second = done
-    short_up, short_down = send(low(above_first), up), send(low(below_second), down)
+    short_up, short_down = send(above_first, up), send(below_second, down)
     far_first, far_second, result_first, result_second = run([first, second, tokens], [far, 0], 4)
     short_up, short_down, far_first, far_second = tie(short_up, short_down, far_first, far_second)
-    long_up, long_down = send(low(far_second), up), send(low(far_first), down)
+    long_up, long_down = send(far_second, up), send(far_first, down)
     from_below[1], from_above[1] = run_both(1)
     long_up, long_down, short_up, short_down, from_below[1], from_above[1] = tie(
         long_up, long_down, short_up, short_down, from_below[1], from_above[1]
@@ -356,8 +387,7 @@
         going_up, going_down = tie(send(going_up, up), send(going_down, down))
         if s > 1:
             going_up, going_down = merge(from_above[s - 1], from_below[s - 1], [going_up], [going_down])
-    result = jnp.concatenate([result_first, result_second], axis=0)
-    moe_out = low(result + going_up.astype(jnp.float32) + going_down.astype(jnp.float32))
+    moe_out = finish(in_hbm(result_first), in_hbm(result_second), going_up, going_down)
 
     arrived = arrived.reshape(devices * slots, width)
     next_span = place_images(

time: 115 us -> 113 us (0.983)
  waiting for transfers between devices: 40.1 us -> 42.1 us
  local copies, waits for them, and re-layouts: 3.99 us -> 2.25 us
  other arithmetic: 3.04 us -> 1.72 us
    all_to_all x1, waiting for transfers between devices: 0.01 us -> 5.57 us  [exchange(): lax.all_to_all(x, 'expert', split_axis=0, concat_axis=0, tiled=True, axis...]
    unnamed x28 -> x20, local copies, waits for them, and re-layouts: 3.99 us -> 1.38 us
    ppermute x21 -> x22, waiting for transfers between devices: 38.4 us -> 36.2 us  [send(): return lax.ppermute(x, 'expert', pairs)]
    convert_element_type x7 -> x2, other arithmetic: 2.29 us -> 0.13 us  [add(): sum([c.astype(jnp.float32) for c in came], mine.astype(jnp.float32))]
    all_to_all x1, waiting for transfers between devices: 1.66 us -> 0.26 us  [local(): lax.all_to_all(table.reshape(devices, 8, -1), 'expert', split_axis=0, con...]
    pallas_call x2, Pallas kernels: 3.43 us -> 2.25 us  [merge(): pl.pallas_call(functools.partial(merge_kernel, parts), out_shape=[jax.Sha...]
    pallas_call x1 -> x2, Pallas kernels: 2.94 us -> 3.7 us  [the longest x1 2.01 us: finish(): pl.pallas_call(finish_kernel, out_shape=jax.ShapeDtypeStruct(came_up.shap...]
    ppermute x21 -> x22, starting transfers between devices: 20.4 us -> 20.1 us  [send(): return lax.ppermute(x, 'expert', pairs)]
  transfers between devices with their start and end apart: 23 -> 24, of which waited for: 13 -> 15; matrix products, arithmetic and copies ran while one was open for 1% -> 2% of each run, Pallas kernels for 32% -> 30%
where the time goes in v5:
time: 113 us; the launch traced here: 112 us
  waiting for transfers between devices  42.1 us (37%)
  Pallas kernels  36.5 us (32%)
  starting transfers between devices  29.1 us (26%)
  local copies, waits for them, and re-layouts  2.25 us (2%)
  other arithmetic  1.72 us (2%)
    ppermute x22, waiting for transfers between devices, send(): return lax.ppermute(x, 'expert', pairs)  36.2 us
    pallas_call x4, Pallas kernels, ffn(): pl.pallas_call(functools.partial(ffn_kernel, len(shards), results, sizes,...  27.2 us
    ppermute x22, starting transfers between devices, send(): return lax.ppermute(x, 'expert', pairs)  20.1 us
    all_to_all x1, waiting for transfers between devices, exchange(): lax.all_to_all(x, 'expert', split_axis=0, concat_axis=0, tiled=True, axis...  5.57 us
    all_to_all x1, starting transfers between devices, local(): lax.all_to_all(table.reshape(devices, 8, -1), 'expert', split_axis=0, con...  5.05 us
    all_to_all x1, starting transfers between devices, exchange(): lax.all_to_all(x, 'expert', split_axis=0, concat_axis=0, tiled=True, axis...  3.9 us
  transfers between devices with their start and end apart: 24, of which 15 were waited for; matrix products, arithmetic and copies ran while one was open for 2% of the time, Pallas kernels for 30%

profile of v5, /device:TPU:0, one launch (start us, length us, event | category | flops | bytes accessed | tf_op | source)
XLA Modules:
  0.0 112.4 jit_solution(17956681120357638914)
XLA Ops:
  0.6 0.5 collective-permute-start.2
  1.1 0.1 collective-permute-start.8
  1.2 0.4 collective-permute-start.9
  1.7 2.7 %collective-permute-start = (bf16[128,2048]{1,0:T(8,128)(2,1)}, bf16[128,2048]{1,0:T(8,128)(2,1)S(1)}, u32[]{:S(2)}, u32[]{:S(2)}) collective-permute-start(bf16[128,2048]{1,0:T(8,128)(2,1)} %refs_2_.1), channel_id=1, source_target_pairs={{0,4},{1,5},{2,0},{3,1},{4,8},{5,9},{6,2},{7,3},{8,12},{9,13},{10,... | collective-permute-start | bytes 1572872 | tf_op jit(solution)/shard_map/ppermute | solution.py:309
  4.3 0.0 collective-permute-start.1
  4.3 0.7 select_reduce_fusion.span_of_ref
  5.1 1.3 %collective-permute-done.2.refs_7_ = bf16[704,2048]{1,0:T(8,128)(2,1)} collective-permute-done((bf16[704,2048]{1,0:T(8,128)(2,1)}, bf16[704,2048]{1,0:T(8,128)(2,1)}, u32[]{:S(2)}, u32[]{:S(2)}) %collective-permute-start.2) | collective-permute-done | bytes 2883616 | tf_op jit(solution)/shard_map/ppermute | solution.py:309
  6.4 1.7 %shard_map.122 = (bf16[8,8,2048]{2,1,0:T(8,128)(2,1)S(1)}, bf16[8,8,2048]{2,1,0:T(8,128)(2,1)S(1)}) custom-call(s32[1]{0:T(128)} %bitcast.me_ref, s32[16]{0:T(128)S(1)} %select_reduce_fusion.span_of_ref, bf16[16,8,2048]{2,1,0:T(8,128)(2,1)} %bitcast.31), custom_call_target="tpu_custom_call" | custom-call | tf_op jit(solution)/shard_map/pallas_call | solution.py:87
  8.1 8.9 %collective-permute-done.refs_0_ = bf16[128,2048]{1,0:T(8,128)(2,1)S(1)} collective-permute-done((bf16[128,2048]{1,0:T(8,128)(2,1)}, bf16[128,2048]{1,0:T(8,128)(2,1)S(1)}, u32[]{:S(2)}, u32[]{:S(2)}) %collective-permute-start) | collective-permute-done | bytes 524320 | tf_op jit(solution)/shard_map/ppermute | solution.py:309
  17.0 1.5 %collective-permute-done.1.refs_1_ = bf16[128,2048]{1,0:T(8,128)(2,1)S(1)} collective-permute-done((bf16[128,2048]{1,0:T(8,128)(2,1)}, bf16[128,2048]{1,0:T(8,128)(2,1)S(1)}, u32[]{:S(2)}, u32[]{:S(2)}) %collective-permute-start.1) | collective-permute-done | bytes 524320 | tf_op jit(solution)/shard_map/ppermute | solution.py:309
  18.5 1.6 %collective-permute-start.3 = (bf16[128,2048]{1,0:T(8,128)(2,1)S(1)}, bf16[128,2048]{1,0:T(8,128)(2,1)S(1)}, u32[]{:S(2)}, u32[]{:S(2)}) collective-permute-start(bf16[128,2048]{1,0:T(8,128)(2,1)S(1)} %collective-permute-done.refs_0_), channel_id=1, source_target_pairs={{0,4},{1,5},{2,0},{3,1},{4,8},{5,9},{6,2},{7,3},{8,12},{9,13},{10,... | collective-permute-start | bytes 1572872 | tf_op jit(solution)/shard_map/ppermute | solution.py:309
  20.1 0.4 collective-permute-start.4
  20.5 0.0 collective-permute-start.5
  20.6 0.7 copy-done.7
  21.2 2.2 %shard_map.123 = f32[128,128]{1,0:T(8,128)} custom-call(s32[6,128]{1,0:T(8,128)S(1)} %bitcast.23, bf16[16,2048]{1,0:T(8,128)(2,1)} %bitcast.33, bf16[128,2048]{1,0:T(8,128)(2,1)} %refs_2_.1), custom_call_target="tpu_custom_call" | custom-call | tf_op jit(solution)/shard_map/pallas_call | solution.py:58
  23.4 5.0 %all-to-all-start = ((f32[16,8,128]{2,1,0:T(8,128)}), f32[16,8,128]{2,1,0:T(8,128)S(1)}, u32[]{:S(2)}, u32[]{:S(2)}) async-start(f32[16,8,128]{2,1,0:T(8,128)} %bitcast.10), calls=%async_computation | async-start | bytes 131072 | tf_op jit(solution)/shard_map/all_to_all | solution.py:333
  28.5 0.9 pad_maximum_fusion
  29.3 2.3 %collective-permute-done.3.refs_0_ = bf16[128,2048]{1,0:T(8,128)(2,1)S(1)} collective-permute-done((bf16[128,2048]{1,0:T(8,128)(2,1)S(1)}, bf16[128,2048]{1,0:T(8,128)(2,1)S(1)}, u32[]{:S(2)}, u32[]{:S(2)}) %collective-permute-start.3) | collective-permute-done | bytes 524320 | tf_op jit(solution)/shard_map/ppermute | solution.py:309
  31.7 1.6 %collective-permute-done.4.refs_1_ = bf16[128,2048]{1,0:T(8,128)(2,1)S(1)} collective-permute-done((bf16[128,2048]{1,0:T(8,128)(2,1)S(1)}, bf16[128,2048]{1,0:T(8,128)(2,1)S(1)}, u32[]{:S(2)}, u32[]{:S(2)}) %collective-permute-start.4) | collective-permute-done | bytes 524320 | tf_op jit(solution)/shard_map/ppermute | solution.py:309
  33.3 1.9 %collective-permute-start.6 = (bf16[128,2048]{1,0:T(8,128)(2,1)S(1)}, bf16[128,2048]{1,0:T(8,128)(2,1)S(1)}, u32[]{:S(2)}, u32[]{:S(2)}) collective-permute-start(bf16[128,2048]{1,0:T(8,128)(2,1)S(1)} %collective-permute-done.3.refs_0_), channel_id=1, source_target_pairs={{0,4},{1,5},{2,0},{3,1},{4,8},{5,9},{6,2},{7,3},{8,12},{9,13},{10,... | collective-permute-start | bytes 1572872 | tf_op jit(solution)/shard_map/ppermute | solution.py:309
  35.2 0.1 collective-permute-start.7
  35.3 0.3 all-to-all-done
  35.6 0.7 copy-done.4
  36.3 9.6 %shard_map.124 = (bf16[128,2048]{1,0:T(8,128)(2,1)S(1)}, bf16[128,2048]{1,0:T(8,128)(2,1)S(1)}, bf16[704,2048]{1,0:T(8,128)(2,1)S(1)}, bf16[704,2048]{1,0:T(8,12...) custom-call(s32[1]{0:T(128)} %bitcast.me_ref, ...), custom_call_target="tpu_custom_call" | custom-call | flops 4429185024 | bytes 17301504 | tf_op jit(solution)/shard_map/pallas_call | solution.py:164
  45.9 0.0 collective-permute-done.6.below_ref.refs_0_
  45.9 0.5 collective-permute-done.7.above_ref.refs_1_
  46.4 0.1 shard_map.125
  46.5 1.4 %collective-permute-start.10 = (bf16[64,2048]{1,0:T(8,128)(2,1)S(1)}, bf16[64,2048]{1,0:T(8,128)(2,1)S(1)}, u32[]{:S(2)}, u32[]{:S(2)}) collective-permute-start(bf16[64,2048]{1,0:T(8,128)(2,1)S(1)} %get-tuple-element.79), channel_id=1, source_target_pairs={{0,4},{1,5},{2,0},{3,1},{4,8},{5,9},{6,2},{7,3},{8,12},{9,13},{10,... | collective-permute-start | bytes 786440 | tf_op jit(solution)/shard_map/ppermute | solution.py:309
  47.9 0.7 collective-permute-start.11
  48.5 5.9 %shard_map.126 = (bf16[64,2048]{1,0:T(8,128)(2,1)S(1)}, bf16[64,2048]{1,0:T(8,128)(2,1)S(1)}, bf16[64,2048]{1,0:T(8,128)(2,1)S(1)}, bf16[64,2048]{1,0:T(8,128)(2,1)S(1)}) custom-call(s32[1]{0:T(128)} %bitcast.me_ref, s32[64]{0:T(128)S(1)} %copy-done.5, bf16[128,2048]{1,0:T(8,128)(2,1)S(1)} %collective-permute-done.6.below_ref.refs_0_, ...), custom_call_target="tpu_custom_call" | custom-call | flops 4429185024 | bytes 17301504 | tf_op jit(solution)/shard_map/pallas_call | solution.py:164
  54.4 0.2 collective-permute-done.11.refs_1_
  54.6 1.2 %collective-permute-start.12 = (bf16[64,2048]{1,0:T(8,128)(2,1)S(1)}, bf16[64,2048]{1,0:T(8,128)(2,1)S(1)}, u32[]{:S(2)}, u32[]{:S(2)}) collective-permute-start(bf16[64,2048]{1,0:T(8,128)(2,1)S(1)} %get-tuple-element.95), channel_id=1, source_target_pairs={{0,4},{1,5},{2,0},{3,1},{4,8},{5,9},{6,2},{7,3},{8,12},{9,13},{10,... | collective-permute-start | bytes 786440 | tf_op jit(solution)/shard_map/ppermute | solution.py:309
  55.8 0.8 collective-permute-start.13
  56.7 5.8 %shard_map.127 = (bf16[64,2048]{1,0:T(8,128)(2,1)S(1)}, bf16[64,2048]{1,0:T(8,128)(2,1)S(1)}, bf16[64,2048]{1,0:T(8,128)(2,1)S(1)}, bf16[64,2048]{1,0:T(8,128)(2,1)S(1)}) custom-call(s32[1]{0:T(128)} %bitcast.me_ref, s32[64]{0:T(128)S(1)} %copy-done.5, bf16[64,2048]{1,0:T(8,128)(2,1)S(1)} %collective-permute-done.10.refs_0_, ...), custom_call_target="tpu_custom_call" | custom-call | flops 4429185024 | bytes 17301504 | tf_op jit(solution)/shard_map/pallas_call | solution.py:164
  62.5 0.0 collective-permute-done.13.refs_5_
  62.5 1.2 %collective-permute-start.14 = (bf16[64,2048]{1,0:T(8,128)(2,1)S(1)}, bf16[64,2048]{1,0:T(8,128)(2,1)S(1)}, u32[]{:S(2)}, u32[]{:S(2)}) collective-permute-start(bf16[64,2048]{1,0:T(8,128)(2,1)S(1)} %get-tuple-element.99), channel_id=1, source_target_pairs={{0,4},{1,5},{2,0},{3,1},{4,8},{5,9},{6,2},{7,3},{8,12},{9,13},{10,... | collective-permute-start | bytes 786440 | tf_op jit(solution)/shard_map/ppermute | solution.py:309
  63.8 0.8 collective-permute-start.15
  64.6 5.8 %shard_map.128 = (bf16[128,2048]{1,0:T(8,128)(2,1)S(1)}, bf16[128,2048]{1,0:T(8,128)(2,1)S(1)}) custom-call(s32[1]{0:T(128)} %bitcast.me_ref, s32[64]{0:T(128)S(1)} %copy-done.5, bf16[128,2048]{1,0:T(8,128)(2,1)S(1)} %collective-permute-done.refs_0_, bf16[128,2048]{1,0:T(8,128)(2,1)S(1)} %collective-permute-done.1.refs_1_, f32[128,128]{1,0:T(8,128)S(1)} %bitcast.21, ...), custom_call_target="tpu_custom_call" | custom-call | flops 4429185024 | bytes 17301504 | tf_op jit(solution)/shard_map/pallas_call | solution.py:164
  70.5 0.0 collective-permute-done.14
  70.5 0.0 collective-permute-done.15
  70.5 0.1 add_convert_fusion
  70.6 1.5 %collective-permute-start.17 = (bf16[64,2048]{1,0:T(8,128)(2,1)S(1)}, bf16[64,2048]{1,0:T(8,128)(2,1)S(1)}, u32[]{:S(2)}, u32[]{:S(2)}) collective-permute-start(bf16[64,2048]{1,0:T(8,128)(2,1)S(1)} %add_convert_fusion), channel_id=1, source_target_pairs={{4,0},{5,1},{0,2},{1,3},{8,4},{9,5},{2,6},{3,7},{12,8},{13,9},{6,1... | collective-permute-start | bytes 786440 | tf_op jit(solution)/shard_map/ppermute | solution.py:309
  72.1 0.1 add_convert_fusion.1
  72.2 0.0 copy-start.1
  72.2 0.0 copy-start.6
  72.2 0.0 copy-start.8
  72.2 0.6 collective-permute-start.16
  72.8 4.2 %collective-permute-done.17.refs_4_ = bf16[64,2048]{1,0:T(8,128)(2,1)S(1)} collective-permute-done((bf16[64,2048]{1,0:T(8,128)(2,1)S(1)}, bf16[64,2048]{1,0:T(8,128)(2,1)S(1)}, u32[]{:S(2)}, u32[]{:S(2)}) %collective-permute-start.17) | collective-permute-done | bytes 262176 | tf_op jit(solution)/shard_map/ppermute | solution.py:309
  77.0 1.6 %collective-permute-done.16.refs_3_ = bf16[64,2048]{1,0:T(8,128)(2,1)S(1)} collective-permute-done((bf16[64,2048]{1,0:T(8,128)(2,1)S(1)}, bf16[64,2048]{1,0:T(8,128)(2,1)S(1)}, u32[]{:S(2)}, u32[]{:S(2)}) %collective-permute-start.16) | collective-permute-done | bytes 262176 | tf_op jit(solution)/shard_map/ppermute | solution.py:309
  78.6 1.1 %shard_map.129 = (bf16[128,2048]{1,0:T(8,128)(2,1)}, bf16[128,2048]{1,0:T(8,128)(2,1)}) custom-call(bf16[128,2048]{1,0:T(8,128)(2,1)S(1)} %get-tuple-element.107.refs_0_, bf16[128,2048]{1,0:T(8,128)(2,1)S(1)} %get-tuple-element.108.refs_1_, bf16[64,2048]{1,0:T(8,128)(2,1)S(1)} %collective-permute-done.12.refs_2_, ...), custom_call_target="tpu_custom_call" | custom-call | tf_op jit(solution)/shard_map/pallas_call | solution.py:254
  79.8 0.6 collective-permute-start.18
  80.4 1.4 %collective-permute-start.19 = (bf16[128,2048]{1,0:T(8,128)(2,1)}, bf16[128,2048]{1,0:T(8,128)(2,1)S(1)}, u32[]{:S(2)}, u32[]{:S(2)}) collective-permute-start(bf16[128,2048]{1,0:T(8,128)(2,1)} %get-tuple-element.116), channel_id=1, source_target_pairs={{4,0},{5,1},{0,2},{1,3},{8,4},{9,5},{2,6},{3,7},{12,8},{13,9},{6,1... | collective-permute-start | bytes 1572872 | tf_op jit(solution)/shard_map/ppermute | solution.py:309
  81.8 0.9 copy.15
  82.7 3.9 %all-to-all-start.1 = ((bf16[8,2,8,2048]{3,2,1,0:T(8,128)(2,1)}), bf16[8,2,8,2048]{3,2,1,0:T(8,128)(2,1)S(1)}, u32[]{:S(2)}, u32[]{:S(2)}) async-start(bf16[8,2,8,2048]{3,2,1,0:T(8,128)(2,1)} %copy.15), calls=%async_computation.1 | async-start | bytes 1048576 | tf_op jit(solution)/shard_map/all_to_all | solution.py:329
  86.6 9.0 %collective-permute-done.18.refs_2_ = bf16[128,2048]{1,0:T(8,128)(2,1)S(1)} collective-permute-done((bf16[128,2048]{1,0:T(8,128)(2,1)}, bf16[128,2048]{1,0:T(8,128)(2,1)S(1)}, u32[]{:S(2)}, u32[]{:S(2)}) %collective-permute-start.18) | collective-permute-done | bytes 524320 | tf_op jit(solution)/shard_map/ppermute | solution.py:309
  95.6 2.3 %collective-permute-done.19.refs_3_ = bf16[128,2048]{1,0:T(8,128)(2,1)S(1)} collective-permute-done((bf16[128,2048]{1,0:T(8,128)(2,1)}, bf16[128,2048]{1,0:T(8,128)(2,1)S(1)}, u32[]{:S(2)}, u32[]{:S(2)}) %collective-permute-start.19) | collective-permute-done | bytes 524320 | tf_op jit(solution)/shard_map/ppermute | solution.py:309
  97.9 1.1 shard_map.130
  99.0 0.9 collective-permute-start.20
  99.9 1.2 %collective-permute-start.21 = (bf16[128,2048]{1,0:T(8,128)(2,1)}, bf16[128,2048]{1,0:T(8,128)(2,1)S(1)}, u32[]{:S(2)}, u32[]{:S(2)}) collective-permute-start(bf16[128,2048]{1,0:T(8,128)(2,1)} %get-tuple-element.120), channel_id=1, source_target_pairs={{4,0},{5,1},{0,2},{1,3},{8,4},{9,5},{2,6},{3,7},{12,8},{13,9},{6,1... | collective-permute-start | bytes 1572872 | tf_op jit(solution)/shard_map/ppermute | solution.py:309
  101.0 5.6 %all-to-all-done.1 = bf16[8,2,8,2048]{3,2,1,0:T(8,128)(2,1)S(1)} async-done(((bf16[8,2,8,2048]{3,2,1,0:T(8,128)(2,1)}), bf16[8,2,8,2048]{3,2,1,0:T(8,128)(2,1)S(1)}, u32[]{:S(2)}, u32[]{:S(2)}) %all-to-all-start.1) | async-done | bytes 524320 | tf_op jit(solution)/shard_map/all_to_all | solution.py:329
  106.6 1.2 %shard_map.132 = bf16[128,2048]{1,0:T(8,128)(2,1)} custom-call(bf16[128,2048]{1,0:T(8,128)(2,1)S(1)} %bitcast.17, s32[16,16]{1,0:T(8,128)S(1)} %copy-done.6, s32[1,16]{1,0:T(1,128)S(1)} %bitcast.24, s32[1]{0:T(128)} %bitcast.me_ref, bf16[128,2048]{1,0:T(8,128)(2,1)S(1)} %copy-done.1), custom_call_target="tpu_custom_call" | custom-call | tf_op jit(solution)/shard_map/pallas_call | solution.py:207
  107.8 0.6 collective-permute-done.20.up_ref
  108.4 2.0 %collective-permute-done.21.down_ref = bf16[128,2048]{1,0:T(8,128)(2,1)S(1)} collective-permute-done((bf16[128,2048]{1,0:T(8,128)(2,1)}, bf16[128,2048]{1,0:T(8,128)(2,1)S(1)}, u32[]{:S(2)}, u32[]{:S(2)}) %collective-permute-start.21) | collective-permute-done | bytes 524320 | tf_op jit(solution)/shard_map/ppermute | solution.py:309
  110.4 2.0 %shard_map.131 = bf16[128,2048]{1,0:T(8,128)(2,1)} custom-call(bf16[64,2048]{1,0:T(8,128)(2,1)} %copy-done.2, bf16[64,2048]{1,0:T(8,128)(2,1)} %copy-done.3, bf16[128,2048]{1,0:T(8,128)(2,1)S(1)} %collective-permute-done.20.up_ref, bf16[128,2048]{1,0:T(8,128)(2,1)S(1)} %collective-permute-done.21.down_ref), custom_call_target="tpu_custom_call" | custom-call | tf_op jit(solution)/shard_map/pallas_call | solution.py:273
  (20 shorter events, 0.0 us)
Async XLA Ops:
  0.6 5.8 %collective-permute-start.2 = (bf16[704,2048]{1,0:T(8,128)(2,1)}, bf16[704,2048]{1,0:T(8,128)(2,1)}, u32[]{:S(2)}, u32[]{:S(2)}) collective-permute-start(bf16[704,2048]{1,0:T(8,128)(2,1)} %bitcast.27), channel_id=1, source_target_pairs={{0,1},{1,0},{2,3},{3,2},{4,5},{5,4},{6,7},{7,6},{8,9},{9,8},{10,11... | collective-permute-start | bytes 8650760 | tf_op jit(solution)/shard_map/ppermute | solution.py:309
  1.1 19.4 %collective-permute-start.8 = (bf16[704,2048]{1,0:T(8,128)(2,1)}, bf16[704,2048]{1,0:T(8,128)(2,1)}, u32[]{:S(2)}, u32[]{:S(2)}) collective-permute-start(bf16[704,2048]{1,0:T(8,128)(2,1)} %bitcast.25), channel_id=1, source_target_pairs={{0,1},{1,0},{2,3},{3,2},{4,5},{5,4},{6,7},{7,6},{8,9},{9,8},{10,11... | collective-permute-start | bytes 8650760 | tf_op jit(solution)/shard_map/ppermute | solution.py:309
  1.2 34.4 %collective-permute-start.9 = (bf16[704,2048]{1,0:T(8,128)(2,1)}, bf16[704,2048]{1,0:T(8,128)(2,1)}, u32[]{:S(2)}, u32[]{:S(2)}) collective-permute-start(bf16[704,2048]{1,0:T(8,128)(2,1)} %bitcast.29), channel_id=1, source_target_pairs={{0,1},{1,0},{2,3},{3,2},{4,5},{5,4},{6,7},{7,6},{8,9},{9,8},{10,11... | collective-permute-start | bytes 8650760 | tf_op jit(solution)/shard_map/ppermute | solution.py:309
  1.7 15.3 %collective-permute-start = (bf16[128,2048]{1,0:T(8,128)(2,1)}, bf16[128,2048]{1,0:T(8,128)(2,1)S(1)}, u32[]{:S(2)}, u32[]{:S(2)}) collective-permute-start(bf16[128,2048]{1,0:T(8,128)(2,1)} %refs_2_.1), channel_id=1, source_target_pairs={{0,4},{1,5},{2,0},{3,1},{4,8},{5,9},{6,2},{7,3},{8,12},{9,13},{10,... | collective-permute-start | bytes 1572872 | tf_op jit(solution)/shard_map/ppermute | solution.py:309
  4.3 14.2 %collective-permute-start.1 = (bf16[128,2048]{1,0:T(8,128)(2,1)}, bf16[128,2048]{1,0:T(8,128)(2,1)S(1)}, u32[]{:S(2)}, u32[]{:S(2)}) collective-permute-start(bf16[128,2048]{1,0:T(8,128)(2,1)} %refs_2_.1), channel_id=1, source_target_pairs={{4,0},{5,1},{0,2},{1,3},{8,4},{9,5},{2,6},{3,7},{12,8},{13,9},{6,1... | collective-permute-start | bytes 1572872 | tf_op jit(solution)/shard_map/ppermute | solution.py:309
  18.5 13.2 %collective-permute-start.3 = (bf16[128,2048]{1,0:T(8,128)(2,1)S(1)}, bf16[128,2048]{1,0:T(8,128)(2,1)S(1)}, u32[]{:S(2)}, u32[]{:S(2)}) collective-permute-start(bf16[128,2048]{1,0:T(8,128)(2,1)S(1)} %collective-permute-done.refs_0_), channel_id=1, source_target_pairs={{0,4},{1,5},{2,0},{3,1},{4,8},{5,9},{6,2},{7,3},{8,12},{9,13},{10,... | collective-permute-start | bytes 1572872 | tf_op jit(solution)/shard_map/ppermute | solution.py:309
  20.1 13.2 %collective-permute-start.4 = (bf16[128,2048]{1,0:T(8,128)(2,1)S(1)}, bf16[128,2048]{1,0:T(8,128)(2,1)S(1)}, u32[]{:S(2)}, u32[]{:S(2)}) collective-permute-start(bf16[128,2048]{1,0:T(8,128)(2,1)S(1)} %collective-permute-done.1.refs_1_), channel_id=1, source_target_pairs={{4,0},{5,1},{0,2},{1,3},{8,4},{9,5},{2,6},{3,7},{12,8},{13,9},{6,1... | collective-permute-start | bytes 1572872 | tf_op jit(solution)/shard_map/ppermute | solution.py:309
  20.5 7.9 %collective-permute-start.5 = (bf16[8,8,2048]{2,1,0:T(8,128)(2,1)S(1)}, bf16[8,8,2048]{2,1,0:T(8,128)(2,1)S(1)}, u32[]{:S(2)}, u32[]{:S(2)}) collective-permute-start(bf16[8,8,2048]{2,1,0:T(8,128)(2,1)S(1)} %get-tuple-element.69), channel_id=1, source_target_pairs={{0,1},{1,0},{2,3},{3,2},{4,5},{5,4},{6,7},{7,6},{8,9},{9,8},{10,11... | collective-permute-start | bytes 786440 | tf_op jit(solution)/shard_map/ppermute | solution.py:309
  20.5 0.7 copy-start.7
  23.4 12.2 %all-to-all-start = ((f32[16,8,128]{2,1,0:T(8,128)}), f32[16,8,128]{2,1,0:T(8,128)S(1)}, u32[]{:S(2)}, u32[]{:S(2)}) async-start(f32[16,8,128]{2,1,0:T(8,128)} %bitcast.10), calls=%async_computation | async-start | bytes 131072 | tf_op jit(solution)/shard_map/all_to_all | solution.py:333
  33.3 12.6 %collective-permute-start.6 = (bf16[128,2048]{1,0:T(8,128)(2,1)S(1)}, bf16[128,2048]{1,0:T(8,128)(2,1)S(1)}, u32[]{:S(2)}, u32[]{:S(2)}) collective-permute-start(bf16[128,2048]{1,0:T(8,128)(2,1)S(1)} %collective-permute-done.3.refs_0_), channel_id=1, source_target_pairs={{0,4},{1,5},{2,0},{3,1},{4,8},{5,9},{6,2},{7,3},{8,12},{9,13},{10,... | collective-permute-start | bytes 1572872 | tf_op jit(solution)/shard_map/ppermute | solution.py:309
  35.2 11.2 %collective-permute-start.7 = (bf16[128,2048]{1,0:T(8,128)(2,1)S(1)}, bf16[128,2048]{1,0:T(8,128)(2,1)S(1)}, u32[]{:S(2)}, u32[]{:S(2)}) collective-permute-start(bf16[128,2048]{1,0:T(8,128)(2,1)S(1)} %collective-permute-done.4.refs_1_), channel_id=1, source_target_pairs={{4,0},{5,1},{0,2},{1,3},{8,4},{9,5},{2,6},{3,7},{12,8},{13,9},{6,1... | collective-permute-start | bytes 1572872 | tf_op jit(solution)/shard_map/ppermute | solution.py:309
  35.6 0.7 copy-start.4
  36.3 12.3 %copy-start.5 = (s32[64]{0:T(128)S(1)}, s32[64]{0:T(128)}, u32[]{:S(2)}) copy-start(s32[64]{0:T(128)} %constant.8.clone.order_ref) | copy-start | bytes 772
  46.5 7.9 %collective-permute-start.10 = (bf16[64,2048]{1,0:T(8,128)(2,1)S(1)}, bf16[64,2048]{1,0:T(8,128)(2,1)S(1)}, u32[]{:S(2)}, u32[]{:S(2)}) collective-permute-start(bf16[64,2048]{1,0:T(8,128)(2,1)S(1)} %get-tuple-element.79), channel_id=1, source_target_pairs={{0,4},{1,5},{2,0},{3,1},{4,8},{5,9},{6,2},{7,3},{8,12},{9,13},{10,... | collective-permute-start | bytes 786440 | tf_op jit(solution)/shard_map/ppermute | solution.py:309
  47.9 6.8 %collective-permute-start.11 = (bf16[64,2048]{1,0:T(8,128)(2,1)S(1)}, bf16[64,2048]{1,0:T(8,128)(2,1)S(1)}, u32[]{:S(2)}, u32[]{:S(2)}) collective-permute-start(bf16[64,2048]{1,0:T(8,128)(2,1)S(1)} %get-tuple-element.80), channel_id=1, source_target_pairs={{4,0},{5,1},{0,2},{1,3},{8,4},{9,5},{2,6},{3,7},{12,8},{13,9},{6,1... | collective-permute-start | bytes 786440 | tf_op jit(solution)/shard_map/ppermute | solution.py:309
  48.5 8.1 %copy-start = (bf16[128,2048]{1,0:T(8,128)(2,1)S(1)}, bf16[128,2048]{1,0:T(8,128)(2,1)}, u32[]{:S(2)}) copy-start(bf16[128,2048]{1,0:T(8,128)(2,1)} %refs_2_.1) | copy-start | bytes 1572868
  54.6 7.9 %collective-permute-start.12 = (bf16[64,2048]{1,0:T(8,128)(2,1)S(1)}, bf16[64,2048]{1,0:T(8,128)(2,1)S(1)}, u32[]{:S(2)}, u32[]{:S(2)}) collective-permute-start(bf16[64,2048]{1,0:T(8,128)(2,1)S(1)} %get-tuple-element.95), channel_id=1, source_target_pairs={{0,4},{1,5},{2,0},{3,1},{4,8},{5,9},{6,2},{7,3},{8,12},{9,13},{10,... | collective-permute-start | bytes 786440 | tf_op jit(solution)/shard_map/ppermute | solution.py:309
  55.8 6.7 %collective-permute-start.13 = (bf16[64,2048]{1,0:T(8,128)(2,1)S(1)}, bf16[64,2048]{1,0:T(8,128)(2,1)S(1)}, u32[]{:S(2)}, u32[]{:S(2)}) collective-permute-start(bf16[64,2048]{1,0:T(8,128)(2,1)S(1)} %get-tuple-element.96), channel_id=1, source_target_pairs={{4,0},{5,1},{0,2},{1,3},{8,4},{9,5},{2,6},{3,7},{12,8},{13,9},{6,1... | collective-permute-start | bytes 786440 | tf_op jit(solution)/shard_map/ppermute | solution.py:309
  62.5 8.0 %copy-start.2 = (bf16[64,2048]{1,0:T(8,128)(2,1)}, bf16[64,2048]{1,0:T(8,128)(2,1)S(1)}, u32[]{:S(2)}) copy-start(bf16[64,2048]{1,0:T(8,128)(2,1)S(1)} %get-tuple-element.93.first_ref) | copy-start | bytes 786436
  62.5 8.0 %copy-start.3 = (bf16[64,2048]{1,0:T(8,128)(2,1)}, bf16[64,2048]{1,0:T(8,128)(2,1)S(1)}, u32[]{:S(2)}) copy-start(bf16[64,2048]{1,0:T(8,128)(2,1)S(1)} %get-tuple-element.94.second_ref) | copy-start | bytes 786436
  62.5 8.0 %collective-permute-start.14 = (bf16[64,2048]{1,0:T(8,128)(2,1)S(1)}, bf16[64,2048]{1,0:T(8,128)(2,1)S(1)}, u32[]{:S(2)}, u32[]{:S(2)}) collective-permute-start(bf16[64,2048]{1,0:T(8,128)(2,1)S(1)} %get-tuple-element.99), channel_id=1, source_target_pairs={{0,4},{1,5},{2,0},{3,1},{4,8},{5,9},{6,2},{7,3},{8,12},{9,13},{10,... | collective-permute-start | bytes 786440 | tf_op jit(solution)/shard_map/ppermute | solution.py:309
  63.8 6.7 %collective-permute-start.15 = (bf16[64,2048]{1,0:T(8,128)(2,1)S(1)}, bf16[64,2048]{1,0:T(8,128)(2,1)S(1)}, u32[]{:S(2)}, u32[]{:S(2)}) collective-permute-start(bf16[64,2048]{1,0:T(8,128)(2,1)S(1)} %get-tuple-element.100), channel_id=1, source_target_pairs={{4,0},{5,1},{0,2},{1,3},{8,4},{9,5},{2,6},{3,7},{12,8},{13,9},{6,1... | collective-permute-start | bytes 786440 | tf_op jit(solution)/shard_map/ppermute | solution.py:309
  70.5 11.3 %copy-start.9 = (bf16[8,2,8,2048]{3,2,0,1:T(8,128)(2,1)S(1)}, bf16[8,2,8,2048]{3,2,0,1:T(8,128)(2,1)}, u32[]{:S(2)}) copy-start(bf16[8,2,8,2048]{3,2,0,1:T(8,128)(2,1)} %pad_maximum_fusion) | copy-start | bytes 1572868
  70.6 6.4 %collective-permute-start.17 = (bf16[64,2048]{1,0:T(8,128)(2,1)S(1)}, bf16[64,2048]{1,0:T(8,128)(2,1)S(1)}, u32[]{:S(2)}, u32[]{:S(2)}) collective-permute-start(bf16[64,2048]{1,0:T(8,128)(2,1)S(1)} %add_convert_fusion), channel_id=1, source_target_pairs={{4,0},{5,1},{0,2},{1,3},{8,4},{9,5},{2,6},{3,7},{12,8},{13,9},{6,1... | collective-permute-start | bytes 786440 | tf_op jit(solution)/shard_map/ppermute | solution.py:309
  72.2 34.4 %copy-start.1 = (bf16[128,2048]{1,0:T(8,128)(2,1)S(1)}, bf16[128,2048]{1,0:T(8,128)(2,1)}, u32[]{:S(2)}) copy-start(bf16[128,2048]{1,0:T(8,128)(2,1)} %text_ref.1) | copy-start | bytes 1572868
  72.2 34.4 %copy-start.6 = (s32[16,16]{1,0:T(8,128)S(1)}, s32[16,16]{1,0:T(8,128)}, u32[]{:S(2)}) copy-start(s32[16,16]{1,0:T(8,128)} %counts_ref.1) | copy-start | bytes 3076
  72.2 34.4 %copy-start.8 = (s32[16]{0:T(128)S(1)}, s32[16]{0:T(128)}, u32[]{:S(2)}) copy-start(s32[16]{0:T(128)} %param.19) | copy-start | bytes 196
  72.2 6.4 %collective-permute-start.16 = (bf16[64,2048]{1,0:T(8,128)(2,1)S(1)}, bf16[64,2048]{1,0:T(8,128)(2,1)S(1)}, u32[]{:S(2)}, u32[]{:S(2)}) collective-permute-start(bf16[64,2048]{1,0:T(8,128)(2,1)S(1)} %add_convert_fusion.1), channel_id=1, source_target_pairs={{0,4},{1,5},{2,0},{3,1},{4,8},{5,9},{6,2},{7,3},{8,12},{9,13},{10,... | collective-permute-start | bytes 786440 | tf_op jit(solution)/shard_map/ppermute | solution.py:309
  79.8 15.8 %collective-permute-start.18 = (bf16[128,2048]{1,0:T(8,128)(2,1)}, bf16[128,2048]{1,0:T(8,128)(2,1)S(1)}, u32[]{:S(2)}, u32[]{:S(2)}) collective-permute-start(bf16[128,2048]{1,0:T(8,128)(2,1)} %get-tuple-element.115), channel_id=1, source_target_pairs={{0,4},{1,5},{2,0},{3,1},{4,8},{5,9},{6,2},{7,3},{8,12},{9,13},{10,... | collective-permute-start | bytes 1572872 | tf_op jit(solution)/shard_map/ppermute | solution.py:309
  80.4 17.5 %collective-permute-start.19 = (bf16[128,2048]{1,0:T(8,128)(2,1)}, bf16[128,2048]{1,0:T(8,128)(2,1)S(1)}, u32[]{:S(2)}, u32[]{:S(2)}) collective-permute-start(bf16[128,2048]{1,0:T(8,128)(2,1)} %get-tuple-element.116), channel_id=1, source_target_pairs={{4,0},{5,1},{0,2},{1,3},{8,4},{9,5},{2,6},{3,7},{12,8},{13,9},{6,1... | collective-permute-start | bytes 1572872 | tf_op jit(solution)/shard_map/ppermute | solution.py:309
  82.7 23.9 %all-to-all-start.1 = ((bf16[8,2,8,2048]{3,2,1,0:T(8,128)(2,1)}), bf16[8,2,8,2048]{3,2,1,0:T(8,128)(2,1)S(1)}, u32[]{:S(2)}, u32[]{:S(2)}) async-start(bf16[8,2,8,2048]{3,2,1,0:T(8,128)(2,1)} %copy.15), calls=%async_computation.1 | async-start | bytes 1048576 | tf_op jit(solution)/shard_map/all_to_all | solution.py:329
  99.0 9.4 %collective-permute-start.20 = (bf16[128,2048]{1,0:T(8,128)(2,1)}, bf16[128,2048]{1,0:T(8,128)(2,1)S(1)}, u32[]{:S(2)}, u32[]{:S(2)}) collective-permute-start(bf16[128,2048]{1,0:T(8,128)(2,1)} %get-tuple-element.119), channel_id=1, source_target_pairs={{0,4},{1,5},{2,0},{3,1},{4,8},{5,9},{6,2},{7,3},{8,12},{9,13},{10,... | collective-permute-start | bytes 1572872 | tf_op jit(solution)/shard_map/ppermute | solution.py:309
  99.9 10.6 %collective-permute-start.21 = (bf16[128,2048]{1,0:T(8,128)(2,1)}, bf16[128,2048]{1,0:T(8,128)(2,1)S(1)}, u32[]{:S(2)}, u32[]{:S(2)}) collective-permute-start(bf16[128,2048]{1,0:T(8,128)(2,1)} %get-tuple-element.120), channel_id=1, source_target_pairs={{4,0},{5,1},{0,2},{1,3},{8,4},{9,5},{2,6},{3,7},{12,8},{13,9},{6,1... | collective-permute-start | bytes 1572872 | tf_op jit(solution)/shard_map/ppermute | solution.py:309

commit v6 on v5

--- a/solution.py
+++ b/solution.py
@@ -92,6 +92,24 @@
         scratch_shapes=[pltpu.SemaphoreType.DMA((devices // 2, 2))],
         compiler_params=pltpu.CompilerParams(vmem_limit_bytes=4 * 2**20),
     )(me[None], span_of, in_hbm(image_rows))
+
+
+def pair_kernel(kept_ref, other_ref, out_ref):
+    for c in range(out_ref.shape[0]):
+        out_ref[c, 0] = kept_ref[c]
+        out_ref[c, 1] = other_ref[c]
+
+
+def pair(kept, other):
+    chips, slots, width = kept.shape
+    vmem = pl.BlockSpec(memory_space=pltpu.VMEM)
+    return pl.pallas_call(
+        pair_kernel,
+        out_shape=jax.ShapeDtypeStruct((chips, 2, slots, width), kept.dtype),
+        in_specs=[vmem] * 2,
+        out_specs=vmem,
+        compiler_params=pltpu.CompilerParams(vmem_limit_bytes=8 * 2**20),
+    )(kept, other)
 
 
 def ffn_kernel(count, results, sizes, offsets, chips, holds, me_ref, order_ref, *refs):
@@ -180,7 +198,10 @@
     )(me[None], order, *shards, table, *weights)
 
 
-def place_kernel(slots, arrived_ref, counts_ref, owner_ref, me_ref, text_ref, out_ref):
+def place_kernel(slots, arrived_ref, counts_ref, owner_ref, me_ref, text_ref, first_ref, second_ref, out_ref, near_ref):
+    half = first_ref.shape[0]
+    near_ref[:half, :] = first_ref[...]
+    near_ref[half:, :] = second_ref[...]
     rows = text_ref.shape[0]
     devices = counts_ref.shape[0]
     held = arrived_ref.shape[0]
@@ -202,15 +223,18 @@
     out_ref[...] = jnp.where(position < total, image, text_ref[...])
 
 
-def place_images(arrived, counts, owner, me, text_block, slots):
+def place_images(arrived, counts, owner, me, text_block, slots, first, second):
     vmem = pl.BlockSpec(memory_space=pltpu.VMEM)
     return pl.pallas_call(
         functools.partial(place_kernel, slots),
-        out_shape=jax.ShapeDtypeStruct(text_block.shape, text_block.dtype),
-        in_specs=[vmem, vmem, vmem, pl.BlockSpec(memory_space=pltpu.SMEM), vmem],
-        out_specs=vmem,
+        out_shape=[
+            jax.ShapeDtypeStruct(text_block.shape, text_block.dtype),
+            pltpu.VMEM(text_block.shape, first.dtype),
+        ],
+        in_specs=[vmem, vmem, vmem, pl.BlockSpec(memory_space=pltpu.SMEM), vmem, vmem, vmem],
+        out_specs=[vmem] * 2,
         compiler_params=pltpu.CompilerParams(vmem_limit_bytes=8 * 2**20),
-    )(arrived, counts, owner[None, :], me[None], text_block)
+    )(arrived, counts, owner[None, :], me[None], text_block, first, second)
 
 
 def cut_kernel(below_ref, above_ref, first_ref, second_ref, sems):
@@ -260,23 +284,20 @@
     )(above, below, *up_parts, *down_parts)
 
 
-def finish_kernel(first_ref, second_ref, up_ref, down_ref, out_ref):
-    half = first_ref.shape[0]
-    for i, mine in enumerate((first_ref, second_ref)):
-        part = pl.ds(i * half, half)
-        total = mine[...].astype(jnp.float32) + up_ref[part, :].astype(jnp.float32)
-        out_ref[part, :] = (total + down_ref[part, :].astype(jnp.float32)).astype(out_ref.dtype)
-
-
-def finish(first, second, came_up, came_down):
+def finish_kernel(near_ref, up_ref, down_ref, out_ref):
+    total = near_ref[...].astype(jnp.float32) + up_ref[...].astype(jnp.float32)
+    out_ref[...] = (total + down_ref[...].astype(jnp.float32)).astype(out_ref.dtype)
+
+
+def finish(near, came_up, came_down):
     vmem = pl.BlockSpec(memory_space=pltpu.VMEM)
     return pl.pallas_call(
         finish_kernel,
-        out_shape=jax.ShapeDtypeStruct(came_up.shape, came_up.dtype),
-        in_specs=[vmem] * 4,
+        out_shape=jax.ShapeDtypeStruct(near.shape, near.dtype),
+        in_specs=[vmem] * 3,
         out_specs=vmem,
         compiler_params=pltpu.CompilerParams(vmem_limit_bytes=8 * 2**20),
-    )(first, second, came_up, came_down)
+    )(near, came_up, came_down)
 
 
 def tie(*arrays):
@@ -353,7 +374,7 @@
         else:
             if s == 1:
                 below[s], above[s], keep, give = tie(below[s], above[s], keep, give)
-                image_send = jnp.stack([keep, send(give, sibling)], axis=1)
+                image_send = pair(keep, send(give, sibling))
             else:
                 below[s], above[s], image_send = tie(below[s], above[s], image_send)
 
@@ -387,12 +408,11 @@
         going_up, going_down = tie(send(going_up, up), send(going_down, down))
         if s > 1:
             going_up, going_down = merge(from_above[s - 1], from_below[s - 1], [going_up], [going_down])
-    moe_out = finish(in_hbm(result_first), in_hbm(result_second), going_up, going_down)
-
     arrived = arrived.reshape(devices * slots, width)
-    next_span = place_images(
-        arrived, image_counts, span_owner, me, text_rows, slots
+    next_span, near = place_images(
+        arrived, image_counts, span_owner, me, text_rows, slots, result_first, result_second
     )
+    moe_out = finish(near, going_up, going_down)
     return (moe_out, next_span)
 
 

time: 113 us -> 113 us (level)
    unnamed x20 -> x18, local copies, waits for them, and re-layouts: 1.38 us -> 2.32 us
    pallas_call x2 -> x3, Pallas kernels: 3.17 us -> 2.97 us  [the longest x1 1.16 us: place_images(): pl.pallas_call(functools.partial(place_kernel, slots), out_shape=[jax.Sha...]
  transfers between devices with their start and end apart: 24 -> 24, of which waited for: 15 -> 14; matrix products, arithmetic and copies ran while one was open for 2% -> 1% of each run, Pallas kernels for 30% -> 31%
where the time goes in v6:
time: 113 us; the launch traced here: 112 us
  waiting for transfers between devices  42.8 us (38%)
  Pallas kernels  36.4 us (32%)
  starting transfers between devices  29.1 us (26%)
  local copies, waits for them, and re-layouts  2.32 us (2%)
    ppermute x22, waiting for transfers between devices, send(): return lax.ppermute(x, 'expert', pairs)  36.5 us
    pallas_call x4, Pallas kernels, ffn(): pl.pallas_call(functools.partial(ffn_kernel, len(shards), results, sizes,...  27.3 us
    ppermute x22, starting transfers between devices, send(): return lax.ppermute(x, 'expert', pairs)  20.1 us
    all_to_all x1, waiting for transfers between devices, exchange(): lax.all_to_all(x, 'expert', split_axis=0, concat_axis=0, tiled=True, axis...  5.98 us
    all_to_all x1, starting transfers between devices, local(): lax.all_to_all(table.reshape(devices, 8, -1), 'expert', split_axis=0, con...  5.05 us
    all_to_all x1, starting transfers between devices, exchange(): lax.all_to_all(x, 'expert', split_axis=0, concat_axis=0, tiled=True, axis...  3.91 us
    unnamed x18, local copies, waits for them, and re-layouts  2.32 us
    pallas_call x2, Pallas kernels, merge(): pl.pallas_call(functools.partial(merge_kernel, parts), out_shape=[jax.Sha...  2.28 us
  transfers between devices with their start and end apart: 24, of which 14 were waited for; matrix products, arithmetic and copies ran while one was open for 1% of the time, Pallas kernels for 31%

profile of v6, /device:TPU:0, one launch (start us, length us, event | category | flops | bytes accessed | tf_op | source)
XLA Modules:
  0.0 112.3 jit_solution(9279397146719246227)
XLA Ops:
  0.6 0.5 collective-permute-start.3
  1.1 0.1 collective-permute-start
  1.2 0.4 collective-permute-start.9
  1.7 2.7 %collective-permute-start.1 = (bf16[128,2048]{1,0:T(8,128)(2,1)}, bf16[128,2048]{1,0:T(8,128)(2,1)S(1)}, u32[]{:S(2)}, u32[]{:S(2)}) collective-permute-start(bf16[128,2048]{1,0:T(8,128)(2,1)} %refs_2_.1), channel_id=1, source_target_pairs={{0,4},{1,5},{2,0},{3,1},{4,8},{5,9},{6,2},{7,3},{8,12},{9,13},{10,... | collective-permute-start | bytes 1572872 | tf_op jit(solution)/shard_map/ppermute | solution.py:330
  4.3 0.7 select_reduce_fusion.span_of_ref
  5.1 1.3 %collective-permute-done.3.refs_7_ = bf16[704,2048]{1,0:T(8,128)(2,1)} collective-permute-done((bf16[704,2048]{1,0:T(8,128)(2,1)}, bf16[704,2048]{1,0:T(8,128)(2,1)}, u32[]{:S(2)}, u32[]{:S(2)}) %collective-permute-start.3) | collective-permute-done | bytes 2883616 | tf_op jit(solution)/shard_map/ppermute | solution.py:330
  6.4 1.7 %shard_map.123 = (bf16[8,8,2048]{2,1,0:T(8,128)(2,1)S(1)}, bf16[8,8,2048]{2,1,0:T(8,128)(2,1)S(1)}) custom-call(s32[1]{0:T(128)} %bitcast.6.me_ref, s32[16]{0:T(128)S(1)} %select_reduce_fusion.span_of_ref, bf16[16,8,2048]{2,1,0:T(8,128)(2,1)} %bitcast.28), custom_call_target="tpu_custom_call" | custom-call | tf_op jit(solution)/shard_map/pallas_call | solution.py:87
  8.1 8.9 %collective-permute-done.1.refs_0_ = bf16[128,2048]{1,0:T(8,128)(2,1)S(1)} collective-permute-done((bf16[128,2048]{1,0:T(8,128)(2,1)}, bf16[128,2048]{1,0:T(8,128)(2,1)S(1)}, u32[]{:S(2)}, u32[]{:S(2)}) %collective-permute-start.1) | collective-permute-done | bytes 524320 | tf_op jit(solution)/shard_map/ppermute | solution.py:330
  17.0 1.5 %collective-permute-done.2.refs_1_ = bf16[128,2048]{1,0:T(8,128)(2,1)S(1)} collective-permute-done((bf16[128,2048]{1,0:T(8,128)(2,1)}, bf16[128,2048]{1,0:T(8,128)(2,1)S(1)}, u32[]{:S(2)}, u32[]{:S(2)}) %collective-permute-start.2) | collective-permute-done | bytes 524320 | tf_op jit(solution)/shard_map/ppermute | solution.py:330
  18.5 1.6 %collective-permute-start.4 = (bf16[128,2048]{1,0:T(8,128)(2,1)S(1)}, bf16[128,2048]{1,0:T(8,128)(2,1)S(1)}, u32[]{:S(2)}, u32[]{:S(2)}) collective-permute-start(bf16[128,2048]{1,0:T(8,128)(2,1)S(1)} %collective-permute-done.1.refs_0_), channel_id=1, source_target_pairs={{0,4},{1,5},{2,0},{3,1},{4,8},{5,9},{6,2},{7,3},{8,12},{9,13},{10,... | collective-permute-start | bytes 1572872 | tf_op jit(solution)/shard_map/ppermute | solution.py:330
  20.1 0.4 collective-permute-start.5
  20.5 0.0 collective-permute-start.6
  20.5 0.0 collective-permute-done.refs_6_
  20.6 0.7 copy-done.7
  21.2 2.2 %shard_map.122 = f32[128,128]{1,0:T(8,128)} custom-call(s32[6,128]{1,0:T(8,128)S(1)} %bitcast.20, bf16[16,2048]{1,0:T(8,128)(2,1)} %bitcast.29, bf16[128,2048]{1,0:T(8,128)(2,1)} %refs_2_.1), custom_call_target="tpu_custom_call" | custom-call | tf_op jit(solution)/shard_map/pallas_call | solution.py:58
  23.4 5.0 %all-to-all-start = ((f32[16,8,128]{2,1,0:T(8,128)}), f32[16,8,128]{2,1,0:T(8,128)S(1)}, u32[]{:S(2)}, u32[]{:S(2)}) async-start(f32[16,8,128]{2,1,0:T(8,128)} %bitcast.4), calls=%async_computation | async-start | bytes 131072 | tf_op jit(solution)/shard_map/all_to_all | solution.py:354
  28.5 0.0 collective-permute-done.6.other_ref
  28.5 0.8 shard_map.124
  29.3 2.4 %collective-permute-done.4.refs_0_ = bf16[128,2048]{1,0:T(8,128)(2,1)S(1)} collective-permute-done((bf16[128,2048]{1,0:T(8,128)(2,1)S(1)}, bf16[128,2048]{1,0:T(8,128)(2,1)S(1)}, u32[]{:S(2)}, u32[]{:S(2)}) %collective-permute-start.4) | collective-permute-done | bytes 524320 | tf_op jit(solution)/shard_map/ppermute | solution.py:330
  31.7 1.6 %collective-permute-done.5.refs_1_ = bf16[128,2048]{1,0:T(8,128)(2,1)S(1)} collective-permute-done((bf16[128,2048]{1,0:T(8,128)(2,1)S(1)}, bf16[128,2048]{1,0:T(8,128)(2,1)S(1)}, u32[]{:S(2)}, u32[]{:S(2)}) %collective-permute-start.5) | collective-permute-done | bytes 524320 | tf_op jit(solution)/shard_map/ppermute | solution.py:330
  33.3 1.9 %collective-permute-start.7 = (bf16[128,2048]{1,0:T(8,128)(2,1)S(1)}, bf16[128,2048]{1,0:T(8,128)(2,1)S(1)}, u32[]{:S(2)}, u32[]{:S(2)}) collective-permute-start(bf16[128,2048]{1,0:T(8,128)(2,1)S(1)} %collective-permute-done.4.refs_0_), channel_id=1, source_target_pairs={{0,4},{1,5},{2,0},{3,1},{4,8},{5,9},{6,2},{7,3},{8,12},{9,13},{10,... | collective-permute-start | bytes 1572872 | tf_op jit(solution)/shard_map/ppermute | solution.py:330
  35.2 0.1 collective-permute-start.8
  35.3 0.3 all-to-all-done
  35.6 0.0 collective-permute-done.9.refs_8_
  35.6 0.7 copy-done.4
  36.3 9.7 %shard_map.125 = (bf16[128,2048]{1,0:T(8,128)(2,1)S(1)}, bf16[128,2048]{1,0:T(8,128)(2,1)S(1)}, bf16[704,2048]{1,0:T(8,128)(2,1)S(1)}, bf16[704,2048]{1,0:T(8,12...) custom-call(s32[1]{0:T(128)} %bitcast.6.me_ref, ...), custom_call_target="tpu_custom_call" | custom-call | flops 4429185024 | bytes 17301504 | tf_op jit(solution)/shard_map/pallas_call | solution.py:182
  45.9 0.5 collective-permute-done.8.above_ref.refs_1_
  46.4 0.1 shard_map.126
  46.5 1.4 %collective-permute-start.10 = (bf16[64,2048]{1,0:T(8,128)(2,1)S(1)}, bf16[64,2048]{1,0:T(8,128)(2,1)S(1)}, u32[]{:S(2)}, u32[]{:S(2)}) collective-permute-start(bf16[64,2048]{1,0:T(8,128)(2,1)S(1)} %get-tuple-element.82), channel_id=1, source_target_pairs={{0,4},{1,5},{2,0},{3,1},{4,8},{5,9},{6,2},{7,3},{8,12},{9,13},{10,... | collective-permute-start | bytes 786440 | tf_op jit(solution)/shard_map/ppermute | solution.py:330
  47.9 0.7 collective-permute-start.11
  48.5 5.9 %shard_map.127 = (bf16[64,2048]{1,0:T(8,128)(2,1)S(1)}, bf16[64,2048]{1,0:T(8,128)(2,1)S(1)}, bf16[64,2048]{1,0:T(8,128)(2,1)S(1)}, bf16[64,2048]{1,0:T(8,128)(2,1)S(1)}) custom-call(s32[1]{0:T(128)} %bitcast.6.me_ref, s32[64]{0:T(128)S(1)} %copy-done.5, bf16[128,2048]{1,0:T(8,128)(2,1)S(1)} %collective-permute-done.7.below_ref.refs_0_, ...), custom_call_target="tpu_custom_call" | custom-call | flops 4429185024 | bytes 17301504 | tf_op jit(solution)/shard_map/pallas_call | solution.py:182
  54.4 0.2 collective-permute-done.11.refs_1_
  54.7 1.2 %collective-permute-start.12 = (bf16[64,2048]{1,0:T(8,128)(2,1)S(1)}, bf16[64,2048]{1,0:T(8,128)(2,1)S(1)}, u32[]{:S(2)}, u32[]{:S(2)}) collective-permute-start(bf16[64,2048]{1,0:T(8,128)(2,1)S(1)} %get-tuple-element.99), channel_id=1, source_target_pairs={{0,4},{1,5},{2,0},{3,1},{4,8},{5,9},{6,2},{7,3},{8,12},{9,13},{10,... | collective-permute-start | bytes 786440 | tf_op jit(solution)/shard_map/ppermute | solution.py:330
  55.8 0.9 collective-permute-start.13
  56.7 5.9 %shard_map.128 = (bf16[64,2048]{1,0:T(8,128)(2,1)S(1)}, bf16[64,2048]{1,0:T(8,128)(2,1)S(1)}, bf16[64,2048]{1,0:T(8,128)(2,1)S(1)}, bf16[64,2048]{1,0:T(8,128)(2,1)S(1)}) custom-call(s32[1]{0:T(128)} %bitcast.6.me_ref, s32[64]{0:T(128)S(1)} %copy-done.5, bf16[64,2048]{1,0:T(8,128)(2,1)S(1)} %collective-permute-done.10.refs_0_, ...), custom_call_target="tpu_custom_call" | custom-call | flops 4429185024 | bytes 17301504 | tf_op jit(solution)/shard_map/pallas_call | solution.py:182
  62.6 0.0 collective-permute-done.13.refs_5_
  62.6 1.2 %collective-permute-start.14 = (bf16[64,2048]{1,0:T(8,128)(2,1)S(1)}, bf16[64,2048]{1,0:T(8,128)(2,1)S(1)}, u32[]{:S(2)}, u32[]{:S(2)}) collective-permute-start(bf16[64,2048]{1,0:T(8,128)(2,1)S(1)} %get-tuple-element.103), channel_id=1, source_target_pairs={{0,4},{1,5},{2,0},{3,1},{4,8},{5,9},{6,2},{7,3},{8,12},{9,13},{10,... | collective-permute-start | bytes 786440 | tf_op jit(solution)/shard_map/ppermute | solution.py:330
  63.8 0.9 collective-permute-start.15
  64.7 5.9 %shard_map.130 = (bf16[128,2048]{1,0:T(8,128)(2,1)S(1)}, bf16[128,2048]{1,0:T(8,128)(2,1)S(1)}) custom-call(s32[1]{0:T(128)} %bitcast.6.me_ref, s32[64]{0:T(128)S(1)} %copy-done.5, bf16[128,2048]{1,0:T(8,128)(2,1)S(1)} %collective-permute-done.1.refs_0_, bf16[128,2048]{1,0:T(8,128)(2,1)S(1)} %collective-permute-done.2.refs_1_, f32[128,128]{1,0:T(8,128)S(1)} %bitcast.19, ...), custom_call_target="tpu_custom_call" | custom-call | flops 4429185024 | bytes 17301504 | tf_op jit(solution)/shard_map/pallas_call | solution.py:182
  70.6 0.0 collective-permute-done.15
  70.6 0.1 add_convert_fusion
  70.7 0.0 copy-start.1
  70.7 0.0 copy-start.6
  70.7 0.0 copy-start.8
  70.7 1.5 %collective-permute-start.17 = (bf16[64,2048]{1,0:T(8,128)(2,1)S(1)}, bf16[64,2048]{1,0:T(8,128)(2,1)S(1)}, u32[]{:S(2)}, u32[]{:S(2)}) collective-permute-start(bf16[64,2048]{1,0:T(8,128)(2,1)S(1)} %add_convert_fusion), channel_id=1, source_target_pairs={{4,0},{5,1},{0,2},{1,3},{8,4},{9,5},{2,6},{3,7},{12,8},{13,9},{6,1... | collective-permute-start | bytes 786440 | tf_op jit(solution)/shard_map/ppermute | solution.py:330
  72.2 0.1 add_convert_fusion.1
  72.3 0.6 collective-permute-start.16
  72.9 4.2 %collective-permute-done.17.refs_4_ = bf16[64,2048]{1,0:T(8,128)(2,1)S(1)} collective-permute-done((bf16[64,2048]{1,0:T(8,128)(2,1)S(1)}, bf16[64,2048]{1,0:T(8,128)(2,1)S(1)}, u32[]{:S(2)}, u32[]{:S(2)}) %collective-permute-start.17) | collective-permute-done | bytes 262176 | tf_op jit(solution)/shard_map/ppermute | solution.py:330
  77.1 1.6 %collective-permute-done.16.refs_3_ = bf16[64,2048]{1,0:T(8,128)(2,1)S(1)} collective-permute-done((bf16[64,2048]{1,0:T(8,128)(2,1)S(1)}, bf16[64,2048]{1,0:T(8,128)(2,1)S(1)}, u32[]{:S(2)}, u32[]{:S(2)}) %collective-permute-start.16) | collective-permute-done | bytes 262176 | tf_op jit(solution)/shard_map/ppermute | solution.py:330
  78.7 1.1 shard_map.131
  79.9 0.6 collective-permute-start.18
  80.4 1.5 %collective-permute-start.19 = (bf16[128,2048]{1,0:T(8,128)(2,1)}, bf16[128,2048]{1,0:T(8,128)(2,1)S(1)}, u32[]{:S(2)}, u32[]{:S(2)}) collective-permute-start(bf16[128,2048]{1,0:T(8,128)(2,1)} %get-tuple-element.120), channel_id=1, source_target_pairs={{4,0},{5,1},{0,2},{1,3},{8,4},{9,5},{2,6},{3,7},{12,8},{13,9},{6,1... | collective-permute-start | bytes 1572872 | tf_op jit(solution)/shard_map/ppermute | solution.py:330
  81.9 3.9 %all-to-all-start.1 = ((bf16[8,2,8,2048]{3,2,1,0:T(8,128)(2,1)}), bf16[8,2,8,2048]{3,2,1,0:T(8,128)(2,1)S(1)}, u32[]{:S(2)}, u32[]{:S(2)}) async-start(bf16[8,2,8,2048]{3,2,1,0:T(8,128)(2,1)} %shard_map.124), calls=%async_computation.1 | async-start | bytes 1048576 | tf_op jit(solution)/shard_map/all_to_all | solution.py:350
  85.8 9.7 %collective-permute-done.18.refs_2_ = bf16[128,2048]{1,0:T(8,128)(2,1)S(1)} collective-permute-done((bf16[128,2048]{1,0:T(8,128)(2,1)}, bf16[128,2048]{1,0:T(8,128)(2,1)S(1)}, u32[]{:S(2)}, u32[]{:S(2)}) %collective-permute-start.18) | collective-permute-done | bytes 524320 | tf_op jit(solution)/shard_map/ppermute | solution.py:330
  95.5 2.8 %collective-permute-done.19.refs_3_ = bf16[128,2048]{1,0:T(8,128)(2,1)S(1)} collective-permute-done((bf16[128,2048]{1,0:T(8,128)(2,1)}, bf16[128,2048]{1,0:T(8,128)(2,1)S(1)}, u32[]{:S(2)}, u32[]{:S(2)}) %collective-permute-start.19) | collective-permute-done | bytes 524320 | tf_op jit(solution)/shard_map/ppermute | solution.py:330
  98.3 1.2 %shard_map.132 = (bf16[128,2048]{1,0:T(8,128)(2,1)}, bf16[128,2048]{1,0:T(8,128)(2,1)}) custom-call(bf16[128,2048]{1,0:T(8,128)(2,1)S(1)} %get-tuple-element.109.refs_0_, bf16[128,2048]{1,0:T(8,128)(2,1)S(1)} %get-tuple-element.110.refs_1_, bf16[128,2048]{1,0:T(8,128)(2,1)S(1)} %collective-permute-done.18.refs_2_, ...), custom_call_target="tpu_custom_call" | custom-call | tf_op jit(solution)/shard_map/pallas_call | solution.py:278
  99.4 1.4 %collective-permute-start.20 = (bf16[128,2048]{1,0:T(8,128)(2,1)}, bf16[128,2048]{1,0:T(8,128)(2,1)S(1)}, u32[]{:S(2)}, u32[]{:S(2)}) collective-permute-start(bf16[128,2048]{1,0:T(8,128)(2,1)} %get-tuple-element.123), channel_id=1, source_target_pairs={{0,4},{1,5},{2,0},{3,1},{4,8},{5,9},{6,2},{7,3},{8,12},{9,13},{10,... | collective-permute-start | bytes 1572872 | tf_op jit(solution)/shard_map/ppermute | solution.py:330
  100.8 0.6 collective-permute-start.21
  101.5 6.0 %all-to-all-done.1 = bf16[8,2,8,2048]{3,2,1,0:T(8,128)(2,1)S(1)} async-done(((bf16[8,2,8,2048]{3,2,1,0:T(8,128)(2,1)}), bf16[8,2,8,2048]{3,2,1,0:T(8,128)(2,1)S(1)}, u32[]{:S(2)}, u32[]{:S(2)}) %all-to-all-start.1) | async-done | bytes 524320 | tf_op jit(solution)/shard_map/all_to_all | solution.py:350
  107.5 0.9 copy-done.3
  108.4 1.2 %shard_map.129 = (bf16[128,2048]{1,0:T(8,128)(2,1)}, bf16[128,2048]{1,0:T(8,128)(2,1)S(1)}) custom-call(bf16[128,2048]{1,0:T(8,128)(2,1)S(1)} %bitcast.15, s32[16,16]{1,0:T(8,128)S(1)} %copy-done.6, s32[1,16]{1,0:T(1,128)S(1)} %bitcast.21, s32[1]{0:T(128)} %bitcast.6.me_ref, bf16[128,2048]{1,0:T(8,128)(2,1)S(1)} %copy-done.1, ...), custom_call_target="tpu_custom_call" | custom-call | tf_op jit(solution)/shard_map/pallas_call | solution.py:228
  109.6 0.0 collective-permute-done.20.up_ref
  109.6 1.8 %collective-permute-done.21.down_ref = bf16[128,2048]{1,0:T(8,128)(2,1)S(1)} collective-permute-done((bf16[128,2048]{1,0:T(8,128)(2,1)}, bf16[128,2048]{1,0:T(8,128)(2,1)S(1)}, u32[]{:S(2)}, u32[]{:S(2)}) %collective-permute-start.21) | collective-permute-done | bytes 524320 | tf_op jit(solution)/shard_map/ppermute | solution.py:330
  111.3 1.0 shard_map.133
  (17 shorter events, 0.0 us)
Async XLA Ops:
  0.6 5.8 %collective-permute-start.3 = (bf16[704,2048]{1,0:T(8,128)(2,1)}, bf16[704,2048]{1,0:T(8,128)(2,1)}, u32[]{:S(2)}, u32[]{:S(2)}) collective-permute-start(bf16[704,2048]{1,0:T(8,128)(2,1)} %bitcast.24), channel_id=1, source_target_pairs={{0,1},{1,0},{2,3},{3,2},{4,5},{5,4},{6,7},{7,6},{8,9},{9,8},{10,11... | collective-permute-start | bytes 8650760 | tf_op jit(solution)/shard_map/ppermute | solution.py:330
  1.1 19.4 %collective-permute-start = (bf16[704,2048]{1,0:T(8,128)(2,1)}, bf16[704,2048]{1,0:T(8,128)(2,1)}, u32[]{:S(2)}, u32[]{:S(2)}) collective-permute-start(bf16[704,2048]{1,0:T(8,128)(2,1)} %bitcast.22), channel_id=1, source_target_pairs={{0,1},{1,0},{2,3},{3,2},{4,5},{5,4},{6,7},{7,6},{8,9},{9,8},{10,11... | collective-permute-start | bytes 8650760 | tf_op jit(solution)/shard_map/ppermute | solution.py:330
  1.2 34.4 %collective-permute-start.9 = (bf16[704,2048]{1,0:T(8,128)(2,1)}, bf16[704,2048]{1,0:T(8,128)(2,1)}, u32[]{:S(2)}, u32[]{:S(2)}) collective-permute-start(bf16[704,2048]{1,0:T(8,128)(2,1)} %bitcast.26), channel_id=1, source_target_pairs={{0,1},{1,0},{2,3},{3,2},{4,5},{5,4},{6,7},{7,6},{8,9},{9,8},{10,11... | collective-permute-start | bytes 8650760 | tf_op jit(solution)/shard_map/ppermute | solution.py:330
  1.7 15.3 %collective-permute-start.1 = (bf16[128,2048]{1,0:T(8,128)(2,1)}, bf16[128,2048]{1,0:T(8,128)(2,1)S(1)}, u32[]{:S(2)}, u32[]{:S(2)}) collective-permute-start(bf16[128,2048]{1,0:T(8,128)(2,1)} %refs_2_.1), channel_id=1, source_target_pairs={{0,4},{1,5},{2,0},{3,1},{4,8},{5,9},{6,2},{7,3},{8,12},{9,13},{10,... | collective-permute-start | bytes 1572872 | tf_op jit(solution)/shard_map/ppermute | solution.py:330
  4.3 14.2 %collective-permute-start.2 = (bf16[128,2048]{1,0:T(8,128)(2,1)}, bf16[128,2048]{1,0:T(8,128)(2,1)S(1)}, u32[]{:S(2)}, u32[]{:S(2)}) collective-permute-start(bf16[128,2048]{1,0:T(8,128)(2,1)} %refs_2_.1), channel_id=1, source_target_pairs={{4,0},{5,1},{0,2},{1,3},{8,4},{9,5},{2,6},{3,7},{12,8},{13,9},{6,1... | collective-permute-start | bytes 1572872 | tf_op jit(solution)/shard_map/ppermute | solution.py:330
  18.5 13.2 %collective-permute-start.4 = (bf16[128,2048]{1,0:T(8,128)(2,1)S(1)}, bf16[128,2048]{1,0:T(8,128)(2,1)S(1)}, u32[]{:S(2)}, u32[]{:S(2)}) collective-permute-start(bf16[128,2048]{1,0:T(8,128)(2,1)S(1)} %collective-permute-done.1.refs_0_), channel_id=1, source_target_pairs={{0,4},{1,5},{2,0},{3,1},{4,8},{5,9},{6,2},{7,3},{8,12},{9,13},{10,... | collective-permute-start | bytes 1572872 | tf_op jit(solution)/shard_map/ppermute | solution.py:330
  20.1 13.2 %collective-permute-start.5 = (bf16[128,2048]{1,0:T(8,128)(2,1)S(1)}, bf16[128,2048]{1,0:T(8,128)(2,1)S(1)}, u32[]{:S(2)}, u32[]{:S(2)}) collective-permute-start(bf16[128,2048]{1,0:T(8,128)(2,1)S(1)} %collective-permute-done.2.refs_1_), channel_id=1, source_target_pairs={{4,0},{5,1},{0,2},{1,3},{8,4},{9,5},{2,6},{3,7},{12,8},{13,9},{6,1... | collective-permute-start | bytes 1572872 | tf_op jit(solution)/shard_map/ppermute | solution.py:330
  20.5 7.9 %collective-permute-start.6 = (bf16[8,8,2048]{2,1,0:T(8,128)(2,1)S(1)}, bf16[8,8,2048]{2,1,0:T(8,128)(2,1)S(1)}, u32[]{:S(2)}, u32[]{:S(2)}) collective-permute-start(bf16[8,8,2048]{2,1,0:T(8,128)(2,1)S(1)} %get-tuple-element.72), channel_id=1, source_target_pairs={{0,1},{1,0},{2,3},{3,2},{4,5},{5,4},{6,7},{7,6},{8,9},{9,8},{10,11... | collective-permute-start | bytes 786440 | tf_op jit(solution)/shard_map/ppermute | solution.py:330
  20.5 0.7 copy-start.7
  23.4 12.2 %all-to-all-start = ((f32[16,8,128]{2,1,0:T(8,128)}), f32[16,8,128]{2,1,0:T(8,128)S(1)}, u32[]{:S(2)}, u32[]{:S(2)}) async-start(f32[16,8,128]{2,1,0:T(8,128)} %bitcast.4), calls=%async_computation | async-start | bytes 131072 | tf_op jit(solution)/shard_map/all_to_all | solution.py:354
  33.3 12.6 %collective-permute-start.7 = (bf16[128,2048]{1,0:T(8,128)(2,1)S(1)}, bf16[128,2048]{1,0:T(8,128)(2,1)S(1)}, u32[]{:S(2)}, u32[]{:S(2)}) collective-permute-start(bf16[128,2048]{1,0:T(8,128)(2,1)S(1)} %collective-permute-done.4.refs_0_), channel_id=1, source_target_pairs={{0,4},{1,5},{2,0},{3,1},{4,8},{5,9},{6,2},{7,3},{8,12},{9,13},{10,... | collective-permute-start | bytes 1572872 | tf_op jit(solution)/shard_map/ppermute | solution.py:330
  35.2 11.2 %collective-permute-start.8 = (bf16[128,2048]{1,0:T(8,128)(2,1)S(1)}, bf16[128,2048]{1,0:T(8,128)(2,1)S(1)}, u32[]{:S(2)}, u32[]{:S(2)}) collective-permute-start(bf16[128,2048]{1,0:T(8,128)(2,1)S(1)} %collective-permute-done.5.refs_1_), channel_id=1, source_target_pairs={{4,0},{5,1},{0,2},{1,3},{8,4},{9,5},{2,6},{3,7},{12,8},{13,9},{6,1... | collective-permute-start | bytes 1572872 | tf_op jit(solution)/shard_map/ppermute | solution.py:330
  35.6 0.7 copy-start.4
  36.3 12.3 %copy-start.5 = (s32[64]{0:T(128)S(1)}, s32[64]{0:T(128)}, u32[]{:S(2)}) copy-start(s32[64]{0:T(128)} %constant.8.clone.order_ref) | copy-start | bytes 772
  46.5 8.0 %collective-permute-start.10 = (bf16[64,2048]{1,0:T(8,128)(2,1)S(1)}, bf16[64,2048]{1,0:T(8,128)(2,1)S(1)}, u32[]{:S(2)}, u32[]{:S(2)}) collective-permute-start(bf16[64,2048]{1,0:T(8,128)(2,1)S(1)} %get-tuple-element.82), channel_id=1, source_target_pairs={{0,4},{1,5},{2,0},{3,1},{4,8},{5,9},{6,2},{7,3},{8,12},{9,13},{10,... | collective-permute-start | bytes 786440 | tf_op jit(solution)/shard_map/ppermute | solution.py:330
  47.9 6.8 %collective-permute-start.11 = (bf16[64,2048]{1,0:T(8,128)(2,1)S(1)}, bf16[64,2048]{1,0:T(8,128)(2,1)S(1)}, u32[]{:S(2)}, u32[]{:S(2)}) collective-permute-start(bf16[64,2048]{1,0:T(8,128)(2,1)S(1)} %get-tuple-element.83), channel_id=1, source_target_pairs={{4,0},{5,1},{0,2},{1,3},{8,4},{9,5},{2,6},{3,7},{12,8},{13,9},{6,1... | collective-permute-start | bytes 786440 | tf_op jit(solution)/shard_map/ppermute | solution.py:330
  48.5 8.2 %copy-start = (bf16[128,2048]{1,0:T(8,128)(2,1)S(1)}, bf16[128,2048]{1,0:T(8,128)(2,1)}, u32[]{:S(2)}) copy-start(bf16[128,2048]{1,0:T(8,128)(2,1)} %refs_2_.1) | copy-start | bytes 1572868
  54.7 7.9 %collective-permute-start.12 = (bf16[64,2048]{1,0:T(8,128)(2,1)S(1)}, bf16[64,2048]{1,0:T(8,128)(2,1)S(1)}, u32[]{:S(2)}, u32[]{:S(2)}) collective-permute-start(bf16[64,2048]{1,0:T(8,128)(2,1)S(1)} %get-tuple-element.99), channel_id=1, source_target_pairs={{0,4},{1,5},{2,0},{3,1},{4,8},{5,9},{6,2},{7,3},{8,12},{9,13},{10,... | collective-permute-start | bytes 786440 | tf_op jit(solution)/shard_map/ppermute | solution.py:330
  55.8 6.8 %collective-permute-start.13 = (bf16[64,2048]{1,0:T(8,128)(2,1)S(1)}, bf16[64,2048]{1,0:T(8,128)(2,1)S(1)}, u32[]{:S(2)}, u32[]{:S(2)}) collective-permute-start(bf16[64,2048]{1,0:T(8,128)(2,1)S(1)} %get-tuple-element.100), channel_id=1, source_target_pairs={{4,0},{5,1},{0,2},{1,3},{8,4},{9,5},{2,6},{3,7},{12,8},{13,9},{6,1... | collective-permute-start | bytes 786440 | tf_op jit(solution)/shard_map/ppermute | solution.py:330
  62.6 8.0 %copy-start.2 = (bf16[64,2048]{1,0:T(8,128)(2,1)}, bf16[64,2048]{1,0:T(8,128)(2,1)S(1)}, u32[]{:S(2)}) copy-start(bf16[64,2048]{1,0:T(8,128)(2,1)S(1)} %get-tuple-element.97.second_ref) | copy-start | bytes 786436
  62.6 8.0 %collective-permute-start.14 = (bf16[64,2048]{1,0:T(8,128)(2,1)S(1)}, bf16[64,2048]{1,0:T(8,128)(2,1)S(1)}, u32[]{:S(2)}, u32[]{:S(2)}) collective-permute-start(bf16[64,2048]{1,0:T(8,128)(2,1)S(1)} %get-tuple-element.103), channel_id=1, source_target_pairs={{0,4},{1,5},{2,0},{3,1},{4,8},{5,9},{6,2},{7,3},{8,12},{9,13},{10,... | collective-permute-start | bytes 786440 | tf_op jit(solution)/shard_map/ppermute | solution.py:330
  63.8 6.8 %collective-permute-start.15 = (bf16[64,2048]{1,0:T(8,128)(2,1)S(1)}, bf16[64,2048]{1,0:T(8,128)(2,1)S(1)}, u32[]{:S(2)}, u32[]{:S(2)}) collective-permute-start(bf16[64,2048]{1,0:T(8,128)(2,1)S(1)} %get-tuple-element.104), channel_id=1, source_target_pairs={{4,0},{5,1},{0,2},{1,3},{8,4},{9,5},{2,6},{3,7},{12,8},{13,9},{6,1... | collective-permute-start | bytes 786440 | tf_op jit(solution)/shard_map/ppermute | solution.py:330
  70.7 36.8 %copy-start.1 = (bf16[128,2048]{1,0:T(8,128)(2,1)S(1)}, bf16[128,2048]{1,0:T(8,128)(2,1)}, u32[]{:S(2)}) copy-start(bf16[128,2048]{1,0:T(8,128)(2,1)} %text_ref.1) | copy-start | bytes 1572868
  70.7 36.8 %copy-start.6 = (s32[16,16]{1,0:T(8,128)S(1)}, s32[16,16]{1,0:T(8,128)}, u32[]{:S(2)}) copy-start(s32[16,16]{1,0:T(8,128)} %counts_ref.1) | copy-start | bytes 3076
  70.7 36.8 %copy-start.8 = (s32[16]{0:T(128)S(1)}, s32[16]{0:T(128)}, u32[]{:S(2)}) copy-start(s32[16]{0:T(128)} %param.19) | copy-start | bytes 196
  70.7 6.4 %collective-permute-start.17 = (bf16[64,2048]{1,0:T(8,128)(2,1)S(1)}, bf16[64,2048]{1,0:T(8,128)(2,1)S(1)}, u32[]{:S(2)}, u32[]{:S(2)}) collective-permute-start(bf16[64,2048]{1,0:T(8,128)(2,1)S(1)} %add_convert_fusion), channel_id=1, source_target_pairs={{4,0},{5,1},{0,2},{1,3},{8,4},{9,5},{2,6},{3,7},{12,8},{13,9},{6,1... | collective-permute-start | bytes 786440 | tf_op jit(solution)/shard_map/ppermute | solution.py:330
  72.3 6.4 %collective-permute-start.16 = (bf16[64,2048]{1,0:T(8,128)(2,1)S(1)}, bf16[64,2048]{1,0:T(8,128)(2,1)S(1)}, u32[]{:S(2)}, u32[]{:S(2)}) collective-permute-start(bf16[64,2048]{1,0:T(8,128)(2,1)S(1)} %add_convert_fusion.1), channel_id=1, source_target_pairs={{0,4},{1,5},{2,0},{3,1},{4,8},{5,9},{6,2},{7,3},{8,12},{9,13},{10,... | collective-permute-start | bytes 786440 | tf_op jit(solution)/shard_map/ppermute | solution.py:330
  79.9 15.7 %collective-permute-start.18 = (bf16[128,2048]{1,0:T(8,128)(2,1)}, bf16[128,2048]{1,0:T(8,128)(2,1)S(1)}, u32[]{:S(2)}, u32[]{:S(2)}) collective-permute-start(bf16[128,2048]{1,0:T(8,128)(2,1)} %get-tuple-element.119), channel_id=1, source_target_pairs={{0,4},{1,5},{2,0},{3,1},{4,8},{5,9},{6,2},{7,3},{8,12},{9,13},{10,... | collective-permute-start | bytes 1572872 | tf_op jit(solution)/shard_map/ppermute | solution.py:330
  80.4 17.9 %collective-permute-start.19 = (bf16[128,2048]{1,0:T(8,128)(2,1)}, bf16[128,2048]{1,0:T(8,128)(2,1)S(1)}, u32[]{:S(2)}, u32[]{:S(2)}) collective-permute-start(bf16[128,2048]{1,0:T(8,128)(2,1)} %get-tuple-element.120), channel_id=1, source_target_pairs={{4,0},{5,1},{0,2},{1,3},{8,4},{9,5},{2,6},{3,7},{12,8},{13,9},{6,1... | collective-permute-start | bytes 1572872 | tf_op jit(solution)/shard_map/ppermute | solution.py:330
  81.9 25.6 %all-to-all-start.1 = ((bf16[8,2,8,2048]{3,2,1,0:T(8,128)(2,1)}), bf16[8,2,8,2048]{3,2,1,0:T(8,128)(2,1)S(1)}, u32[]{:S(2)}, u32[]{:S(2)}) async-start(bf16[8,2,8,2048]{3,2,1,0:T(8,128)(2,1)} %shard_map.124), calls=%async_computation.1 | async-start | bytes 1048576 | tf_op jit(solution)/shard_map/all_to_all | solution.py:350
  99.4 10.1 %collective-permute-start.20 = (bf16[128,2048]{1,0:T(8,128)(2,1)}, bf16[128,2048]{1,0:T(8,128)(2,1)S(1)}, u32[]{:S(2)}, u32[]{:S(2)}) collective-permute-start(bf16[128,2048]{1,0:T(8,128)(2,1)} %get-tuple-element.123), channel_id=1, source_target_pairs={{0,4},{1,5},{2,0},{3,1},{4,8},{5,9},{6,2},{7,3},{8,12},{9,13},{10,... | collective-permute-start | bytes 1572872 | tf_op jit(solution)/shard_map/ppermute | solution.py:330
  100.8 10.5 %collective-permute-start.21 = (bf16[128,2048]{1,0:T(8,128)(2,1)}, bf16[128,2048]{1,0:T(8,128)(2,1)S(1)}, u32[]{:S(2)}, u32[]{:S(2)}) collective-permute-start(bf16[128,2048]{1,0:T(8,128)(2,1)} %get-tuple-element.124), channel_id=1, source_target_pairs={{4,0},{5,1},{0,2},{1,3},{8,4},{9,5},{2,6},{3,7},{12,8},{13,9},{6,1... | collective-permute-start | bytes 1572872 | tf_op jit(solution)/shard_map/ppermute | solution.py:330
  107.5 1.0 copy-start.3

commit v7 on v6

--- a/solution.py
+++ b/solution.py
@@ -1,5 +1,4 @@
 import functools
-import math
 
 import jax
 import jax.numpy as jnp
@@ -12,10 +11,26 @@
 NT = (((1,), (1,)), ((), ()))
 
 
+def folded(chips):
+    return chips <= 8
+
+
+def chip_at(place, chips):
+    if not folded(chips):
+        return place
+    return jnp.where(place < chips // 2, 2 * place, 2 * chips - 1 - 2 * place)
+
+
+def place_of(chip, chips):
+    if not folded(chips):
+        return chip
+    return jnp.where(chip % 2 == 0, chip // 2, (2 * chips - 1 - chip) // 2)
+
+
 def ring_of(chips):
-    if chips <= 8:
-        return list(range(0, chips, 2)) + list(range(chips - 1, 0, -2))
-    return list(range(chips))
+    if not folded(chips):
+        return list(range(chips))
+    return list(range(0, chips, 2)) + list(range(chips - 1, 0, -2))
 
 
 def route_kernel(picks_ref, router_hbm, tokens_hbm, out_ref, router_ref, tokens_ref, sems):
@@ -112,7 +127,7 @@
     )(kept, other)
 
 
-def ffn_kernel(count, results, sizes, offsets, chips, holds, me_ref, order_ref, *refs):
+def ffn_kernel(count, results, sizes, offsets, chips, holds, *refs):
     shards = refs[:count]
     table = refs[count]
     weights = refs[count + 1 : count + 7]
@@ -124,7 +139,8 @@
         sems = refs[-1]
         for i in range(6):
             copies.append(pltpu.make_async_copy(weights[i], kept[i], sems.at[i]))
-            copies[i].start()
+        for copy in copies[:3]:
+            copy.start()
         weights = kept
     rows = sum(sizes)
     width = x.shape[1]
@@ -133,13 +149,14 @@
     for ref, m in zip(shards, sizes):
         x[pl.ds(at, m), :] = ref[...]
         at += m
-    me = me_ref[0]
+    me = lax.axis_index("expert")
+    place = place_of(me // 2, chips)
     tokens = rows // len(offsets)
     square = (tokens, tokens)
     eye = lax.broadcasted_iota(jnp.int32, square, 0) == lax.broadcasted_iota(jnp.int32, square, 1)
     routes = [[], []]
     for offset in offsets:
-        source = 2 * order_ref[(me // 2) * chips + offset] + me % 2
+        source = 2 * chip_at((place + offset) % chips, chips) + me % 2
         lines = table[pl.ds(pl.multiple_of(source * 8, 8), 8), :]
         for e in range(2):
             routes[e].append(jnp.sum(jnp.where(eye, lines[e : e + 1], 0.0), axis=1, keepdims=True))
@@ -151,6 +168,8 @@
         gate = lax.dot_general(x[...], wg[...], NT, preferred_element_type=jnp.float32)
         if holds:
             copies[3 * e + 1].wait()
+            for copy in copies[3 * (e + 1) :]:
+                copy.start()
         upward = lax.dot_general(x[...], wu[...], NT, preferred_element_type=jnp.float32)
         hidden[...] = (gate / (1.0 + jnp.exp(-gate)) * upward).astype(jnp.bfloat16)
         if holds:
@@ -167,15 +186,13 @@
                     out[:, lanes] = row[k * block : (k + 1) * block].astype(out.dtype)
 
 
-def ffn(shards, offsets, results, me, order, table, weights, holds):
+def ffn(shards, offsets, results, chips, table, weights, holds):
     sizes = [s.shape[0] for s in shards]
     rows = sum(sizes)
     ff, width = weights[0].shape
     block = rows // results
     vmem = pl.BlockSpec(memory_space=pltpu.VMEM)
-    smem = pl.BlockSpec(memory_space=pltpu.SMEM)
     hbm = pl.BlockSpec(memory_space=pl.ANY)
-    chips = math.isqrt(order.shape[0])
     kept = 6 if holds else 0
     if holds:
         weights = [in_hbm(w) for w in weights]
@@ -183,7 +200,7 @@
         functools.partial(ffn_kernel, len(shards), results, sizes, offsets, chips, kept),
         out_shape=[jax.ShapeDtypeStruct((block, width), jnp.bfloat16)] * results
         + [pltpu.VMEM(w.shape, w.dtype) for w in weights[:kept]],
-        in_specs=[smem] * 2 + [vmem] * (len(shards) + 1) + [hbm if holds else vmem] * 6,
+        in_specs=[vmem] * (len(shards) + 1) + [hbm if holds else vmem] * 6,
         out_specs=[vmem] * (results + kept),
         scratch_shapes=[
             pltpu.VMEM((rows, width), jnp.bfloat16),
@@ -195,7 +212,7 @@
         cost_estimate=pl.CostEstimate(
             flops=12 * rows * ff * width, bytes_accessed=12 * ff * width, transcendentals=2 * rows * ff
         ),
-    )(me[None], order, *shards, table, *weights)
+    )(*shards, table, *weights)
 
 
 def place_kernel(slots, arrived_ref, counts_ref, owner_ref, me_ref, text_ref, first_ref, second_ref, out_ref, near_ref):
@@ -336,10 +353,8 @@
     own = [gate_weight[0].T, up_weight[0].T, down_weight[0]]
     others = [send(w, sibling) for w in own]
 
-    order = jnp.array([ring[(pos[c] + offset) % chips] for c in range(chips) for offset in range(chips)], jnp.int32)
-
     def run(shards, offsets, results=None, holds=False):
-        return ffn(shards, offsets, results or len(shards), me, order, table, weights, holds)
+        return ffn(shards, offsets, results or len(shards), chips, table, weights, holds)
 
     def run_both(s):
         return run([below[s], above[s]], [chips - s, s])

time: 113 us -> 112 us (level)
  Pallas kernels: 36.4 us -> 33.8 us
  waiting for transfers between devices: 42.8 us -> 44.7 us
    ppermute x22, waiting for transfers between devices: 36.5 us -> 39.9 us  [send(): return lax.ppermute(x, 'expert', pairs)]
    pallas_call x4, Pallas kernels: 27.3 us -> 24.6 us  [ffn(): pl.pallas_call(functools.partial(ffn_kernel, len(shards), results, sizes,...]
    all_to_all x1, waiting for transfers between devices: 5.98 us -> 4.57 us  [exchange(): lax.all_to_all(x, 'expert', split_axis=0, concat_axis=0, tiled=True, axis...]
    unnamed x18 -> x14, local copies, waits for them, and re-layouts: 2.32 us -> 1.66 us
  transfers between devices with their start and end apart: 24 -> 24, of which waited for: 14 -> 18; matrix products, arithmetic and copies ran while one was open for 1% -> 1% of each run, Pallas kernels for 31% -> 28%
where the time goes in v7:
time: 112 us; the launch traced here: 111 us
  waiting for transfers between devices  44.7 us (40%)
  Pallas kernels  33.8 us (30%)
  starting transfers between devices  29.5 us (26%)
  local copies, waits for them, and re-layouts  1.66 us (1%)
    ppermute x22, waiting for transfers between devices, send(): return lax.ppermute(x, 'expert', pairs)  39.9 us
    pallas_call x4, Pallas kernels, ffn(): pl.pallas_call(functools.partial(ffn_kernel, len(shards), results, sizes,...  24.6 us
    ppermute x22, starting transfers between devices, send(): return lax.ppermute(x, 'expert', pairs)  20.5 us
    all_to_all x1, starting transfers between devices, local(): lax.all_to_all(table.reshape(devices, 8, -1), 'expert', split_axis=0, con...  5.05 us
    all_to_all x1, waiting for transfers between devices, exchange(): lax.all_to_all(x, 'expert', split_axis=0, concat_axis=0, tiled=True, axis...  4.57 us
    all_to_all x1, starting transfers between devices, exchange(): lax.all_to_all(x, 'expert', split_axis=0, concat_axis=0, tiled=True, axis...  4.02 us
    pallas_call x2, Pallas kernels, merge(): pl.pallas_call(functools.partial(merge_kernel, parts), out_shape=[jax.Sha...  2.28 us
  transfers between devices with their start and end apart: 24, of which 18 were waited for; matrix products, arithmetic and copies ran while one was open for 1% of the time, Pallas kernels for 28%

profile of v7, /device:TPU:0, one launch (start us, length us, event | category | flops | bytes accessed | tf_op | source)
XLA Modules:
  0.0 111.4 jit_solution(7283196248929307049)
XLA Ops:
  0.6 0.5 collective-permute-start.3
  1.1 0.1 collective-permute-start
  1.2 0.4 collective-permute-start.9
  1.7 2.7 %collective-permute-start.1 = (bf16[128,2048]{1,0:T(8,128)(2,1)}, bf16[128,2048]{1,0:T(8,128)(2,1)S(1)}, u32[]{:S(2)}, u32[]{:S(2)}) collective-permute-start(bf16[128,2048]{1,0:T(8,128)(2,1)} %refs_2_.1), channel_id=1, source_target_pairs={{0,4},{1,5},{2,0},{3,1},{4,8},{5,9},{6,2},{7,3},{8,12},{9,13},{10,... | collective-permute-start | bytes 1572872 | tf_op jit(solution)/shard_map/ppermute | solution.py:347
  4.3 0.7 select_reduce_fusion.span_of_ref
  5.1 1.3 %collective-permute-done.3.refs_7_ = bf16[704,2048]{1,0:T(8,128)(2,1)} collective-permute-done((bf16[704,2048]{1,0:T(8,128)(2,1)}, bf16[704,2048]{1,0:T(8,128)(2,1)}, u32[]{:S(2)}, u32[]{:S(2)}) %collective-permute-start.3) | collective-permute-done | bytes 2883616 | tf_op jit(solution)/shard_map/ppermute | solution.py:347
  6.4 1.7 %shard_map.114 = (bf16[8,8,2048]{2,1,0:T(8,128)(2,1)S(1)}, bf16[8,8,2048]{2,1,0:T(8,128)(2,1)S(1)}) custom-call(s32[1]{0:T(128)} %bitcast.6.me_ref, s32[16]{0:T(128)S(1)} %select_reduce_fusion.span_of_ref, bf16[16,8,2048]{2,1,0:T(8,128)(2,1)} %bitcast.28), custom_call_target="tpu_custom_call" | custom-call | tf_op jit(solution)/shard_map/pallas_call | solution.py:102
  8.1 8.9 %collective-permute-done.1.refs_0_ = bf16[128,2048]{1,0:T(8,128)(2,1)S(1)} collective-permute-done((bf16[128,2048]{1,0:T(8,128)(2,1)}, bf16[128,2048]{1,0:T(8,128)(2,1)S(1)}, u32[]{:S(2)}, u32[]{:S(2)}) %collective-permute-start.1) | collective-permute-done | bytes 524320 | tf_op jit(solution)/shard_map/ppermute | solution.py:347
  17.0 1.5 %collective-permute-done.2.refs_1_ = bf16[128,2048]{1,0:T(8,128)(2,1)S(1)} collective-permute-done((bf16[128,2048]{1,0:T(8,128)(2,1)}, bf16[128,2048]{1,0:T(8,128)(2,1)S(1)}, u32[]{:S(2)}, u32[]{:S(2)}) %collective-permute-start.2) | collective-permute-done | bytes 524320 | tf_op jit(solution)/shard_map/ppermute | solution.py:347
  18.5 1.6 %collective-permute-start.4 = (bf16[128,2048]{1,0:T(8,128)(2,1)S(1)}, bf16[128,2048]{1,0:T(8,128)(2,1)S(1)}, u32[]{:S(2)}, u32[]{:S(2)}) collective-permute-start(bf16[128,2048]{1,0:T(8,128)(2,1)S(1)} %collective-permute-done.1.refs_0_), channel_id=1, source_target_pairs={{0,4},{1,5},{2,0},{3,1},{4,8},{5,9},{6,2},{7,3},{8,12},{9,13},{10,... | collective-permute-start | bytes 1572872 | tf_op jit(solution)/shard_map/ppermute | solution.py:347
  20.1 0.4 collective-permute-start.5
  20.5 0.0 collective-permute-start.6
  20.5 0.0 collective-permute-done.refs_6_
  20.6 0.7 copy-done.5
  21.2 2.2 %shard_map.113 = f32[128,128]{1,0:T(8,128)} custom-call(s32[6,128]{1,0:T(8,128)S(1)} %bitcast.20, bf16[16,2048]{1,0:T(8,128)(2,1)} %bitcast.29, bf16[128,2048]{1,0:T(8,128)(2,1)} %refs_2_.1), custom_call_target="tpu_custom_call" | custom-call | tf_op jit(solution)/shard_map/pallas_call | solution.py:73
  23.4 5.0 %all-to-all-start = ((f32[16,8,128]{2,1,0:T(8,128)}), f32[16,8,128]{2,1,0:T(8,128)S(1)}, u32[]{:S(2)}, u32[]{:S(2)}) async-start(f32[16,8,128]{2,1,0:T(8,128)} %bitcast.4), calls=%async_computation | async-start | bytes 131072 | tf_op jit(solution)/shard_map/all_to_all | solution.py:369
  28.5 0.0 collective-permute-done.6.other_ref
  28.5 0.8 shard_map.115
  29.3 2.4 %collective-permute-done.4.refs_0_ = bf16[128,2048]{1,0:T(8,128)(2,1)S(1)} collective-permute-done((bf16[128,2048]{1,0:T(8,128)(2,1)S(1)}, bf16[128,2048]{1,0:T(8,128)(2,1)S(1)}, u32[]{:S(2)}, u32[]{:S(2)}) %collective-permute-start.4) | collective-permute-done | bytes 524320 | tf_op jit(solution)/shard_map/ppermute | solution.py:347
  31.7 1.6 %collective-permute-done.5.refs_1_ = bf16[128,2048]{1,0:T(8,128)(2,1)S(1)} collective-permute-done((bf16[128,2048]{1,0:T(8,128)(2,1)S(1)}, bf16[128,2048]{1,0:T(8,128)(2,1)S(1)}, u32[]{:S(2)}, u32[]{:S(2)}) %collective-permute-start.5) | collective-permute-done | bytes 524320 | tf_op jit(solution)/shard_map/ppermute | solution.py:347
  33.3 1.9 %collective-permute-start.7 = (bf16[128,2048]{1,0:T(8,128)(2,1)S(1)}, bf16[128,2048]{1,0:T(8,128)(2,1)S(1)}, u32[]{:S(2)}, u32[]{:S(2)}) collective-permute-start(bf16[128,2048]{1,0:T(8,128)(2,1)S(1)} %collective-permute-done.4.refs_0_), channel_id=1, source_target_pairs={{0,4},{1,5},{2,0},{3,1},{4,8},{5,9},{6,2},{7,3},{8,12},{9,13},{10,... | collective-permute-start | bytes 1572872 | tf_op jit(solution)/shard_map/ppermute | solution.py:347
  35.2 0.1 collective-permute-start.8
  35.3 0.3 all-to-all-done
  35.6 0.0 collective-permute-done.9.refs_8_
  35.6 9.0 %shard_map.116 = (bf16[128,2048]{1,0:T(8,128)(2,1)S(1)}, bf16[128,2048]{1,0:T(8,128)(2,1)S(1)}, bf16[704,2048]{1,0:T(8,128)(2,1)S(1)}, bf16[704,2048]{1,0:T(8,12...) custom-call(bf16[128,2048]{1,0:T(8,128)(2,1)S(1)} %collective-permut, ...), custom_call_target="tpu_custom_call" | custom-call | flops 4429185024 | bytes 17301504 | tf_op jit(solution)/shard_map/pallas_call | solution.py:199
  44.7 0.5 collective-permute-done.7.below_ref.refs_0_
  45.2 1.2 %collective-permute-done.8.above_ref.refs_1_ = bf16[128,2048]{1,0:T(8,128)(2,1)S(1)} collective-permute-done((bf16[128,2048]{1,0:T(8,128)(2,1)S(1)}, bf16[128,2048]{1,0:T(8,128)(2,1)S(1)}, u32[]{:S(2)}, u32[]{:S(2)}) %collective-permute-start.8) | collective-permute-done | bytes 524320 | tf_op jit(solution)/shard_map/ppermute | solution.py:347
  46.4 0.1 shard_map.117
  46.5 1.4 %collective-permute-start.10 = (bf16[64,2048]{1,0:T(8,128)(2,1)S(1)}, bf16[64,2048]{1,0:T(8,128)(2,1)S(1)}, u32[]{:S(2)}, u32[]{:S(2)}) collective-permute-start(bf16[64,2048]{1,0:T(8,128)(2,1)S(1)} %get-tuple-element.82), channel_id=1, source_target_pairs={{0,4},{1,5},{2,0},{3,1},{4,8},{5,9},{6,2},{7,3},{8,12},{9,13},{10,... | collective-permute-start | bytes 786440 | tf_op jit(solution)/shard_map/ppermute | solution.py:347
  47.9 0.7 collective-permute-start.11
  48.5 5.2 %shard_map.118 = (bf16[64,2048]{1,0:T(8,128)(2,1)S(1)}, bf16[64,2048]{1,0:T(8,128)(2,1)S(1)}, bf16[64,2048]{1,0:T(8,128)(2,1)S(1)}, bf16[64,2048]{1,0:T(8,128)(2,1)S(1)}) custom-call(bf16[128,2048]{1,0:T(8,128)(2,1)S(1)} %collective-permute-done.7.below_ref.refs_0_, bf16[128,2048]{1,0:T(8,128)(2,1)S(1)} %collective-permute-done.8.above_ref.refs_1_, ...), custom_call_target="tpu_custom_call" | custom-call | flops 4429185024 | bytes 17301504 | tf_op jit(solution)/shard_map/pallas_call | solution.py:199
  53.8 0.5 collective-permute-done.11.refs_1_
  54.2 0.9 collective-permute-start.12
  55.2 1.1 collective-permute-start.13
  56.3 5.2 %shard_map.119 = (bf16[64,2048]{1,0:T(8,128)(2,1)S(1)}, bf16[64,2048]{1,0:T(8,128)(2,1)S(1)}, bf16[64,2048]{1,0:T(8,128)(2,1)S(1)}, bf16[64,2048]{1,0:T(8,128)(2,1)S(1)}) custom-call(bf16[64,2048]{1,0:T(8,128)(2,1)S(1)} %collective-permute-done.10.refs_0_, bf16[64,2048]{1,0:T(8,128)(2,1)S(1)} %collective-permute-done.11.refs_1_, ...), custom_call_target="tpu_custom_call" | custom-call | flops 4429185024 | bytes 17301504 | tf_op jit(solution)/shard_map/pallas_call | solution.py:199
  61.5 0.0 collective-permute-done.12.refs_2_
  61.5 0.3 collective-permute-done.13.refs_5_
  61.7 0.8 collective-permute-start.14
  62.6 1.2 %collective-permute-start.15 = (bf16[64,2048]{1,0:T(8,128)(2,1)S(1)}, bf16[64,2048]{1,0:T(8,128)(2,1)S(1)}, u32[]{:S(2)}, u32[]{:S(2)}) collective-permute-start(bf16[64,2048]{1,0:T(8,128)(2,1)S(1)} %get-tuple-element.104), channel_id=1, source_target_pairs={{4,0},{5,1},{0,2},{1,3},{8,4},{9,5},{2,6},{3,7},{12,8},{13,9},{6,1... | collective-permute-start | bytes 786440 | tf_op jit(solution)/shard_map/ppermute | solution.py:347
  63.8 5.2 %shard_map.121 = (bf16[128,2048]{1,0:T(8,128)(2,1)S(1)}, bf16[128,2048]{1,0:T(8,128)(2,1)S(1)}) custom-call(bf16[128,2048]{1,0:T(8,128)(2,1)S(1)} %collective-permute-done.1.refs_0_, bf16[128,2048]{1,0:T(8,128)(2,1)S(1)} %collective-permute-done.2.refs_1_, f32[128,128]{1,0:T(8,128)S(1)} %bitcast.19, bf16[704,2048]{1,0:T(8,128)(2,1)S(1)} %get-tuple-element.84.refs_3_.refs_4_, ...), custom_call_target="tpu_custom_call" | custom-call | flops 4429185024 | bytes 17301504 | tf_op jit(solution)/shard_map/pallas_call | solution.py:199
  69.0 1.0 collective-permute-done.15
  70.0 0.1 add_convert_fusion
  70.1 0.0 copy-start.1
  70.1 0.0 copy-start.4
  70.1 0.0 copy-start.6
  70.1 1.0 collective-permute-start.17
  71.1 0.1 add_convert_fusion.1
  71.2 1.1 collective-permute-start.16
  72.3 4.7 %collective-permute-done.17.refs_4_ = bf16[64,2048]{1,0:T(8,128)(2,1)S(1)} collective-permute-done((bf16[64,2048]{1,0:T(8,128)(2,1)S(1)}, bf16[64,2048]{1,0:T(8,128)(2,1)S(1)}, u32[]{:S(2)}, u32[]{:S(2)}) %collective-permute-start.17) | collective-permute-done | bytes 262176 | tf_op jit(solution)/shard_map/ppermute | solution.py:347
  77.0 2.6 %collective-permute-done.16.refs_3_ = bf16[64,2048]{1,0:T(8,128)(2,1)S(1)} collective-permute-done((bf16[64,2048]{1,0:T(8,128)(2,1)S(1)}, bf16[64,2048]{1,0:T(8,128)(2,1)S(1)}, u32[]{:S(2)}, u32[]{:S(2)}) %collective-permute-start.16) | collective-permute-done | bytes 262176 | tf_op jit(solution)/shard_map/ppermute | solution.py:347
  79.6 1.1 %shard_map.122 = (bf16[128,2048]{1,0:T(8,128)(2,1)}, bf16[128,2048]{1,0:T(8,128)(2,1)}) custom-call(bf16[128,2048]{1,0:T(8,128)(2,1)S(1)} %get-tuple-element.111.refs_0_, bf16[128,2048]{1,0:T(8,128)(2,1)S(1)} %get-tuple-element.112.refs_1_, bf16[64,2048]{1,0:T(8,128)(2,1)S(1)} %collective-permute-done.12.refs_2_, ...), custom_call_target="tpu_custom_call" | custom-call | tf_op jit(solution)/shard_map/pallas_call | solution.py:295
  80.7 1.6 %collective-permute-start.18 = (bf16[128,2048]{1,0:T(8,128)(2,1)}, bf16[128,2048]{1,0:T(8,128)(2,1)S(1)}, u32[]{:S(2)}, u32[]{:S(2)}) collective-permute-start(bf16[128,2048]{1,0:T(8,128)(2,1)} %get-tuple-element.119), channel_id=1, source_target_pairs={{0,4},{1,5},{2,0},{3,1},{4,8},{5,9},{6,2},{7,3},{8,12},{9,13},{10,... | collective-permute-start | bytes 1572872 | tf_op jit(solution)/shard_map/ppermute | solution.py:347
  82.3 0.5 collective-permute-start.19
  82.7 4.0 %all-to-all-start.1 = ((bf16[8,2,8,2048]{3,2,1,0:T(8,128)(2,1)}), bf16[8,2,8,2048]{3,2,1,0:T(8,128)(2,1)S(1)}, u32[]{:S(2)}, u32[]{:S(2)}) async-start(bf16[8,2,8,2048]{3,2,1,0:T(8,128)(2,1)} %shard_map.115), calls=%async_computation.1 | async-start | bytes 1048576 | tf_op jit(solution)/shard_map/all_to_all | solution.py:365
  86.8 8.8 %collective-permute-done.18.refs_2_ = bf16[128,2048]{1,0:T(8,128)(2,1)S(1)} collective-permute-done((bf16[128,2048]{1,0:T(8,128)(2,1)}, bf16[128,2048]{1,0:T(8,128)(2,1)S(1)}, u32[]{:S(2)}, u32[]{:S(2)}) %collective-permute-start.18) | collective-permute-done | bytes 524320 | tf_op jit(solution)/shard_map/ppermute | solution.py:347
  95.5 1.1 %collective-permute-done.19.refs_3_ = bf16[128,2048]{1,0:T(8,128)(2,1)S(1)} collective-permute-done((bf16[128,2048]{1,0:T(8,128)(2,1)}, bf16[128,2048]{1,0:T(8,128)(2,1)S(1)}, u32[]{:S(2)}, u32[]{:S(2)}) %collective-permute-start.19) | collective-permute-done | bytes 524320 | tf_op jit(solution)/shard_map/ppermute | solution.py:347
  96.7 1.1 %shard_map.123 = (bf16[128,2048]{1,0:T(8,128)(2,1)}, bf16[128,2048]{1,0:T(8,128)(2,1)}) custom-call(bf16[128,2048]{1,0:T(8,128)(2,1)S(1)} %get-tuple-element.109.refs_0_, bf16[128,2048]{1,0:T(8,128)(2,1)S(1)} %get-tuple-element.110.refs_1_, bf16[128,2048]{1,0:T(8,128)(2,1)S(1)} %collective-permute-done.18.refs_2_, ...), custom_call_target="tpu_custom_call" | custom-call | tf_op jit(solution)/shard_map/pallas_call | solution.py:295
  97.8 2.4 %collective-permute-start.20 = (bf16[128,2048]{1,0:T(8,128)(2,1)}, bf16[128,2048]{1,0:T(8,128)(2,1)S(1)}, u32[]{:S(2)}, u32[]{:S(2)}) collective-permute-start(bf16[128,2048]{1,0:T(8,128)(2,1)} %get-tuple-element.123), channel_id=1, source_target_pairs={{0,4},{1,5},{2,0},{3,1},{4,8},{5,9},{6,2},{7,3},{8,12},{9,13},{10,... | collective-permute-start | bytes 1572872 | tf_op jit(solution)/shard_map/ppermute | solution.py:347
  100.3 4.6 %all-to-all-done.1 = bf16[8,2,8,2048]{3,2,1,0:T(8,128)(2,1)S(1)} async-done(((bf16[8,2,8,2048]{3,2,1,0:T(8,128)(2,1)}), bf16[8,2,8,2048]{3,2,1,0:T(8,128)(2,1)S(1)}, u32[]{:S(2)}, u32[]{:S(2)}) %all-to-all-start.1) | async-done | bytes 524320 | tf_op jit(solution)/shard_map/all_to_all | solution.py:365
  104.9 0.9 copy-done.3
  105.8 1.2 %shard_map.120 = (bf16[128,2048]{1,0:T(8,128)(2,1)}, bf16[128,2048]{1,0:T(8,128)(2,1)S(1)}) custom-call(bf16[128,2048]{1,0:T(8,128)(2,1)S(1)} %bitcast.15, s32[16,16]{1,0:T(8,128)S(1)} %copy-done.4, s32[1,16]{1,0:T(1,128)S(1)} %bitcast.21, s32[1]{0:T(128)} %bitcast.6.me_ref, bf16[128,2048]{1,0:T(8,128)(2,1)S(1)} %copy-done.1, ...), custom_call_target="tpu_custom_call" | custom-call | tf_op jit(solution)/shard_map/pallas_call | solution.py:245
  107.0 1.0 collective-permute-done.20.up_ref
  107.9 2.4 %collective-permute-done.21.down_ref = bf16[128,2048]{1,0:T(8,128)(2,1)S(1)} collective-permute-done((bf16[128,2048]{1,0:T(8,128)(2,1)}, bf16[128,2048]{1,0:T(8,128)(2,1)S(1)}, u32[]{:S(2)}, u32[]{:S(2)}) %collective-permute-start.21) | collective-permute-done | bytes 524320 | tf_op jit(solution)/shard_map/ppermute | solution.py:347
  110.4 1.0 shard_map.124
  (13 shorter events, 0.0 us)
Async XLA Ops:
  0.6 5.8 %collective-permute-start.3 = (bf16[704,2048]{1,0:T(8,128)(2,1)}, bf16[704,2048]{1,0:T(8,128)(2,1)}, u32[]{:S(2)}, u32[]{:S(2)}) collective-permute-start(bf16[704,2048]{1,0:T(8,128)(2,1)} %bitcast.24), channel_id=1, source_target_pairs={{0,1},{1,0},{2,3},{3,2},{4,5},{5,4},{6,7},{7,6},{8,9},{9,8},{10,11... | collective-permute-start | bytes 8650760 | tf_op jit(solution)/shard_map/ppermute | solution.py:347
  1.1 19.4 %collective-permute-start = (bf16[704,2048]{1,0:T(8,128)(2,1)}, bf16[704,2048]{1,0:T(8,128)(2,1)}, u32[]{:S(2)}, u32[]{:S(2)}) collective-permute-start(bf16[704,2048]{1,0:T(8,128)(2,1)} %bitcast.22), channel_id=1, source_target_pairs={{0,1},{1,0},{2,3},{3,2},{4,5},{5,4},{6,7},{7,6},{8,9},{9,8},{10,11... | collective-permute-start | bytes 8650760 | tf_op jit(solution)/shard_map/ppermute | solution.py:347
  1.2 34.4 %collective-permute-start.9 = (bf16[704,2048]{1,0:T(8,128)(2,1)}, bf16[704,2048]{1,0:T(8,128)(2,1)}, u32[]{:S(2)}, u32[]{:S(2)}) collective-permute-start(bf16[704,2048]{1,0:T(8,128)(2,1)} %bitcast.26), channel_id=1, source_target_pairs={{0,1},{1,0},{2,3},{3,2},{4,5},{5,4},{6,7},{7,6},{8,9},{9,8},{10,11... | collective-permute-start | bytes 8650760 | tf_op jit(solution)/shard_map/ppermute | solution.py:347
  1.7 15.3 %collective-permute-start.1 = (bf16[128,2048]{1,0:T(8,128)(2,1)}, bf16[128,2048]{1,0:T(8,128)(2,1)S(1)}, u32[]{:S(2)}, u32[]{:S(2)}) collective-permute-start(bf16[128,2048]{1,0:T(8,128)(2,1)} %refs_2_.1), channel_id=1, source_target_pairs={{0,4},{1,5},{2,0},{3,1},{4,8},{5,9},{6,2},{7,3},{8,12},{9,13},{10,... | collective-permute-start | bytes 1572872 | tf_op jit(solution)/shard_map/ppermute | solution.py:347
  4.3 14.2 %collective-permute-start.2 = (bf16[128,2048]{1,0:T(8,128)(2,1)}, bf16[128,2048]{1,0:T(8,128)(2,1)S(1)}, u32[]{:S(2)}, u32[]{:S(2)}) collective-permute-start(bf16[128,2048]{1,0:T(8,128)(2,1)} %refs_2_.1), channel_id=1, source_target_pairs={{4,0},{5,1},{0,2},{1,3},{8,4},{9,5},{2,6},{3,7},{12,8},{13,9},{6,1... | collective-permute-start | bytes 1572872 | tf_op jit(solution)/shard_map/ppermute | solution.py:347
  18.5 13.2 %collective-permute-start.4 = (bf16[128,2048]{1,0:T(8,128)(2,1)S(1)}, bf16[128,2048]{1,0:T(8,128)(2,1)S(1)}, u32[]{:S(2)}, u32[]{:S(2)}) collective-permute-start(bf16[128,2048]{1,0:T(8,128)(2,1)S(1)} %collective-permute-done.1.refs_0_), channel_id=1, source_target_pairs={{0,4},{1,5},{2,0},{3,1},{4,8},{5,9},{6,2},{7,3},{8,12},{9,13},{10,... | collective-permute-start | bytes 1572872 | tf_op jit(solution)/shard_map/ppermute | solution.py:347
  20.1 13.2 %collective-permute-start.5 = (bf16[128,2048]{1,0:T(8,128)(2,1)S(1)}, bf16[128,2048]{1,0:T(8,128)(2,1)S(1)}, u32[]{:S(2)}, u32[]{:S(2)}) collective-permute-start(bf16[128,2048]{1,0:T(8,128)(2,1)S(1)} %collective-permute-done.2.refs_1_), channel_id=1, source_target_pairs={{4,0},{5,1},{0,2},{1,3},{8,4},{9,5},{2,6},{3,7},{12,8},{13,9},{6,1... | collective-permute-start | bytes 1572872 | tf_op jit(solution)/shard_map/ppermute | solution.py:347
  20.5 7.9 %collective-permute-start.6 = (bf16[8,8,2048]{2,1,0:T(8,128)(2,1)S(1)}, bf16[8,8,2048]{2,1,0:T(8,128)(2,1)S(1)}, u32[]{:S(2)}, u32[]{:S(2)}) collective-permute-start(bf16[8,8,2048]{2,1,0:T(8,128)(2,1)S(1)} %get-tuple-element.72), channel_id=1, source_target_pairs={{0,1},{1,0},{2,3},{3,2},{4,5},{5,4},{6,7},{7,6},{8,9},{9,8},{10,11... | collective-permute-start | bytes 786440 | tf_op jit(solution)/shard_map/ppermute | solution.py:347
  20.5 0.7 copy-start.5
  23.4 12.2 %all-to-all-start = ((f32[16,8,128]{2,1,0:T(8,128)}), f32[16,8,128]{2,1,0:T(8,128)S(1)}, u32[]{:S(2)}, u32[]{:S(2)}) async-start(f32[16,8,128]{2,1,0:T(8,128)} %bitcast.4), calls=%async_computation | async-start | bytes 131072 | tf_op jit(solution)/shard_map/all_to_all | solution.py:369
  33.3 11.9 %collective-permute-start.7 = (bf16[128,2048]{1,0:T(8,128)(2,1)S(1)}, bf16[128,2048]{1,0:T(8,128)(2,1)S(1)}, u32[]{:S(2)}, u32[]{:S(2)}) collective-permute-start(bf16[128,2048]{1,0:T(8,128)(2,1)S(1)} %collective-permute-done.4.refs_0_), channel_id=1, source_target_pairs={{0,4},{1,5},{2,0},{3,1},{4,8},{5,9},{6,2},{7,3},{8,12},{9,13},{10,... | collective-permute-start | bytes 1572872 | tf_op jit(solution)/shard_map/ppermute | solution.py:347
  35.2 11.2 %collective-permute-start.8 = (bf16[128,2048]{1,0:T(8,128)(2,1)S(1)}, bf16[128,2048]{1,0:T(8,128)(2,1)S(1)}, u32[]{:S(2)}, u32[]{:S(2)}) collective-permute-start(bf16[128,2048]{1,0:T(8,128)(2,1)S(1)} %collective-permute-done.5.refs_1_), channel_id=1, source_target_pairs={{4,0},{5,1},{0,2},{1,3},{8,4},{9,5},{2,6},{3,7},{12,8},{13,9},{6,1... | collective-permute-start | bytes 1572872 | tf_op jit(solution)/shard_map/ppermute | solution.py:347
  46.5 7.3 %collective-permute-start.10 = (bf16[64,2048]{1,0:T(8,128)(2,1)S(1)}, bf16[64,2048]{1,0:T(8,128)(2,1)S(1)}, u32[]{:S(2)}, u32[]{:S(2)}) collective-permute-start(bf16[64,2048]{1,0:T(8,128)(2,1)S(1)} %get-tuple-element.82), channel_id=1, source_target_pairs={{0,4},{1,5},{2,0},{3,1},{4,8},{5,9},{6,2},{7,3},{8,12},{9,13},{10,... | collective-permute-start | bytes 786440 | tf_op jit(solution)/shard_map/ppermute | solution.py:347
  47.9 6.4 %collective-permute-start.11 = (bf16[64,2048]{1,0:T(8,128)(2,1)S(1)}, bf16[64,2048]{1,0:T(8,128)(2,1)S(1)}, u32[]{:S(2)}, u32[]{:S(2)}) collective-permute-start(bf16[64,2048]{1,0:T(8,128)(2,1)S(1)} %get-tuple-element.83), channel_id=1, source_target_pairs={{4,0},{5,1},{0,2},{1,3},{8,4},{9,5},{2,6},{3,7},{12,8},{13,9},{6,1... | collective-permute-start | bytes 786440 | tf_op jit(solution)/shard_map/ppermute | solution.py:347
  48.5 7.7 %copy-start = (bf16[128,2048]{1,0:T(8,128)(2,1)S(1)}, bf16[128,2048]{1,0:T(8,128)(2,1)}, u32[]{:S(2)}) copy-start(bf16[128,2048]{1,0:T(8,128)(2,1)} %refs_2_.1) | copy-start | bytes 1572868
  54.2 7.2 %collective-permute-start.12 = (bf16[64,2048]{1,0:T(8,128)(2,1)S(1)}, bf16[64,2048]{1,0:T(8,128)(2,1)S(1)}, u32[]{:S(2)}, u32[]{:S(2)}) collective-permute-start(bf16[64,2048]{1,0:T(8,128)(2,1)S(1)} %get-tuple-element.99), channel_id=1, source_target_pairs={{0,4},{1,5},{2,0},{3,1},{4,8},{5,9},{6,2},{7,3},{8,12},{9,13},{10,... | collective-permute-start | bytes 786440 | tf_op jit(solution)/shard_map/ppermute | solution.py:347
  55.2 6.6 %collective-permute-start.13 = (bf16[64,2048]{1,0:T(8,128)(2,1)S(1)}, bf16[64,2048]{1,0:T(8,128)(2,1)S(1)}, u32[]{:S(2)}, u32[]{:S(2)}) collective-permute-start(bf16[64,2048]{1,0:T(8,128)(2,1)S(1)} %get-tuple-element.100), channel_id=1, source_target_pairs={{4,0},{5,1},{0,2},{1,3},{8,4},{9,5},{2,6},{3,7},{12,8},{13,9},{6,1... | collective-permute-start | bytes 786440 | tf_op jit(solution)/shard_map/ppermute | solution.py:347
  61.5 7.5 %copy-start.2 = (bf16[64,2048]{1,0:T(8,128)(2,1)}, bf16[64,2048]{1,0:T(8,128)(2,1)S(1)}, u32[]{:S(2)}) copy-start(bf16[64,2048]{1,0:T(8,128)(2,1)S(1)} %get-tuple-element.97.second_ref) | copy-start | bytes 786436
  61.7 7.2 %collective-permute-start.14 = (bf16[64,2048]{1,0:T(8,128)(2,1)S(1)}, bf16[64,2048]{1,0:T(8,128)(2,1)S(1)}, u32[]{:S(2)}, u32[]{:S(2)}) collective-permute-start(bf16[64,2048]{1,0:T(8,128)(2,1)S(1)} %get-tuple-element.103), channel_id=1, source_target_pairs={{0,4},{1,5},{2,0},{3,1},{4,8},{5,9},{6,2},{7,3},{8,12},{9,13},{10,... | collective-permute-start | bytes 786440 | tf_op jit(solution)/shard_map/ppermute | solution.py:347
  62.6 7.4 %collective-permute-start.15 = (bf16[64,2048]{1,0:T(8,128)(2,1)S(1)}, bf16[64,2048]{1,0:T(8,128)(2,1)S(1)}, u32[]{:S(2)}, u32[]{:S(2)}) collective-permute-start(bf16[64,2048]{1,0:T(8,128)(2,1)S(1)} %get-tuple-element.104), channel_id=1, source_target_pairs={{4,0},{5,1},{0,2},{1,3},{8,4},{9,5},{2,6},{3,7},{12,8},{13,9},{6,1... | collective-permute-start | bytes 786440 | tf_op jit(solution)/shard_map/ppermute | solution.py:347
  70.1 34.8 %copy-start.1 = (bf16[128,2048]{1,0:T(8,128)(2,1)S(1)}, bf16[128,2048]{1,0:T(8,128)(2,1)}, u32[]{:S(2)}) copy-start(bf16[128,2048]{1,0:T(8,128)(2,1)} %text_ref.1) | copy-start | bytes 1572868
  70.1 34.8 %copy-start.4 = (s32[16,16]{1,0:T(8,128)S(1)}, s32[16,16]{1,0:T(8,128)}, u32[]{:S(2)}) copy-start(s32[16,16]{1,0:T(8,128)} %counts_ref.1) | copy-start | bytes 3076
  70.1 34.8 %copy-start.6 = (s32[16]{0:T(128)S(1)}, s32[16]{0:T(128)}, u32[]{:S(2)}) copy-start(s32[16]{0:T(128)} %param.18) | copy-start | bytes 196
  70.1 6.9 %collective-permute-start.17 = (bf16[64,2048]{1,0:T(8,128)(2,1)S(1)}, bf16[64,2048]{1,0:T(8,128)(2,1)S(1)}, u32[]{:S(2)}, u32[]{:S(2)}) collective-permute-start(bf16[64,2048]{1,0:T(8,128)(2,1)S(1)} %add_convert_fusion), channel_id=1, source_target_pairs={{4,0},{5,1},{0,2},{1,3},{8,4},{9,5},{2,6},{3,7},{12,8},{13,9},{6,1... | collective-permute-start | bytes 786440 | tf_op jit(solution)/shard_map/ppermute | solution.py:347
  71.2 8.4 %collective-permute-start.16 = (bf16[64,2048]{1,0:T(8,128)(2,1)S(1)}, bf16[64,2048]{1,0:T(8,128)(2,1)S(1)}, u32[]{:S(2)}, u32[]{:S(2)}) collective-permute-start(bf16[64,2048]{1,0:T(8,128)(2,1)S(1)} %add_convert_fusion.1), channel_id=1, source_target_pairs={{0,4},{1,5},{2,0},{3,1},{4,8},{5,9},{6,2},{7,3},{8,12},{9,13},{10,... | collective-permute-start | bytes 786440 | tf_op jit(solution)/shard_map/ppermute | solution.py:347
  80.7 14.8 %collective-permute-start.18 = (bf16[128,2048]{1,0:T(8,128)(2,1)}, bf16[128,2048]{1,0:T(8,128)(2,1)S(1)}, u32[]{:S(2)}, u32[]{:S(2)}) collective-permute-start(bf16[128,2048]{1,0:T(8,128)(2,1)} %get-tuple-element.119), channel_id=1, source_target_pairs={{0,4},{1,5},{2,0},{3,1},{4,8},{5,9},{6,2},{7,3},{8,12},{9,13},{10,... | collective-permute-start | bytes 1572872 | tf_op jit(solution)/shard_map/ppermute | solution.py:347
  82.3 14.4 %collective-permute-start.19 = (bf16[128,2048]{1,0:T(8,128)(2,1)}, bf16[128,2048]{1,0:T(8,128)(2,1)S(1)}, u32[]{:S(2)}, u32[]{:S(2)}) collective-permute-start(bf16[128,2048]{1,0:T(8,128)(2,1)} %get-tuple-element.120), channel_id=1, source_target_pairs={{4,0},{5,1},{0,2},{1,3},{8,4},{9,5},{2,6},{3,7},{12,8},{13,9},{6,1... | collective-permute-start | bytes 1572872 | tf_op jit(solution)/shard_map/ppermute | solution.py:347
  82.7 22.1 %all-to-all-start.1 = ((bf16[8,2,8,2048]{3,2,1,0:T(8,128)(2,1)}), bf16[8,2,8,2048]{3,2,1,0:T(8,128)(2,1)S(1)}, u32[]{:S(2)}, u32[]{:S(2)}) async-start(bf16[8,2,8,2048]{3,2,1,0:T(8,128)(2,1)} %shard_map.115), calls=%async_computation.1 | async-start | bytes 1048576 | tf_op jit(solution)/shard_map/all_to_all | solution.py:365
  97.8 10.1 %collective-permute-start.20 = (bf16[128,2048]{1,0:T(8,128)(2,1)}, bf16[128,2048]{1,0:T(8,128)(2,1)S(1)}, u32[]{:S(2)}, u32[]{:S(2)}) collective-permute-start(bf16[128,2048]{1,0:T(8,128)(2,1)} %get-tuple-element.123), channel_id=1, source_target_pairs={{0,4},{1,5},{2,0},{3,1},{4,8},{5,9},{6,2},{7,3},{8,12},{9,13},{10,... | collective-permute-start | bytes 1572872 | tf_op jit(solution)/shard_map/ppermute | solution.py:347
  100.3 10.1 %collective-permute-start.21 = (bf16[128,2048]{1,0:T(8,128)(2,1)}, bf16[128,2048]{1,0:T(8,128)(2,1)S(1)}, u32[]{:S(2)}, u32[]{:S(2)}) collective-permute-start(bf16[128,2048]{1,0:T(8,128)(2,1)} %get-tuple-element.124), channel_id=1, source_target_pairs={{4,0},{5,1},{0,2},{1,3},{8,4},{9,5},{2,6},{3,7},{12,8},{13,9},{6,1... | collective-permute-start | bytes 1572872 | tf_op jit(solution)/shard_map/ppermute | solution.py:347
  104.8 1.0 copy-start.3

commit v8 on v7

--- a/solution.py
+++ b/solution.py
@@ -279,26 +279,24 @@
     )(below, above)
 
 
-def merge_kernel(parts, *refs):
-    for i in range(2):
-        total, out = refs[i], refs[2 + 2 * parts + i]
-        at = 0
-        for came in refs[2 + i * parts : 2 + (i + 1) * parts]:
-            part = pl.ds(at, came.shape[0])
-            out[part, :] = (total[part, :].astype(jnp.float32) + came[...].astype(jnp.float32)).astype(out.dtype)
-            at += came.shape[0]
-
-
-def merge(above, below, up_parts, down_parts):
-    parts = len(up_parts)
-    vmem = pl.BlockSpec(memory_space=pltpu.VMEM)
-    return pl.pallas_call(
-        functools.partial(merge_kernel, parts),
-        out_shape=[jax.ShapeDtypeStruct(above.shape, jnp.bfloat16)] * 2,
-        in_specs=[vmem] * (2 + 2 * parts),
-        out_specs=[vmem] * 2,
+def merge_kernel(total_ref, *refs):
+    out = refs[-1]
+    at = 0
+    for came in refs[:-1]:
+        part = pl.ds(at, came.shape[0])
+        out[part, :] = (total_ref[part, :].astype(jnp.float32) + came[...].astype(jnp.float32)).astype(out.dtype)
+        at += came.shape[0]
+
+
+def merge(total, *came):
+    vmem = pl.BlockSpec(memory_space=pltpu.VMEM)
+    return pl.pallas_call(
+        merge_kernel,
+        out_shape=jax.ShapeDtypeStruct(total.shape, jnp.bfloat16),
+        in_specs=[vmem] * (1 + len(came)),
+        out_specs=vmem,
         compiler_params=pltpu.CompilerParams(vmem_limit_bytes=8 * 2**20),
-    )(above, below, *up_parts, *down_parts)
+    )(total, *came)
 
 
 def finish_kernel(near_ref, up_ref, down_ref, out_ref):
@@ -413,16 +411,16 @@
         long_up, long_down, short_up, short_down, from_below[1], from_above[1]
     )
     long_up, long_down = send(add(above_second, long_up), up), send(add(below_first, long_down), down)
-    going_up, going_down = merge(
-        from_above[far - 2], from_below[far - 2], [short_up, long_up], [long_down, short_down]
-    )
+    going_up = merge(from_above[far - 2], short_up, long_up)
+    going_down = merge(from_below[far - 2], long_down, short_down)
     for s in range(2, far - 2):
         if s not in from_below:
             from_below[s], from_above[s] = run_both(s)
     for s in range(far - 2, 0, -1):
-        going_up, going_down = tie(send(going_up, up), send(going_down, down))
+        going_up, going_down = send(going_up, up), send(going_down, down)
         if s > 1:
-            going_up, going_down = merge(from_above[s - 1], from_below[s - 1], [going_up], [going_down])
+            going_up, going_down = merge(from_above[s - 1], going_up), merge(from_below[s - 1], going_down)
+
     arrived = arrived.reshape(devices * slots, width)
     next_span, near = place_images(
         arrived, image_counts, span_owner, me, text_rows, slots, result_first, result_second

time: 112 us -> 110 us (0.982)
  waiting for transfers between devices: 44.7 us -> 42.9 us
    ppermute x22, waiting for transfers between devices: 39.9 us -> 38.2 us  [send(): return lax.ppermute(x, 'expert', pairs)]
    pallas_call x2 -> x4, Pallas kernels: 2.28 us -> 1.53 us  [merge(): pl.pallas_call(merge_kernel, out_shape=jax.ShapeDtypeStruct(total.shape,...]
  transfers between devices with their start and end apart: 24 -> 24, of which waited for: 18 -> 16; matrix products, arithmetic and copies ran while one was open for 1% -> 1% of each run, Pallas kernels for 28% -> 29%
where the time goes in v8:
time: 110 us; the launch traced here: 109 us
  waiting for transfers between devices  42.9 us (39%)
  Pallas kernels  33 us (30%)
  starting transfers between devices  29 us (26%)
  local copies, waits for them, and re-layouts  2.7 us (2%)
    ppermute x22, waiting for transfers between devices, send(): return lax.ppermute(x, 'expert', pairs)  38.2 us
    pallas_call x4, Pallas kernels, ffn(): pl.pallas_call(functools.partial(ffn_kernel, len(shards), results, sizes,...  24.6 us
    ppermute x22, starting transfers between devices, send(): return lax.ppermute(x, 'expert', pairs)  20.2 us
    all_to_all x1, starting transfers between devices, local(): lax.all_to_all(table.reshape(devices, 8, -1), 'expert', split_axis=0, con...  5.05 us
    all_to_all x1, waiting for transfers between devices, exchange(): lax.all_to_all(x, 'expert', split_axis=0, concat_axis=0, tiled=True, axis...  4.41 us
    all_to_all x1, starting transfers between devices, exchange(): lax.all_to_all(x, 'expert', split_axis=0, concat_axis=0, tiled=True, axis...  3.71 us
    unnamed x14, local copies, waits for them, and re-layouts  2.7 us
  transfers between devices with their start and end apart: 24, of which 16 were waited for; matrix products, arithmetic and copies ran while one was open for 1% of the time, Pallas kernels for 29%

profile of v8, /device:TPU:0, one launch (start us, length us, event | category | flops | bytes accessed | tf_op | source)
XLA Modules:
  0.0 109.3 jit_solution(8937238673492587659)
XLA Ops:
  0.6 0.5 collective-permute-start.3
  1.1 0.1 collective-permute-start
  1.2 0.4 collective-permute-start.9
  1.7 2.7 %collective-permute-start.1 = (bf16[128,2048]{1,0:T(8,128)(2,1)}, bf16[128,2048]{1,0:T(8,128)(2,1)S(1)}, u32[]{:S(2)}, u32[]{:S(2)}) collective-permute-start(bf16[128,2048]{1,0:T(8,128)(2,1)} %refs_2_.1), channel_id=1, source_target_pairs={{0,4},{1,5},{2,0},{3,1},{4,8},{5,9},{6,2},{7,3},{8,12},{9,13},{10,... | collective-permute-start | bytes 1572872 | tf_op jit(solution)/shard_map/ppermute | solution.py:345
  4.3 0.0 collective-permute-start.2
  4.3 0.7 select_reduce_fusion.span_of_ref
  5.1 1.3 %collective-permute-done.3.refs_7_ = bf16[704,2048]{1,0:T(8,128)(2,1)} collective-permute-done((bf16[704,2048]{1,0:T(8,128)(2,1)}, bf16[704,2048]{1,0:T(8,128)(2,1)}, u32[]{:S(2)}, u32[]{:S(2)}) %collective-permute-start.3) | collective-permute-done | bytes 2883616 | tf_op jit(solution)/shard_map/ppermute | solution.py:345
  6.4 1.7 %shard_map.114 = (bf16[8,8,2048]{2,1,0:T(8,128)(2,1)S(1)}, bf16[8,8,2048]{2,1,0:T(8,128)(2,1)S(1)}) custom-call(s32[1]{0:T(128)} %bitcast.6.me_ref, s32[16]{0:T(128)S(1)} %select_reduce_fusion.span_of_ref, bf16[16,8,2048]{2,1,0:T(8,128)(2,1)} %bitcast.28), custom_call_target="tpu_custom_call" | custom-call | tf_op jit(solution)/shard_map/pallas_call | solution.py:102
  8.1 8.9 %collective-permute-done.1.refs_0_ = bf16[128,2048]{1,0:T(8,128)(2,1)S(1)} collective-permute-done((bf16[128,2048]{1,0:T(8,128)(2,1)}, bf16[128,2048]{1,0:T(8,128)(2,1)S(1)}, u32[]{:S(2)}, u32[]{:S(2)}) %collective-permute-start.1) | collective-permute-done | bytes 524320 | tf_op jit(solution)/shard_map/ppermute | solution.py:345
  17.0 1.5 %collective-permute-done.2.refs_1_ = bf16[128,2048]{1,0:T(8,128)(2,1)S(1)} collective-permute-done((bf16[128,2048]{1,0:T(8,128)(2,1)}, bf16[128,2048]{1,0:T(8,128)(2,1)S(1)}, u32[]{:S(2)}, u32[]{:S(2)}) %collective-permute-start.2) | collective-permute-done | bytes 524320 | tf_op jit(solution)/shard_map/ppermute | solution.py:345
  18.5 1.6 %collective-permute-start.4 = (bf16[128,2048]{1,0:T(8,128)(2,1)S(1)}, bf16[128,2048]{1,0:T(8,128)(2,1)S(1)}, u32[]{:S(2)}, u32[]{:S(2)}) collective-permute-start(bf16[128,2048]{1,0:T(8,128)(2,1)S(1)} %collective-permute-done.1.refs_0_), channel_id=1, source_target_pairs={{0,4},{1,5},{2,0},{3,1},{4,8},{5,9},{6,2},{7,3},{8,12},{9,13},{10,... | collective-permute-start | bytes 1572872 | tf_op jit(solution)/shard_map/ppermute | solution.py:345
  20.1 0.4 collective-permute-start.5
  20.5 0.0 collective-permute-start.6
  20.6 0.7 copy-done.5
  21.2 2.2 %shard_map.113 = f32[128,128]{1,0:T(8,128)} custom-call(s32[6,128]{1,0:T(8,128)S(1)} %bitcast.20, bf16[16,2048]{1,0:T(8,128)(2,1)} %bitcast.29, bf16[128,2048]{1,0:T(8,128)(2,1)} %refs_2_.1), custom_call_target="tpu_custom_call" | custom-call | tf_op jit(solution)/shard_map/pallas_call | solution.py:73
  23.4 5.0 %all-to-all-start = ((f32[16,8,128]{2,1,0:T(8,128)}), f32[16,8,128]{2,1,0:T(8,128)S(1)}, u32[]{:S(2)}, u32[]{:S(2)}) async-start(f32[16,8,128]{2,1,0:T(8,128)} %bitcast.4), calls=%async_computation | async-start | bytes 131072 | tf_op jit(solution)/shard_map/all_to_all | solution.py:367
  28.5 0.8 shard_map.115
  29.3 2.4 %collective-permute-done.4.refs_0_ = bf16[128,2048]{1,0:T(8,128)(2,1)S(1)} collective-permute-done((bf16[128,2048]{1,0:T(8,128)(2,1)S(1)}, bf16[128,2048]{1,0:T(8,128)(2,1)S(1)}, u32[]{:S(2)}, u32[]{:S(2)}) %collective-permute-start.4) | collective-permute-done | bytes 524320 | tf_op jit(solution)/shard_map/ppermute | solution.py:345
  31.7 1.6 %collective-permute-done.5.refs_1_ = bf16[128,2048]{1,0:T(8,128)(2,1)S(1)} collective-permute-done((bf16[128,2048]{1,0:T(8,128)(2,1)S(1)}, bf16[128,2048]{1,0:T(8,128)(2,1)S(1)}, u32[]{:S(2)}, u32[]{:S(2)}) %collective-permute-start.5) | collective-permute-done | bytes 524320 | tf_op jit(solution)/shard_map/ppermute | solution.py:345
  33.3 1.9 %collective-permute-start.7 = (bf16[128,2048]{1,0:T(8,128)(2,1)S(1)}, bf16[128,2048]{1,0:T(8,128)(2,1)S(1)}, u32[]{:S(2)}, u32[]{:S(2)}) collective-permute-start(bf16[128,2048]{1,0:T(8,128)(2,1)S(1)} %collective-permute-done.4.refs_0_), channel_id=1, source_target_pairs={{0,4},{1,5},{2,0},{3,1},{4,8},{5,9},{6,2},{7,3},{8,12},{9,13},{10,... | collective-permute-start | bytes 1572872 | tf_op jit(solution)/shard_map/ppermute | solution.py:345
  35.2 0.1 collective-permute-start.8
  35.3 0.3 all-to-all-done
  35.6 9.0 %shard_map.116 = (bf16[128,2048]{1,0:T(8,128)(2,1)S(1)}, bf16[128,2048]{1,0:T(8,128)(2,1)S(1)}, bf16[704,2048]{1,0:T(8,128)(2,1)S(1)}, bf16[704,2048]{1,0:T(8,12...) custom-call(bf16[128,2048]{1,0:T(8,128)(2,1)S(1)} %collective-permut, ...), custom_call_target="tpu_custom_call" | custom-call | flops 4429185024 | bytes 17301504 | tf_op jit(solution)/shard_map/pallas_call | solution.py:199
  44.7 0.5 collective-permute-done.7.below_ref.refs_0_
  45.2 1.2 %collective-permute-done.8.above_ref.refs_1_ = bf16[128,2048]{1,0:T(8,128)(2,1)S(1)} collective-permute-done((bf16[128,2048]{1,0:T(8,128)(2,1)S(1)}, bf16[128,2048]{1,0:T(8,128)(2,1)S(1)}, u32[]{:S(2)}, u32[]{:S(2)}) %collective-permute-start.8) | collective-permute-done | bytes 524320 | tf_op jit(solution)/shard_map/ppermute | solution.py:345
  46.4 0.1 shard_map.117
  46.5 1.4 %collective-permute-start.10 = (bf16[64,2048]{1,0:T(8,128)(2,1)S(1)}, bf16[64,2048]{1,0:T(8,128)(2,1)S(1)}, u32[]{:S(2)}, u32[]{:S(2)}) collective-permute-start(bf16[64,2048]{1,0:T(8,128)(2,1)S(1)} %get-tuple-element.74), channel_id=1, source_target_pairs={{0,4},{1,5},{2,0},{3,1},{4,8},{5,9},{6,2},{7,3},{8,12},{9,13},{10,... | collective-permute-start | bytes 786440 | tf_op jit(solution)/shard_map/ppermute | solution.py:345
  47.9 0.7 collective-permute-start.11
  48.5 5.2 %shard_map.118 = (bf16[64,2048]{1,0:T(8,128)(2,1)S(1)}, bf16[64,2048]{1,0:T(8,128)(2,1)S(1)}, bf16[64,2048]{1,0:T(8,128)(2,1)S(1)}, bf16[64,2048]{1,0:T(8,128)(2,1)S(1)}) custom-call(bf16[128,2048]{1,0:T(8,128)(2,1)S(1)} %collective-permute-done.7.below_ref.refs_0_, bf16[128,2048]{1,0:T(8,128)(2,1)S(1)} %collective-permute-done.8.above_ref.refs_1_, ...), custom_call_target="tpu_custom_call" | custom-call | flops 4429185024 | bytes 17301504 | tf_op jit(solution)/shard_map/pallas_call | solution.py:199
  53.8 0.5 collective-permute-done.11.refs_1_
  54.2 0.9 collective-permute-start.12
  55.2 1.1 %collective-permute-start.13 = (bf16[64,2048]{1,0:T(8,128)(2,1)S(1)}, bf16[64,2048]{1,0:T(8,128)(2,1)S(1)}, u32[]{:S(2)}, u32[]{:S(2)}) collective-permute-start(bf16[64,2048]{1,0:T(8,128)(2,1)S(1)} %get-tuple-element.92), channel_id=1, source_target_pairs={{4,0},{5,1},{0,2},{1,3},{8,4},{9,5},{2,6},{3,7},{12,8},{13,9},{6,1... | collective-permute-start | bytes 786440 | tf_op jit(solution)/shard_map/ppermute | solution.py:345
  56.3 5.2 %shard_map.119 = (bf16[64,2048]{1,0:T(8,128)(2,1)S(1)}, bf16[64,2048]{1,0:T(8,128)(2,1)S(1)}, bf16[64,2048]{1,0:T(8,128)(2,1)S(1)}, bf16[64,2048]{1,0:T(8,128)(2,1)S(1)}) custom-call(bf16[64,2048]{1,0:T(8,128)(2,1)S(1)} %collective-permute-done.10.refs_0_, bf16[64,2048]{1,0:T(8,128)(2,1)S(1)} %collective-permute-done.11.refs_1_, ...), custom_call_target="tpu_custom_call" | custom-call | flops 4429185024 | bytes 17301504 | tf_op jit(solution)/shard_map/pallas_call | solution.py:199
  61.5 0.0 copy-start.2
  61.5 0.0 collective-permute-done.12.refs_0_
  61.5 0.2 collective-permute-done.13.refs_1_
  61.7 0.8 collective-permute-start.14
  62.6 1.2 %collective-permute-start.15 = (bf16[64,2048]{1,0:T(8,128)(2,1)S(1)}, bf16[64,2048]{1,0:T(8,128)(2,1)S(1)}, u32[]{:S(2)}, u32[]{:S(2)}) collective-permute-start(bf16[64,2048]{1,0:T(8,128)(2,1)S(1)} %get-tuple-element.96), channel_id=1, source_target_pairs={{4,0},{5,1},{0,2},{1,3},{8,4},{9,5},{2,6},{3,7},{12,8},{13,9},{6,1... | collective-permute-start | bytes 786440 | tf_op jit(solution)/shard_map/ppermute | solution.py:345
  63.8 5.2 %shard_map.121 = (bf16[128,2048]{1,0:T(8,128)(2,1)S(1)}, bf16[128,2048]{1,0:T(8,128)(2,1)S(1)}) custom-call(bf16[128,2048]{1,0:T(8,128)(2,1)S(1)} %collective-permute-done.1.refs_0_, bf16[128,2048]{1,0:T(8,128)(2,1)S(1)} %collective-permute-done.2.refs_1_, f32[128,128]{1,0:T(8,128)S(1)} %bitcast.19, bf16[704,2048]{1,0:T(8,128)(2,1)S(1)} %get-tuple-element.76.refs_3_.refs_4_, ...), custom_call_target="tpu_custom_call" | custom-call | flops 4429185024 | bytes 17301504 | tf_op jit(solution)/shard_map/pallas_call | solution.py:199
  69.0 1.1 collective-permute-done.15
  70.0 0.1 add_convert_fusion
  70.1 1.0 collective-permute-start.19
  71.1 0.1 add_convert_fusion.1
  71.2 1.1 %collective-permute-start.16 = (bf16[64,2048]{1,0:T(8,128)(2,1)S(1)}, bf16[64,2048]{1,0:T(8,128)(2,1)S(1)}, u32[]{:S(2)}, u32[]{:S(2)}) collective-permute-start(bf16[64,2048]{1,0:T(8,128)(2,1)S(1)} %add_convert_fusion.1), channel_id=1, source_target_pairs={{0,4},{1,5},{2,0},{3,1},{4,8},{5,9},{6,2},{7,3},{8,12},{9,13},{10,... | collective-permute-start | bytes 786440 | tf_op jit(solution)/shard_map/ppermute | solution.py:345
  72.3 6.4 %collective-permute-done.19.refs_0_ = bf16[64,2048]{1,0:T(8,128)(2,1)S(1)} collective-permute-done((bf16[64,2048]{1,0:T(8,128)(2,1)S(1)}, bf16[64,2048]{1,0:T(8,128)(2,1)S(1)}, u32[]{:S(2)}, u32[]{:S(2)}) %collective-permute-start.19) | collective-permute-done | bytes 262176 | tf_op jit(solution)/shard_map/ppermute | solution.py:345
  78.7 0.1 shard_map.124
  78.8 0.0 copy-start.4
  78.9 0.0 copy-start.6
  78.9 0.7 collective-permute-start.20
  79.6 0.2 collective-permute-done.16.refs_1_
  79.8 0.1 shard_map.122
  79.9 1.4 %collective-permute-start.17 = (bf16[128,2048]{1,0:T(8,128)(2,1)S(1)}, bf16[128,2048]{1,0:T(8,128)(2,1)}, u32[]{:S(2)}, u32[]{:S(2)}) collective-permute-start(bf16[128,2048]{1,0:T(8,128)(2,1)S(1)} %shard_map.122), channel_id=1, source_target_pairs={{0,4},{1,5},{2,0},{3,1},{4,8},{5,9},{6,2},{7,3},{8,12},{9,13},{10,... | collective-permute-start | bytes 1572872 | tf_op jit(solution)/shard_map/ppermute | solution.py:345
  81.3 3.7 %all-to-all-start.1 = ((bf16[8,2,8,2048]{3,2,1,0:T(8,128)(2,1)}), bf16[8,2,8,2048]{3,2,1,0:T(8,128)(2,1)S(1)}, u32[]{:S(2)}, u32[]{:S(2)}) async-start(bf16[8,2,8,2048]{3,2,1,0:T(8,128)(2,1)} %shard_map.115), calls=%async_computation.1 | async-start | bytes 1048576 | tf_op jit(solution)/shard_map/all_to_all | solution.py:363
  85.0 12.0 %collective-permute-done.20.refs_0_ = bf16[128,2048]{1,0:T(8,128)(2,1)S(1)} collective-permute-done((bf16[128,2048]{1,0:T(8,128)(2,1)S(1)}, bf16[128,2048]{1,0:T(8,128)(2,1)S(1)}, u32[]{:S(2)}, u32[]{:S(2)}) %collective-permute-start.20) | collective-permute-done | bytes 524320 | tf_op jit(solution)/shard_map/ppermute | solution.py:345
  97.0 0.1 shard_map.125
  97.2 0.1 collective-permute-start.21
  97.2 1.2 %shard_map.123 = bf16[128,2048]{1,0:T(8,128)(2,1)S(1)} custom-call(bf16[128,2048]{1,0:T(8,128)(2,1)S(1)} %get-tuple-element.101.total_ref, bf16[128,2048]{1,0:T(8,128)(2,1)} %collective-permute-done.17.refs_0_), custom_call_target="tpu_custom_call" | custom-call | tf_op jit(solution)/shard_map/pallas_call | solution.py:293
  98.4 2.1 %collective-permute-start.18 = (bf16[128,2048]{1,0:T(8,128)(2,1)S(1)}, bf16[128,2048]{1,0:T(8,128)(2,1)S(1)}, u32[]{:S(2)}, u32[]{:S(2)}) collective-permute-start(bf16[128,2048]{1,0:T(8,128)(2,1)S(1)} %shard_map.123), channel_id=1, source_target_pairs={{0,4},{1,5},{2,0},{3,1},{4,8},{5,9},{6,2},{7,3},{8,12},{9,13},{10,... | collective-permute-start | bytes 1572872 | tf_op jit(solution)/shard_map/ppermute | solution.py:345
  100.5 4.4 %all-to-all-done.1 = bf16[8,2,8,2048]{3,2,1,0:T(8,128)(2,1)S(1)} async-done(((bf16[8,2,8,2048]{3,2,1,0:T(8,128)(2,1)}), bf16[8,2,8,2048]{3,2,1,0:T(8,128)(2,1)S(1)}, u32[]{:S(2)}, u32[]{:S(2)}) %all-to-all-start.1) | async-done | bytes 524320 | tf_op jit(solution)/shard_map/all_to_all | solution.py:363
  104.9 1.0 copy-done.1
  105.9 0.9 copy-done.3
  106.9 1.2 %shard_map.120 = (bf16[128,2048]{1,0:T(8,128)(2,1)}, bf16[128,2048]{1,0:T(8,128)(2,1)S(1)}) custom-call(bf16[128,2048]{1,0:T(8,128)(2,1)S(1)} %bitcast.15, s32[16,16]{1,0:T(8,128)S(1)} %copy-done.4, s32[1,16]{1,0:T(1,128)S(1)} %bitcast.21, s32[1]{0:T(128)} %bitcast.6.me_ref, bf16[128,2048]{1,0:T(8,128)(2,1)S(1)} %copy-done.1, ...), custom_call_target="tpu_custom_call" | custom-call | tf_op jit(solution)/shard_map/pallas_call | solution.py:245
  108.0 0.3 collective-permute-done.18.up_ref
  108.3 1.0 shard_map.126
  (15 shorter events, 0.0 us)
Async XLA Ops:
  0.6 5.8 %collective-permute-start.3 = (bf16[704,2048]{1,0:T(8,128)(2,1)}, bf16[704,2048]{1,0:T(8,128)(2,1)}, u32[]{:S(2)}, u32[]{:S(2)}) collective-permute-start(bf16[704,2048]{1,0:T(8,128)(2,1)} %bitcast.24), channel_id=1, source_target_pairs={{0,1},{1,0},{2,3},{3,2},{4,5},{5,4},{6,7},{7,6},{8,9},{9,8},{10,11... | collective-permute-start | bytes 8650760 | tf_op jit(solution)/shard_map/ppermute | solution.py:345
  1.1 19.4 %collective-permute-start = (bf16[704,2048]{1,0:T(8,128)(2,1)}, bf16[704,2048]{1,0:T(8,128)(2,1)}, u32[]{:S(2)}, u32[]{:S(2)}) collective-permute-start(bf16[704,2048]{1,0:T(8,128)(2,1)} %bitcast.22), channel_id=1, source_target_pairs={{0,1},{1,0},{2,3},{3,2},{4,5},{5,4},{6,7},{7,6},{8,9},{9,8},{10,11... | collective-permute-start | bytes 8650760 | tf_op jit(solution)/shard_map/ppermute | solution.py:345
  1.2 34.4 %collective-permute-start.9 = (bf16[704,2048]{1,0:T(8,128)(2,1)}, bf16[704,2048]{1,0:T(8,128)(2,1)}, u32[]{:S(2)}, u32[]{:S(2)}) collective-permute-start(bf16[704,2048]{1,0:T(8,128)(2,1)} %bitcast.26), channel_id=1, source_target_pairs={{0,1},{1,0},{2,3},{3,2},{4,5},{5,4},{6,7},{7,6},{8,9},{9,8},{10,11... | collective-permute-start | bytes 8650760 | tf_op jit(solution)/shard_map/ppermute | solution.py:345
  1.7 15.3 %collective-permute-start.1 = (bf16[128,2048]{1,0:T(8,128)(2,1)}, bf16[128,2048]{1,0:T(8,128)(2,1)S(1)}, u32[]{:S(2)}, u32[]{:S(2)}) collective-permute-start(bf16[128,2048]{1,0:T(8,128)(2,1)} %refs_2_.1), channel_id=1, source_target_pairs={{0,4},{1,5},{2,0},{3,1},{4,8},{5,9},{6,2},{7,3},{8,12},{9,13},{10,... | collective-permute-start | bytes 1572872 | tf_op jit(solution)/shard_map/ppermute | solution.py:345
  4.3 14.2 %collective-permute-start.2 = (bf16[128,2048]{1,0:T(8,128)(2,1)}, bf16[128,2048]{1,0:T(8,128)(2,1)S(1)}, u32[]{:S(2)}, u32[]{:S(2)}) collective-permute-start(bf16[128,2048]{1,0:T(8,128)(2,1)} %refs_2_.1), channel_id=1, source_target_pairs={{4,0},{5,1},{0,2},{1,3},{8,4},{9,5},{2,6},{3,7},{12,8},{13,9},{6,1... | collective-permute-start | bytes 1572872 | tf_op jit(solution)/shard_map/ppermute | solution.py:345
  18.5 13.2 %collective-permute-start.4 = (bf16[128,2048]{1,0:T(8,128)(2,1)S(1)}, bf16[128,2048]{1,0:T(8,128)(2,1)S(1)}, u32[]{:S(2)}, u32[]{:S(2)}) collective-permute-start(bf16[128,2048]{1,0:T(8,128)(2,1)S(1)} %collective-permute-done.1.refs_0_), channel_id=1, source_target_pairs={{0,4},{1,5},{2,0},{3,1},{4,8},{5,9},{6,2},{7,3},{8,12},{9,13},{10,... | collective-permute-start | bytes 1572872 | tf_op jit(solution)/shard_map/ppermute | solution.py:345
  20.1 13.2 %collective-permute-start.5 = (bf16[128,2048]{1,0:T(8,128)(2,1)S(1)}, bf16[128,2048]{1,0:T(8,128)(2,1)S(1)}, u32[]{:S(2)}, u32[]{:S(2)}) collective-permute-start(bf16[128,2048]{1,0:T(8,128)(2,1)S(1)} %collective-permute-done.2.refs_1_), channel_id=1, source_target_pairs={{4,0},{5,1},{0,2},{1,3},{8,4},{9,5},{2,6},{3,7},{12,8},{13,9},{6,1... | collective-permute-start | bytes 1572872 | tf_op jit(solution)/shard_map/ppermute | solution.py:345
  20.5 7.9 %collective-permute-start.6 = (bf16[8,8,2048]{2,1,0:T(8,128)(2,1)S(1)}, bf16[8,8,2048]{2,1,0:T(8,128)(2,1)S(1)}, u32[]{:S(2)}, u32[]{:S(2)}) collective-permute-start(bf16[8,8,2048]{2,1,0:T(8,128)(2,1)S(1)} %get-tuple-element.64), channel_id=1, source_target_pairs={{0,1},{1,0},{2,3},{3,2},{4,5},{5,4},{6,7},{7,6},{8,9},{9,8},{10,11... | collective-permute-start | bytes 786440 | tf_op jit(solution)/shard_map/ppermute | solution.py:345
  20.5 0.7 copy-start.5
  23.4 12.2 %all-to-all-start = ((f32[16,8,128]{2,1,0:T(8,128)}), f32[16,8,128]{2,1,0:T(8,128)S(1)}, u32[]{:S(2)}, u32[]{:S(2)}) async-start(f32[16,8,128]{2,1,0:T(8,128)} %bitcast.4), calls=%async_computation | async-start | bytes 131072 | tf_op jit(solution)/shard_map/all_to_all | solution.py:367
  33.3 11.9 %collective-permute-start.7 = (bf16[128,2048]{1,0:T(8,128)(2,1)S(1)}, bf16[128,2048]{1,0:T(8,128)(2,1)S(1)}, u32[]{:S(2)}, u32[]{:S(2)}) collective-permute-start(bf16[128,2048]{1,0:T(8,128)(2,1)S(1)} %collective-permute-done.4.refs_0_), channel_id=1, source_target_pairs={{0,4},{1,5},{2,0},{3,1},{4,8},{5,9},{6,2},{7,3},{8,12},{9,13},{10,... | collective-permute-start | bytes 1572872 | tf_op jit(solution)/shard_map/ppermute | solution.py:345
  35.2 11.2 %collective-permute-start.8 = (bf16[128,2048]{1,0:T(8,128)(2,1)S(1)}, bf16[128,2048]{1,0:T(8,128)(2,1)S(1)}, u32[]{:S(2)}, u32[]{:S(2)}) collective-permute-start(bf16[128,2048]{1,0:T(8,128)(2,1)S(1)} %collective-permute-done.5.refs_1_), channel_id=1, source_target_pairs={{4,0},{5,1},{0,2},{1,3},{8,4},{9,5},{2,6},{3,7},{12,8},{13,9},{6,1... | collective-permute-start | bytes 1572872 | tf_op jit(solution)/shard_map/ppermute | solution.py:345
  46.5 7.3 %collective-permute-start.10 = (bf16[64,2048]{1,0:T(8,128)(2,1)S(1)}, bf16[64,2048]{1,0:T(8,128)(2,1)S(1)}, u32[]{:S(2)}, u32[]{:S(2)}) collective-permute-start(bf16[64,2048]{1,0:T(8,128)(2,1)S(1)} %get-tuple-element.74), channel_id=1, source_target_pairs={{0,4},{1,5},{2,0},{3,1},{4,8},{5,9},{6,2},{7,3},{8,12},{9,13},{10,... | collective-permute-start | bytes 786440 | tf_op jit(solution)/shard_map/ppermute | solution.py:345
  47.9 6.4 %collective-permute-start.11 = (bf16[64,2048]{1,0:T(8,128)(2,1)S(1)}, bf16[64,2048]{1,0:T(8,128)(2,1)S(1)}, u32[]{:S(2)}, u32[]{:S(2)}) collective-permute-start(bf16[64,2048]{1,0:T(8,128)(2,1)S(1)} %get-tuple-element.75), channel_id=1, source_target_pairs={{4,0},{5,1},{0,2},{1,3},{8,4},{9,5},{2,6},{3,7},{12,8},{13,9},{6,1... | collective-permute-start | bytes 786440 | tf_op jit(solution)/shard_map/ppermute | solution.py:345
  48.5 7.7 %copy-start = (bf16[128,2048]{1,0:T(8,128)(2,1)S(1)}, bf16[128,2048]{1,0:T(8,128)(2,1)}, u32[]{:S(2)}) copy-start(bf16[128,2048]{1,0:T(8,128)(2,1)} %refs_2_.1) | copy-start | bytes 1572868
  54.2 7.2 %collective-permute-start.12 = (bf16[64,2048]{1,0:T(8,128)(2,1)S(1)}, bf16[64,2048]{1,0:T(8,128)(2,1)S(1)}, u32[]{:S(2)}, u32[]{:S(2)}) collective-permute-start(bf16[64,2048]{1,0:T(8,128)(2,1)S(1)} %get-tuple-element.91), channel_id=1, source_target_pairs={{0,4},{1,5},{2,0},{3,1},{4,8},{5,9},{6,2},{7,3},{8,12},{9,13},{10,... | collective-permute-start | bytes 786440 | tf_op jit(solution)/shard_map/ppermute | solution.py:345
  55.2 6.6 %collective-permute-start.13 = (bf16[64,2048]{1,0:T(8,128)(2,1)S(1)}, bf16[64,2048]{1,0:T(8,128)(2,1)S(1)}, u32[]{:S(2)}, u32[]{:S(2)}) collective-permute-start(bf16[64,2048]{1,0:T(8,128)(2,1)S(1)} %get-tuple-element.92), channel_id=1, source_target_pairs={{4,0},{5,1},{0,2},{1,3},{8,4},{9,5},{2,6},{3,7},{12,8},{13,9},{6,1... | collective-permute-start | bytes 786440 | tf_op jit(solution)/shard_map/ppermute | solution.py:345
  61.5 7.5 %copy-start.2 = (bf16[64,2048]{1,0:T(8,128)(2,1)}, bf16[64,2048]{1,0:T(8,128)(2,1)S(1)}, u32[]{:S(2)}) copy-start(bf16[64,2048]{1,0:T(8,128)(2,1)S(1)} %get-tuple-element.89.second_ref) | copy-start | bytes 786436
  61.7 7.2 %collective-permute-start.14 = (bf16[64,2048]{1,0:T(8,128)(2,1)S(1)}, bf16[64,2048]{1,0:T(8,128)(2,1)S(1)}, u32[]{:S(2)}, u32[]{:S(2)}) collective-permute-start(bf16[64,2048]{1,0:T(8,128)(2,1)S(1)} %get-tuple-element.95), channel_id=1, source_target_pairs={{0,4},{1,5},{2,0},{3,1},{4,8},{5,9},{6,2},{7,3},{8,12},{9,13},{10,... | collective-permute-start | bytes 786440 | tf_op jit(solution)/shard_map/ppermute | solution.py:345
  62.6 7.5 %collective-permute-start.15 = (bf16[64,2048]{1,0:T(8,128)(2,1)S(1)}, bf16[64,2048]{1,0:T(8,128)(2,1)S(1)}, u32[]{:S(2)}, u32[]{:S(2)}) collective-permute-start(bf16[64,2048]{1,0:T(8,128)(2,1)S(1)} %get-tuple-element.96), channel_id=1, source_target_pairs={{4,0},{5,1},{0,2},{1,3},{8,4},{9,5},{2,6},{3,7},{12,8},{13,9},{6,1... | collective-permute-start | bytes 786440 | tf_op jit(solution)/shard_map/ppermute | solution.py:345
  70.1 8.6 %collective-permute-start.19 = (bf16[64,2048]{1,0:T(8,128)(2,1)S(1)}, bf16[64,2048]{1,0:T(8,128)(2,1)S(1)}, u32[]{:S(2)}, u32[]{:S(2)}) collective-permute-start(bf16[64,2048]{1,0:T(8,128)(2,1)S(1)} %add_convert_fusion), channel_id=1, source_target_pairs={{4,0},{5,1},{0,2},{1,3},{8,4},{9,5},{2,6},{3,7},{12,8},{13,9},{6,1... | collective-permute-start | bytes 786440 | tf_op jit(solution)/shard_map/ppermute | solution.py:345
  71.2 8.6 %collective-permute-start.16 = (bf16[64,2048]{1,0:T(8,128)(2,1)S(1)}, bf16[64,2048]{1,0:T(8,128)(2,1)S(1)}, u32[]{:S(2)}, u32[]{:S(2)}) collective-permute-start(bf16[64,2048]{1,0:T(8,128)(2,1)S(1)} %add_convert_fusion.1), channel_id=1, source_target_pairs={{0,4},{1,5},{2,0},{3,1},{4,8},{5,9},{6,2},{7,3},{8,12},{9,13},{10,... | collective-permute-start | bytes 786440 | tf_op jit(solution)/shard_map/ppermute | solution.py:345
  78.8 26.0 %copy-start.4 = (s32[16,16]{1,0:T(8,128)S(1)}, s32[16,16]{1,0:T(8,128)}, u32[]{:S(2)}) copy-start(s32[16,16]{1,0:T(8,128)} %counts_ref.1) | copy-start | bytes 3076
  78.9 26.0 %copy-start.6 = (s32[16]{0:T(128)S(1)}, s32[16]{0:T(128)}, u32[]{:S(2)}) copy-start(s32[16]{0:T(128)} %param.18) | copy-start | bytes 196
  78.9 18.2 %collective-permute-start.20 = (bf16[128,2048]{1,0:T(8,128)(2,1)S(1)}, bf16[128,2048]{1,0:T(8,128)(2,1)S(1)}, u32[]{:S(2)}, u32[]{:S(2)}) collective-permute-start(bf16[128,2048]{1,0:T(8,128)(2,1)S(1)} %shard_map.124), channel_id=1, source_target_pairs={{4,0},{5,1},{0,2},{1,3},{8,4},{9,5},{2,6},{3,7},{12,8},{13,9},{6,1... | collective-permute-start | bytes 1572872 | tf_op jit(solution)/shard_map/ppermute | solution.py:345
  79.9 17.3 %collective-permute-start.17 = (bf16[128,2048]{1,0:T(8,128)(2,1)S(1)}, bf16[128,2048]{1,0:T(8,128)(2,1)}, u32[]{:S(2)}, u32[]{:S(2)}) collective-permute-start(bf16[128,2048]{1,0:T(8,128)(2,1)S(1)} %shard_map.122), channel_id=1, source_target_pairs={{0,4},{1,5},{2,0},{3,1},{4,8},{5,9},{6,2},{7,3},{8,12},{9,13},{10,... | collective-permute-start | bytes 1572872 | tf_op jit(solution)/shard_map/ppermute | solution.py:345
  81.3 23.6 %all-to-all-start.1 = ((bf16[8,2,8,2048]{3,2,1,0:T(8,128)(2,1)}), bf16[8,2,8,2048]{3,2,1,0:T(8,128)(2,1)S(1)}, u32[]{:S(2)}, u32[]{:S(2)}) async-start(bf16[8,2,8,2048]{3,2,1,0:T(8,128)(2,1)} %shard_map.115), calls=%async_computation.1 | async-start | bytes 1048576 | tf_op jit(solution)/shard_map/all_to_all | solution.py:363
  97.2 10.9 %collective-permute-start.21 = (bf16[128,2048]{1,0:T(8,128)(2,1)S(1)}, bf16[128,2048]{1,0:T(8,128)(2,1)S(1)}, u32[]{:S(2)}, u32[]{:S(2)}) collective-permute-start(bf16[128,2048]{1,0:T(8,128)(2,1)S(1)} %shard_map.125), channel_id=1, source_target_pairs={{4,0},{5,1},{0,2},{1,3},{8,4},{9,5},{2,6},{3,7},{12,8},{13,9},{6,1... | collective-permute-start | bytes 1572872 | tf_op jit(solution)/shard_map/ppermute | solution.py:345
  98.4 9.9 %collective-permute-start.18 = (bf16[128,2048]{1,0:T(8,128)(2,1)S(1)}, bf16[128,2048]{1,0:T(8,128)(2,1)S(1)}, u32[]{:S(2)}, u32[]{:S(2)}) collective-permute-start(bf16[128,2048]{1,0:T(8,128)(2,1)S(1)} %shard_map.123), channel_id=1, source_target_pairs={{0,4},{1,5},{2,0},{3,1},{4,8},{5,9},{6,2},{7,3},{8,12},{9,13},{10,... | collective-permute-start | bytes 1572872 | tf_op jit(solution)/shard_map/ppermute | solution.py:345
  104.9 1.0 copy-start.1
  105.9 0.9 copy-start.3
